TPU v7x, 512 devices: a whole 4x8x8 slice. The times are simulated.
512 devices in a mesh: section: 64 (over y, z_lo, core), dp: 8 (over x, z_hi).
Axes of the slice: x: 4, y: 8, z: 8 (z_hi: 2, z_lo: 4; z = z_hi * 4 + z_lo), core: 2. Of those that a mesh axis runs over, the one named last changes fastest.
Arguments:
- inputs: bfloat16 [8, 128, 8192], P(None, 'dp', 'section'), may hold values from -6 to 6
- gain: float32 [64, 8192], P('section'), may hold values from 0.1 to 1.9
- w_in: bfloat16 [64, 8192, 128], P('section'), may hold values from -0.0625 to 0.0625
- w_out: bfloat16 [64, 128, 8192], P('section'), may hold values from -0.5 to 0.5
Outputs:
- grad_in: bfloat16 [64, 8192, 128], P('section', 'dp')
- grad_out: bfloat16 [64, 128, 8192], P('section', None, 'dp')
All inputs are finite; a program needn't handle non-finite values.
Results may differ from a plain program's by a relative error of at most 0.034.
Values may be sent and summed in bfloat16 or wider, within the bound.
No kernel may reach another device: no remote copies, remote signals or barrier semaphores. Data moves between devices by JAX's collectives and lax.ppermute only.
A program may use at most 64 MiB of HBM per device.

v0:
```python
import math

import jax
import jax.numpy as jnp
from jax import lax
from jax.sharding import PartitionSpec as P

epsilon = 1e-05


def shifted(value, axis, steps):
    count = lax.axis_size(axis)
    leading, last = (max(0, -steps), min(count, count - steps))
    return lax.ppermute(value, axis, [(source, source + steps) for source in range(leading, last)])


def section_forward(inputs, gain_row, w_first, w_second):
    hidden = inputs.astype(jnp.float32)
    inverse = lax.rsqrt(jnp.mean(hidden * hidden, axis=-1, keepdims=True) + epsilon)
    normed = (hidden * inverse * gain_row).astype(jnp.bfloat16)
    project = jnp.dot(normed, w_first, preferred_element_type=jnp.float32)
    active = jax.nn.silu(project).astype(jnp.bfloat16)
    result = hidden + jnp.dot(active, w_second, preferred_element_type=jnp.float32)
    return (hidden, inverse, normed, project, active, result)


def section_backward(inputs, incoming, is_last, gain_row, w_first, w_second):
    hidden, inverse, normed, project, active, result = section_forward(
        inputs, gain_row, w_first, w_second
    )
    cotangent = jnp.where(is_last, result.astype(jnp.bfloat16), incoming)
    upper = lax.dot_general(
        cotangent, w_second, (((1,), (1,)), ((), ())), preferred_element_type=jnp.float32
    )
    sigma = jax.nn.sigmoid(project)
    grad_project = (upper * sigma * (1.0 + project * (1.0 - sigma))).astype(jnp.bfloat16)
    grad_normed = lax.dot_general(
        grad_project, w_first, (((1,), (1,)), ((), ())), preferred_element_type=jnp.float32
    )
    scaled = grad_normed * gain_row
    grad_hidden = (
        cotangent.astype(jnp.float32)
        + inverse * scaled
        - hidden * inverse**3 * jnp.mean(hidden * scaled, axis=-1, keepdims=True)
    )
    return (grad_hidden.astype(jnp.bfloat16), normed, active, grad_project, cotangent)


def store_slot(table, fresh, slot, valid):
    kept = jnp.where(valid, fresh, table[slot])
    return lax.dynamic_update_index_in_dim(table, kept, slot, 0)


def local(inputs, gain, w_in, w_out):
    sections = lax.axis_size("section")
    replicas = lax.axis_size("dp")
    position = lax.axis_index("section")
    micro = inputs.shape[0]
    per_rows = inputs.shape[1]
    width = w_in.shape[1]
    inner = w_in.shape[2]
    gain_row = gain[0]
    w_first = w_in[0]
    w_second = w_out[0]
    batches = lax.all_gather(inputs, "section", axis=2, tiled=True)
    ticks = micro + sections - 1
    blank = jnp.zeros((per_rows, width), jnp.bfloat16)
    narrow = jnp.zeros((per_rows, inner), jnp.bfloat16)

    def forward_tick(tick, carry):
        incoming, stash = carry
        index = tick - position
        valid = (index >= 0) & (index < micro)
        slot = jnp.clip(index, 0, micro - 1)
        feeding = jnp.where(position == 0, batches[slot], incoming)
        output = lax.cond(
            valid,
            lambda value: section_forward(value, gain_row, w_first, w_second)[5].astype(
                jnp.bfloat16
            ),
            lambda value: jnp.zeros_like(value),
            feeding,
        )
        stash = store_slot(stash, feeding, slot, valid)
        incoming = shifted(output, "section", 1)
        return (incoming, stash)

    stash_init = jnp.zeros((micro, per_rows, width), jnp.bfloat16)
    last_in, stash = lax.fori_loop(0, ticks, forward_tick, (blank, stash_init))
    is_last = position == sections - 1

    def backward_tick(tick, carry):
        incoming, normed_all, active_all, grad_all, cot_all = carry
        index = tick - (sections - 1 - position)
        valid = (index >= 0) & (index < micro)
        slot = jnp.clip(index, 0, micro - 1)

        def compute(pair):
            return section_backward(pair[0], pair[1], is_last, gain_row, w_first, w_second)

        def skipped(pair):
            return (blank, blank, narrow, narrow, blank)

        sent, normed, active, grad_project, cotangent = lax.cond(
            valid, compute, skipped, (stash[slot], incoming)
        )
        normed_all = store_slot(normed_all, normed, slot, valid)
        active_all = store_slot(active_all, active, slot, valid)
        grad_all = store_slot(grad_all, grad_project, slot, valid)
        cot_all = store_slot(cot_all, cotangent, slot, valid)
        incoming = shifted(sent, "section", -1)
        return (incoming, normed_all, active_all, grad_all, cot_all)

    wide_init = jnp.zeros((micro, per_rows, width), jnp.bfloat16)
    small_init = jnp.zeros((micro, per_rows, inner), jnp.bfloat16)
    final = lax.fori_loop(
        0, ticks, backward_tick, (blank, wide_init, small_init, small_init, wide_init)
    )
    flat_normed = final[1].reshape(micro * per_rows, width)
    flat_active = final[2].reshape(micro * per_rows, inner)
    flat_grad = final[3].reshape(micro * per_rows, inner)
    flat_cot = final[4].reshape(micro * per_rows, width)
    scale = 1.0 / math.sqrt(replicas * micro * per_rows)
    term_first = lax.dot_general(
        flat_normed, flat_grad, (((0,), (0,)), ((), ())), preferred_element_type=jnp.float32
    )
    term_second = lax.dot_general(
        flat_cot, flat_active, (((0,), (0,)), ((), ())), preferred_element_type=jnp.float32
    )
    sum_first, sum_second = (
        lax.psum_scatter(
            term_first.astype(jnp.bfloat16), "dp", scatter_dimension=0, tiled=True
        ).astype(jnp.float32),
        lax.psum_scatter(
            term_second.astype(jnp.bfloat16), "dp", scatter_dimension=0, tiled=True
        ).astype(jnp.float32),
    )
    grad_in = (sum_first * scale).astype(jnp.bfloat16)[None]
    grad_out = (sum_second * scale).astype(jnp.bfloat16).T[None]
    return (grad_in, grad_out)


def solution(mesh):
    return jax.shard_map(
        local,
        mesh=mesh,
        in_specs=(
            P(None, "dp", "section"),
            P("section", None),
            P("section", None, None),
            P("section", None, None),
        ),
        out_specs=(P("section", "dp", None), P("section", None, "dp")),
        check_vma=False,
    )
```

profile of v0, /device:TPU:1, one launch (start us, length us, event | category | flops | bytes accessed | tf_op | source)
XLA Modules:
  0.0 2483.7 jit_solution(8943568492861006506)
XLA Ops:
  8.0 125.0 %all-gather.2.cloned.1.call-done = bf16[8,16,8192]{2,1,0:T(8,128)(2,1)} async-done(((bf16[8,16,128]{2,1,0:T(8,128)(2,1)}), bf16[8,16,8192]{2,1,0:T(8,128)(2,1)}) %all-gather.2.cloned.1.call-update) | async-done | bytes 2097168 | tf_op jit(solution)/shard_map/all_gather | solution.py:65
  134.5 918.7 %while.39 = (s32[]{:T(128)}, bf16[16,8192]{1,0:T(8,128)(2,1)S(1)}, bf16[8,16,8192]{2,1,0:T(8,128)(2,1)}, s32[]{:T(128)}, pred[]{:T(512)}, /*index=5*/bf16[8,16,8...) while((s32[]{:T(128)}, bf16[16,8192]{1,0:T(8,128)(2,1)S(1)}, ...), condition=%wide.region_4.5_spmd, body=%wide.region_0.4_spmd.sunk | while | flops 68691992 | bytes 7898132 | solution.py:89
  337.2 9.7 collective-permute-start
  352.9 7.1 collective-permute-start
  366.1 9.7 collective-permute-start
  381.8 7.1 collective-permute-start
  395.0 9.7 collective-permute-start
  410.8 7.1 collective-permute-start
  423.9 7.1 collective-permute-start
  437.1 7.1 collective-permute-start
  450.3 7.1 collective-permute-start
  463.4 7.1 collective-permute-start
  476.6 7.1 collective-permute-start
  489.8 7.1 collective-permute-start
  502.9 7.1 collective-permute-start
  516.1 7.1 collective-permute-start
  529.3 7.1 collective-permute-start
  542.4 7.1 collective-permute-start
  555.6 7.1 collective-permute-start
  568.8 7.1 collective-permute-start
  581.9 7.1 collective-permute-start
  595.1 7.1 collective-permute-start
  608.3 7.1 collective-permute-start
  621.4 7.1 collective-permute-start
  634.6 7.1 collective-permute-start
  647.8 7.1 collective-permute-start
  660.9 7.1 collective-permute-start
  674.1 7.1 collective-permute-start
  687.3 7.1 collective-permute-start
  700.4 7.1 collective-permute-start
  713.6 7.1 collective-permute-start
  726.8 7.1 collective-permute-start
  739.9 7.1 collective-permute-start
  753.1 7.1 collective-permute-start
  766.3 7.1 collective-permute-start
  779.4 7.1 collective-permute-start
  792.6 7.1 collective-permute-start
  805.8 7.1 collective-permute-start
  818.9 7.1 collective-permute-start
  832.1 7.1 collective-permute-start
  845.3 7.1 collective-permute-start
  858.4 7.1 collective-permute-start
  871.6 7.1 collective-permute-start
  884.8 7.1 collective-permute-start
  897.9 7.1 collective-permute-start
  911.1 7.1 collective-permute-start
  924.3 7.1 collective-permute-start
  937.4 7.1 collective-permute-start
  1003.3 7.1 collective-permute-start
  1016.4 7.1 collective-permute-start
  1029.6 7.1 collective-permute-start
  1042.8 7.1 collective-permute-start
  1056.3 1219.6 %while.40 = (s32[]{:T(128)}, bf16[16,8192]{1,0:T(8,128)(2,1)S(1)}, bf16[8,16,8192]{2,1,0:T(8,128)(2,1)}, bf16[8,16,128]{2,1,0:T(8,128)(2,1)S(1)}, bf16[8,16,128]...) while((s32[]{:T(128)}, bf16[16,8192]{1,0:T(8,128)(2,1)S(1)}, ...), condition=%wide.region_10.11_spmd, body=%wide.region_5.10_spmd.sunk | while | flops 137527360 | bytes 26879640 | solution.py:116
  1819.9 269.9 %collective-permute-done.1 = bf16[16,8192]{1,0:T(8,128)(2,1)S(1)} collective-permute-done((bf16[16,8192]{1,0:T(8,128)(2,1)S(1)}, bf16[16,8192]{1,0:T(8,128)(2,1)S(1)}, u32[]{:S(2)}, u32[]{:S(2)}) %collective-permute-start.1) | collective-permute-done | bytes 262176 | tf_op jit(solution)/shard_map/while/body/eval_jaxpr/ppermute | solution.py:14
  2089.8 10.7 conditional.5
  2112.1 10.7 conditional.5
  2134.5 10.7 conditional.5
  2156.8 10.7 conditional.5
  2179.1 10.7 conditional.5
  2201.4 10.7 conditional.5
  2223.8 10.7 conditional.5
  2246.1 10.7 conditional.5
  2283.3 90.4 %reduce-scatter.5.cloned.1.call-done = bf16[1024,128]{1,0:T(8,128)(2,1)} async-done(((bf16[8192,128]{1,0:T(8,128)(2,1)}), bf16[1024,128]{1,0:T(8,128)(2,1)}) %reduce-scatter.5.cloned.1.call-update) | async-done | bytes 262160 | tf_op jit(solution)/shard_map/reduce_scatter | solution.py:134
  2375.6 99.9 %reduce-scatter.3.cloned.1.call-done = bf16[1024,128]{1,0:T(8,128)(2,1)} async-done(((bf16[8192,128]{1,0:T(8,128)(2,1)}), bf16[1024,128]{1,0:T(8,128)(2,1)}) %reduce-scatter.3.cloned.1.call-update) | async-done | bytes 262160 | tf_op jit(solution)/shard_map/reduce_scatter | solution.py:131
  (1481 shorter events, 1663.9 us)
Async XLA Ops:
  7.2 125.7 %all-gather.2.cloned.1.call-start = ((), (), s32[]{:S(2)}) async-start(), calls=%async_computation.2 | async-start | bytes 2129920 | tf_op jit(solution)/shard_map/all_gather | solution.py:65
  7.9 2365.8 %reduce-scatter.5.cloned.1.call-start = ((), (), s32[]{:S(2)}) async-start(), calls=%async_computation.4 | async-start | bytes 2359296 | tf_op jit(solution)/shard_map/reduce_scatter | solution.py:134
  337.2 13.0 collective-permute-start
  352.9 10.4 collective-permute-start
  366.1 13.0 collective-permute-start
  381.8 10.4 collective-permute-start
  395.0 13.0 collective-permute-start
  410.8 10.4 collective-permute-start
  423.9 10.4 collective-permute-start
  437.1 10.4 collective-permute-start
  450.3 10.4 collective-permute-start
  463.4 10.4 collective-permute-start
  476.6 10.4 collective-permute-start
  489.8 10.4 collective-permute-start
  502.9 10.4 collective-permute-start
  516.1 10.4 collective-permute-start
  529.3 10.4 collective-permute-start
  542.4 10.4 collective-permute-start
  555.6 10.4 collective-permute-start
  568.8 10.4 collective-permute-start
  581.9 10.4 collective-permute-start
  595.1 10.4 collective-permute-start
  608.3 10.4 collective-permute-start
  621.4 10.4 collective-permute-start
  634.6 10.4 collective-permute-start
  647.8 10.4 collective-permute-start
  660.9 10.4 collective-permute-start
  674.1 10.4 collective-permute-start
  687.3 10.4 collective-permute-start
  700.4 10.4 collective-permute-start
  713.6 10.4 collective-permute-start
  726.8 10.4 collective-permute-start
  739.9 10.4 collective-permute-start
  753.1 10.4 collective-permute-start
  766.3 10.4 collective-permute-start
  779.4 10.4 collective-permute-start
  792.6 10.4 collective-permute-start
  805.8 10.4 collective-permute-start
  818.9 10.4 collective-permute-start
  832.1 10.4 collective-permute-start
  845.3 10.4 collective-permute-start
  858.4 10.4 collective-permute-start
  871.6 10.4 collective-permute-start
  884.8 10.4 collective-permute-start
  897.9 10.4 collective-permute-start
  911.1 10.4 collective-permute-start
  924.3 10.4 collective-permute-start
  937.4 10.4 collective-permute-start
  950.6 10.4 collective-permute-start
  963.8 10.4 collective-permute-start
  976.9 10.4 collective-permute-start
  1058.3 11.1 collective-permute-start.1
  1083.6 11.1 collective-permute-start.1
  1109.0 11.1 collective-permute-start.1
  1134.3 11.1 collective-permute-start.1
  1815.1 274.8 %collective-permute-start.1 = (bf16[16,8192]{1,0:T(8,128)(2,1)S(1)}, bf16[16,8192]{1,0:T(8,128)(2,1)S(1)}, u32[]{:S(2)}, u32[]{:S(2)}) collective-permute-start(bf16[16,8192]{1,0:T(8,128)(2,1)S(1)} %get-tuple-element.721), channel_id=1, source_target_pairs={{8,0},{16,8},{24,16},{32,24},{40,32},{48,40},{56,48},{64,56},{72,6... | collective-permute-start | bytes 786440 | tf_op jit(solution)/shard_map/while/body/eval_jaxpr/ppermute | solution.py:14
  2100.5 11.6 collective-permute-start.1
  2122.9 11.6 collective-permute-start.1
  2145.2 11.6 collective-permute-start.1
  2167.5 11.6 collective-permute-start.1
  2189.8 11.6 collective-permute-start.1
  2212.2 11.6 collective-permute-start.1
  2234.5 11.6 collective-permute-start.1
  2279.6 195.9 %reduce-scatter.3.cloned.1.call-start = ((), (), s32[]{:S(2)}) async-start(), calls=%async_computation.3 | async-start | bytes 2359296 | tf_op jit(solution)/shard_map/reduce_scatter | solution.py:131
  (108 other events, 1125.3 us)
Sparse Core Ops, SparseCore 0:
  10.1 122.8 all-gather.1
  2279.7 93.9 reduce-scatter.4
  2379.0 96.3 reduce-scatter.2
where the time goes:
time: 2500 us; the launch traced here: 2480 us
  waiting for transfers between devices  1200 us (48%)
  starting transfers between devices  607 us (24%)
  local copies, waits for them, and re-layouts  339 us (14%)
  other arithmetic  241 us (10%)
  matrix products  81.7 us (3%)
    ppermute x142, waiting for transfers between devices, shifted(): lax.ppermute(value, axis, [(source, source + steps) for source in range(l...  880 us
    ppermute x142, starting transfers between devices, shifted(): lax.ppermute(value, axis, [(source, source + steps) for source in range(l...  607 us
    dynamic_slice x355, local copies, waits for them, and re-layouts, store_slot(): kept = jnp.where(valid, fresh, table[slot])  208 us
    dynamic_update_slice x213, other arithmetic, store_slot(): return lax.dynamic_update_index_in_dim(table, kept, slot, 0)  208 us
    all_gather x1, waiting for transfers between devices, local(): batches = lax.all_gather(inputs, 'section', axis=2, tiled=True)  125 us
    reduce_scatter x1, waiting for transfers between devices, local(): lax.psum_scatter(term_first.astype(jnp.bfloat16), 'dp', scatter_dimension...  99.9 us
    reduce_scatter x1, waiting for transfers between devices, local(): lax.psum_scatter(term_second.astype(jnp.bfloat16), 'dp', scatter_dimensio...  90.4 us
    broadcast_in_dim x126, local copies, waits for them, and re-layouts, local(): narrow = jnp.zeros((per_rows, inner), jnp.bfloat16)  75.1 us
  transfers between devices with their start and end apart: 145, of which 144 were waited for; matrix products, arithmetic and copies ran while one was open for 9% of the time, Pallas kernels for 0%

commit v1 on v0

v1 whole, which is shorter than its diff:
```python
import functools
import math

import jax
import jax.numpy as jnp
from jax import lax
from jax.experimental import pallas as pl
from jax.experimental.pallas import tpu as pltpu
from jax.sharding import Mesh, PartitionSpec as P

epsilon = 1e-05
f32 = jnp.float32
bf16 = jnp.bfloat16

D = 8192
HD = 128
LAYERS = 8
ROWS = 16
PARTS = 8
SLICE = D // PARTS
WIDE = SLICE + HD
SLOTS = 4
AHEAD = 3
NT = (((1,), (1,)), ((), ()))


def fetch_weights(place, pieces_in, pieces_out, held_in, held_out, sems, layer):
    slot = lax.rem(layer, SLOTS)
    apart = lax.rem(layer // 2 - place[1] + 4, 4)
    other = (lax.rem(layer, 2) != place[2]).astype(jnp.int32)
    which = apart * 2 + other
    for index in range(8):

        @pl.when(which == index)
        def _():
            pltpu.make_async_copy(pieces_in[index], held_in.at[slot], sems.at[0, slot]).start()
            pltpu.make_async_copy(pieces_out[index], held_out.at[slot], sems.at[1, slot]).start()


def forward_kernel(tick, place, x_ref, gain_ref, *refs):
    pieces_in, pieces_out = refs[:8], refs[8:16]
    (_, _, sent_ref, stash_ref, small_ref) = refs[16:21]
    (held_in, held_out, hidden, scaled, wide, small, sems, out_sems) = refs[21:]

    @pl.when(place[0] == tick)
    def _():
        for layer in range(AHEAD):
            fetch_weights(place, pieces_in, pieces_out, held_in, held_out, sems, jnp.int32(layer))
        hidden[...] = x_ref[...].astype(f32)

        def step(layer, carry):
            slot = lax.rem(layer, SLOTS)

            @pl.when(layer + AHEAD < LAYERS)
            def _():
                fetch_weights(place, pieces_in, pieces_out, held_in, held_out, sems, layer + AHEAD)

            squares = jnp.zeros((ROWS, 128), f32)
            for part in range(PARTS):
                lanes = slice(part * SLICE, (part + 1) * SLICE)
                value = hidden[:, lanes]
                wide[layer, part, :, :SLICE] = value.astype(bf16)
                scaled[:, lanes] = (value * gain_ref[pl.ds(layer, 1), lanes]).astype(bf16)
                square = value * value
                for at in range(0, SLICE, 128):
                    squares = squares + square[:, at : at + 128]
            inverse = lax.rsqrt(jnp.sum(squares, axis=-1, keepdims=True) * (1.0 / D) + epsilon)
            pltpu.make_async_copy(pieces_in[0], held_in.at[slot], sems.at[0, slot]).wait()
            project = inverse * jnp.dot(
                scaled[...], held_in[slot], preferred_element_type=f32
            )
            active = (project * jax.nn.sigmoid(project)).astype(bf16)
            small[layer, 0] = project
            small[layer, 1] = jnp.broadcast_to(inverse, (ROWS, HD))
            for part in range(PARTS):
                wide[layer, part, :, SLICE:] = active
            pltpu.make_async_copy(wide.at[layer], stash_ref.at[layer], out_sems.at[layer]).start()
            pltpu.make_async_copy(pieces_out[0], held_out.at[slot], sems.at[1, slot]).wait()
            for at in range(0, D, 512):
                hidden[:, at : at + 512] += jnp.dot(
                    active, held_out[slot, :, at : at + 512], preferred_element_type=f32
                )
            return carry

        lax.fori_loop(0, LAYERS, step, 0)
        last = pltpu.make_async_copy(small, small_ref, out_sems.at[LAYERS])
        last.start()
        sent_ref[...] = hidden[...].astype(bf16)
        for layer in range(LAYERS):
            pltpu.make_async_copy(wide.at[layer], stash_ref.at[layer], out_sems.at[layer]).wait()
        last.wait()


def backward_kernel(tick, place, c_ref, gain_ref, *refs):
    pieces_in, pieces_out = refs[:8], refs[8:16]
    (stash_ref, small_in, _, sent_ref, stash_out) = refs[16:21]
    (held_in, held_out, cotangent, rounded, stash, wide, small, sems, in_sems, out_sems) = refs[21:]

    @pl.when(place[0] == tick)
    def _():
        first = pltpu.make_async_copy(small_in, small, in_sems.at[LAYERS])
        first.start()
        for back in range(AHEAD):
            layer = LAYERS - 1 - back
            fetch_weights(place, pieces_in, pieces_out, held_in, held_out, sems, jnp.int32(layer))
        for back in range(LAYERS):
            layer = LAYERS - 1 - back
            pltpu.make_async_copy(stash_ref.at[layer], stash.at[layer], in_sems.at[layer]).start()
        cotangent[...] = c_ref[...].astype(f32)
        first.wait()

        def step(back, carry):
            layer = LAYERS - 1 - back
            slot = lax.rem(layer, SLOTS)

            @pl.when(layer - AHEAD >= 0)
            def _():
                fetch_weights(place, pieces_in, pieces_out, held_in, held_out, sems, layer - AHEAD)

            for part in range(PARTS):
                lanes = slice(part * SLICE, (part + 1) * SLICE)
                value = cotangent[:, lanes].astype(bf16)
                rounded[:, lanes] = value
                wide[layer, part, :, :SLICE] = value
            pltpu.make_async_copy(pieces_out[0], held_out.at[slot], sems.at[1, slot]).wait()
            upper = lax.dot_general(
                rounded[...], held_out[slot], NT, preferred_element_type=f32
            )
            project = small[layer, 0]
            inverse = small[layer, 1]
            sigma = jax.nn.sigmoid(project)
            slope = upper * sigma * (1.0 + project * (1.0 - sigma))
            factor = (slope * inverse).astype(bf16)
            for part in range(PARTS):
                wide[layer, part, :, SLICE:] = factor
            pltpu.make_async_copy(wide.at[layer], stash_out.at[layer], out_sems.at[layer]).start()
            inner = jnp.sum(slope * project, axis=-1, keepdims=True) * (1.0 / D)
            inner = inner * inverse[:, :1] * inverse[:, :1]
            pltpu.make_async_copy(stash_ref.at[layer], stash.at[layer], in_sems.at[layer]).wait()
            pltpu.make_async_copy(pieces_in[0], held_in.at[slot], sems.at[0, slot]).wait()
            for part in range(PARTS):
                for at in range(0, SLICE, 512):
                    start = part * SLICE + at
                    lanes = slice(start, start + 512)
                    grad = lax.dot_general(
                        factor, held_in[slot, lanes, :], NT, preferred_element_type=f32
                    )
                    hidden = stash[layer, part, :, at : at + 512].astype(f32)
                    cotangent[:, lanes] += (
                        grad * gain_ref[pl.ds(layer, 1), lanes] - hidden * inner
                    )
            return carry

        lax.fori_loop(0, LAYERS, step, 0)
        sent_ref[...] = cotangent[...].astype(bf16)
        for layer in range(LAYERS):
            pltpu.make_async_copy(wide.at[layer], stash_out.at[layer], out_sems.at[layer]).wait()


STASH = jax.ShapeDtypeStruct((LAYERS, PARTS, ROWS, WIDE), bf16)
SMALL = jax.ShapeDtypeStruct((LAYERS, 2, ROWS, HD), f32)
SENT = jax.ShapeDtypeStruct((ROWS, D), bf16)
ANY = pl.BlockSpec(memory_space=pl.ANY)
VMEM = pl.BlockSpec(memory_space=pltpu.VMEM)
SMEM = pl.BlockSpec(memory_space=pltpu.SMEM)
HELD = [
    pltpu.VMEM((SLOTS, D, HD), bf16),
    pltpu.VMEM((SLOTS, HD, D), bf16),
    pltpu.VMEM((ROWS, D), f32),
    pltpu.VMEM((ROWS, D), bf16),
]
PARAMS = pltpu.CompilerParams(vmem_limit_bytes=40 * 2**20)


def run_forward(tick, place, x, gains, pieces_in, pieces_out, stash, small):
    return pl.pallas_call(
        functools.partial(forward_kernel, tick),
        in_specs=[SMEM, VMEM, VMEM] + [ANY] * 18,
        out_specs=[VMEM, ANY, ANY],
        out_shape=[SENT, STASH, SMALL],
        input_output_aliases={19: 1, 20: 2},
        scratch_shapes=HELD
        + [
            pltpu.VMEM(STASH.shape, bf16),
            pltpu.VMEM(SMALL.shape, f32),
            pltpu.SemaphoreType.DMA((2, SLOTS)),
            pltpu.SemaphoreType.DMA((LAYERS + 1,)),
        ],
        compiler_params=PARAMS,
        name="team_forward",
    )(place, x, gains, *pieces_in, *pieces_out, stash, small)


def run_backward(tick, place, c, gains, pieces_in, pieces_out, stash, small, cots):
    return pl.pallas_call(
        functools.partial(backward_kernel, tick),
        in_specs=[SMEM, VMEM, VMEM] + [ANY] * 19,
        out_specs=[VMEM, ANY],
        out_shape=[SENT, STASH],
        input_output_aliases={21: 1},
        scratch_shapes=HELD
        + [
            pltpu.VMEM(STASH.shape, bf16),
            pltpu.VMEM(STASH.shape, bf16),
            pltpu.VMEM(SMALL.shape, f32),
            pltpu.SemaphoreType.DMA((2, SLOTS)),
            pltpu.SemaphoreType.DMA((LAYERS + 1,)),
            pltpu.SemaphoreType.DMA((LAYERS,)),
        ],
        compiler_params=PARAMS,
        name="team_backward",
    )(place, c, gains, *pieces_in, *pieces_out, stash, small, cots)


def along_z(value, steps):
    index = [(z % 4) * 2 + z // 4 for z in range(8)]
    pairs = [(index[z], index[(z + steps) % 8]) for z in range(8)]
    return lax.ppermute(value, ("zl", "zh"), pairs)


def swap_cores(value):
    return lax.ppermute(value, "core", [(0, 1), (1, 0)])


def along_y(value, source, target):
    return lax.ppermute(value, "y", [(source, target)])


PLANE = ("zl", "core", "x", "zh")


def exchange(stash):
    flat = stash.reshape(LAYERS * PARTS, ROWS, WIDE)
    flat = lax.all_to_all(flat, PLANE, 0, 0, tiled=True)
    return flat.reshape(LAYERS * PARTS * ROWS, WIDE)


def local(inputs, gain, w_in, w_out):
    y = lax.axis_index("y")
    place = jnp.stack([y, lax.axis_index("zl"), lax.axis_index("core")]).astype(jnp.int32)
    own_in, own_out = w_in[0], w_out[0]
    before_in, after_out = along_z(own_in, 1), along_z(own_out, -1)
    before_out, after_in = along_z(own_out, 1), along_z(own_in, -1)
    far_in, far_out = along_z(before_in, 1), along_z(after_out, -1)
    pieces_in = [own_in, swap_cores(own_in), after_in, swap_cores(after_in)]
    pieces_in += [far_in, swap_cores(far_in), before_in, swap_cores(before_in)]
    pieces_out = [own_out, swap_cores(own_out), after_out, swap_cores(after_out)]
    pieces_out += [far_out, swap_cores(far_out), before_out, swap_cores(before_out)]
    gains = lax.all_gather(gain, ("zl", "core"), axis=0, tiled=True)
    x = lax.all_to_all(inputs, ("zl", "core"), 0, 0, tiled=True)
    x = x.transpose(1, 0, 2).reshape(ROWS, SLICE)
    x = lax.all_gather(x, "y", axis=1, tiled=True)

    stash = jnp.zeros(STASH.shape, bf16)
    small = jnp.zeros(SMALL.shape, f32)
    for tick in range(8):
        x, stash, small = run_forward(tick, place, x, gains, pieces_in, pieces_out, stash, small)
        if tick < 7:
            x = along_y(x, tick, tick + 1)
    cots = jnp.zeros(STASH.shape, bf16)
    for tick in range(7, -1, -1):
        x, cots = run_backward(tick, place, x, gains, pieces_in, pieces_out, stash, small, cots)
        if tick > 0:
            x = along_y(x, tick, tick - 1)

    first = exchange(stash)
    second = exchange(cots)
    part = lax.axis_index("x") * 2 + lax.axis_index("zh")
    own_gain = lax.dynamic_slice(gain, (0, part * SLICE), (1, SLICE)).reshape(SLICE, 1)
    scale = 1.0 / math.sqrt(LAYERS * PARTS * ROWS)
    rows = (((0,), (0,)), ((), ()))
    sum_in = lax.dot_general(
        first[:, :SLICE], second[:, SLICE:], rows, preferred_element_type=f32
    )
    sum_out = lax.dot_general(
        first[:, SLICE:], second[:, :SLICE], rows, preferred_element_type=f32
    )
    grad_in = (sum_in * own_gain * scale).astype(bf16)[None]
    grad_out = (sum_out * scale).astype(bf16)[None]
    return (grad_in, grad_out)


def solution(mesh):
    axes = ("y", "zl", "core", "x", "zh")
    split = Mesh(mesh.devices.reshape(8, 4, 2, 4, 2), axes)
    section, replica = ("y", "zl", "core"), ("x", "zh")
    return jax.shard_map(
        local,
        mesh=split,
        in_specs=(
            P(None, replica, section),
            P(section, None),
            P(section, None, None),
            P(section, None, None),
        ),
        out_specs=(P(section, replica, None), P(section, None, replica)),
        check_vma=False,
    )
```

time: 2500 us -> 697 us (0.28)
  waiting for transfers between devices: 1200 us -> 504 us
  starting transfers between devices: 607 us -> 93.4 us
  local copies, waits for them, and re-layouts: 339 us -> 9.12 us
  other arithmetic: 241 us -> 0.08 us
  matrix products: 81.7 us -> 5.18 us
  Pallas kernels: 0 us -> 47.5 us
  blocking collectives: 0 us -> 34.8 us
    ppermute x142 -> x28, starting transfers between devices: 607 us -> 63.9 us  [the longest x6 27 us: along_z(): return lax.ppermute(value, ('zl', 'zh'), pairs)]
    ppermute x142 -> x28, waiting for transfers between devices: 880 us -> 449 us  [the longest x14 342 us: along_y(): return lax.ppermute(value, 'y', [(source, target)])]
    dynamic_update_slice x213 -> x0, other arithmetic: 208 us -> none  [store_slot(): return lax.dynamic_update_index_in_dim(table, kept, slot, 0)]
    dynamic_slice x355 -> x1, local copies, waits for them, and re-layouts: 208 us -> 0.69 us  [local(): lax.dynamic_slice(gain, (0, part * SLICE), (1, SLICE)).reshape(SLICE, 1)]
    reduce_scatter x2 -> x0, waiting for transfers between devices: 190 us -> none  [the longest x1 99.9 us: local(): lax.psum_scatter(term_first.astype(jnp.bfloat16), 'dp', scatter_dimension...]
    all_gather x1 -> x0, waiting for transfers between devices: 125 us -> none  [local(): batches = lax.all_gather(inputs, 'section', axis=2, tiled=True)]
    dot_general x42 -> x2, matrix products: 81.7 us -> 5.18 us  [the longest x1 3.06 us: local(): lax.dot_general(first[:, :SLICE], second[:, SLICE:], rows, preferred_elem...]
    broadcast_in_dim x128 -> x1, local copies, waits for them, and re-layouts: 75.1 us -> 0.01 us  [local(): small = jnp.zeros(SMALL.shape, f32)]
  transfers between devices with their start and end apart: 145 -> 31, of which waited for: 144 -> 8; matrix products, arithmetic and copies ran while one was open for 9% -> 0% of each run, Pallas kernels for 0% -> 4%
where the time goes in v1:
time: 697 us; the launch traced here: 696 us
  waiting for transfers between devices  504 us (72%)
  starting transfers between devices  93.4 us (13%)
  Pallas kernels  47.5 us (7%)
  blocking collectives  34.8 us (5%)
  local copies, waits for them, and re-layouts  9.12 us (1%)
    ppermute x14, waiting for transfers between devices, along_y(): return lax.ppermute(value, 'y', [(source, target)])  342 us
    ppermute x6, waiting for transfers between devices, along_z(): return lax.ppermute(value, ('zl', 'zh'), pairs)  107 us
    all_to_all x2, waiting for transfers between devices, exchange(): flat = lax.all_to_all(flat, PLANE, 0, 0, tiled=True)  55.6 us
    pallas_call x8, Pallas kernels, run_backward(): pl.pallas_call(functools.partial(backward_kernel, tick), in_specs=[SMEM,...  30.4 us
    ppermute x6, starting transfers between devices, along_z(): return lax.ppermute(value, ('zl', 'zh'), pairs)  27 us
    ppermute x8, starting transfers between devices, swap_cores(): return lax.ppermute(value, 'core', [(0, 1), (1, 0)])  26.1 us
    all_to_all x2, starting transfers between devices, exchange(): flat = lax.all_to_all(flat, PLANE, 0, 0, tiled=True)  25.8 us
    all_gather x1, blocking collectives, local(): x = lax.all_gather(x, 'y', axis=1, tiled=True)  20 us
  transfers between devices with their start and end apart: 31, of which 8 were waited for; matrix products, arithmetic and copies ran while one was open for 0% of the time, Pallas kernels for 4%

profile of v1, /device:TPU:1, one launch (start us, length us, event | category | flops | bytes accessed | tf_op | source)
XLA Modules:
  0.0 695.7 jit_solution(12732062786191246730)
XLA Ops:
  0.6 11.6 %collective-permute-start.8 = (bf16[128,8192]{1,0:T(8,128)(2,1)}, bf16[128,8192]{1,0:T(8,128)(2,1)}, u32[]{:S(2)}, u32[]{:S(2)}) collective-permute-start(bf16[128,8192]{1,0:T(8,128)(2,1)} %bitcast.60), channel_id=1, source_target_pairs={{0,49},{16,0},{32,16},{48,32},{1,48},{17,1},{33,17},{49,33},{2,51}... | collective-permute-start | bytes 6291464 | tf_op jit(solution)/shard_map/ppermute | solution.py:218
  12.3 1.9 collective-permute-start.3
  14.2 1.9 collective-permute-start.12
  16.1 4.6 collective-permute-start.1
  20.7 3.4 collective-permute-start
  24.2 32.7 %collective-permute-done.8.refs_10_ = bf16[128,8192]{1,0:T(8,128)(2,1)} collective-permute-done((bf16[128,8192]{1,0:T(8,128)(2,1)}, bf16[128,8192]{1,0:T(8,128)(2,1)}, u32[]{:S(2)}, u32[]{:S(2)}) %collective-permute-start.8) | collective-permute-done | bytes 2097184 | tf_op jit(solution)/shard_map/ppermute | solution.py:218
  56.9 4.6 collective-permute-start.7
  61.8 5.0 collective-permute-start.10
  66.8 40.0 %collective-permute-done.12.refs_14_ = bf16[128,8192]{1,0:T(8,128)(2,1)} collective-permute-done((bf16[128,8192]{1,0:T(8,128)(2,1)}, bf16[128,8192]{1,0:T(8,128)(2,1)}, u32[]{:S(2)}, u32[]{:S(2)}) %collective-permute-start.12) | collective-permute-done | bytes 2097184 | tf_op jit(solution)/shard_map/ppermute | solution.py:218
  106.8 1.9 collective-permute-start.4
  108.7 3.8 collective-permute-start.6
  112.6 1.3 copy-done.1
  113.8 1.9 collective-permute-start.9
  115.8 2.4 collective-permute-start.13
  118.2 28.6 %collective-permute-done.10.refs_12_ = bf16[128,8192]{1,0:T(8,128)(2,1)} collective-permute-done((bf16[128,8192]{1,0:T(8,128)(2,1)}, bf16[128,8192]{1,0:T(8,128)(2,1)}, u32[]{:S(2)}, u32[]{:S(2)}) %collective-permute-start.10) | collective-permute-done | bytes 2097184 | tf_op jit(solution)/shard_map/ppermute | solution.py:218
  146.8 3.4 collective-permute-start.2
  150.2 5.1 collective-permute-done.4.refs_4_
  155.3 4.7 collective-permute-start.11
  160.0 1.4 copy-done.6
  161.4 1.9 collective-permute-start.5
  163.3 3.8 all-to-all-start
  167.0 14.8 %all-gather = f32[8,1,8192]{2,1,0:T(1,128)S(1)} all-gather(f32[1,1,8192]{2,1,0:T(1,128)} %bitcast.82), channel_id=1, replica_groups=mesh['y'=8,'zl'=4,'core'=2,'x'=4,'zh'=2] {'zl','core'}, dimensions={0}, use_global_device_ids=true | all-gather | bytes 294912 | tf_op jit(solution)/shard_map/all_gather | solution.py:249
  182.1 20.0 %all_gather.6.x_ref = bf16[16,8192]{1,0:T(8,128)(2,1)S(1)} all-gather(bf16[16,1024]{1,0:T(8,128)(2,1)S(1)} %copy_bitcast_fusion.1), channel_id=1, replica_groups=mesh['y'=8,'zl'=4,'core'=2,'x'=4,'zh'=2] {'y'}, dimensions={1}, use_global_device_ids=true | all-gather | bytes 294912 | tf_op jit(solution)/shard_map/all_gather | solution.py:252
  202.1 1.6 broadcast_1_refs_16__refs_18_.2.clone.refs_16_
  203.7 1.6 copy-done.2
  205.3 11.9 %team_forward.8 = (bf16[16,8192]{1,0:T(8,128)(2,1)S(1)}, bf16[8,8,16,1152]{3,2,1,0:T(8,128)(2,1)}, f32[8,2,16,128]{3,2,1,0:T(8,128)S(1)}) custom-call(s32[3]{0:T(128)S(1)} %pad_add_fusion.place, bf16[16,8192]{1,0:T(8,128)(2,1)S(1)} %all_gather.6.x_ref, f32[8,8192]{1,0:T(8,128)S(1)} %bitcast.43, ...), custom_call_target="tpu_custom_call", output_to_operand_aliasing={{1}: (19, {}), {2}: (20, {})} | custom-call | tf_op jit(solution)/shard_map/team_forward/pallas_call | solution.py:176
  217.2 1.3 collective-permute-start.14
  218.5 3.3 collective-permute-done.14.x_ref
  221.8 0.7 team_forward.9
  222.5 0.7 collective-permute-start.15
  223.2 0.7 team_forward.10
  223.9 0.7 collective-permute-start.16
  224.6 0.7 team_forward.11
  225.3 0.7 collective-permute-start.17
  226.0 0.7 team_forward.12
  226.7 0.7 collective-permute-start.18
  227.4 0.7 team_forward.13
  228.2 0.7 collective-permute-start.19
  228.9 0.7 team_forward.14
  229.6 0.7 collective-permute-start.20
  230.3 0.9 team_forward.15
  231.2 15.4 %all-to-all-start.1 = ((bf16[64,16,1152]{2,1,0:T(8,128)(2,1)}), bf16[64,16,1152]{2,1,0:T(8,128)(2,1)}, u32[]{:S(2)}, u32[]{:S(2)}) async-start(bf16[64,16,1152]{2,1,0:T(8,128)(2,1)} %bitcast.59), calls=%async_computation.1 | async-start | bytes 4718592 | tf_op jit(solution)/shard_map/all_to_all | solution.py:234
  246.6 1.7 broadcast_1_refs_16__refs_18_.2.refs_18_
  248.2 0.8 copy-done.3
  249.0 0.8 team_backward.8
  249.8 0.7 collective-permute-start.21
  250.5 0.8 team_backward.9
  251.3 0.7 collective-permute-start.22
  252.0 0.8 team_backward.10
  252.8 0.7 collective-permute-start.23
  253.5 0.8 team_backward.11
  254.2 0.7 collective-permute-start.24
  254.9 0.8 team_backward.12
  256.4 0.8 team_backward.13
  257.2 0.7 collective-permute-start.26
  257.9 0.8 team_backward.14
  258.7 1.3 collective-permute-start.27
  260.0 338.8 %collective-permute-done.27.c_ref = bf16[16,8192]{1,0:T(8,128)(2,1)S(1)} collective-permute-done((bf16[16,8192]{1,0:T(8,128)(2,1)S(1)}, bf16[16,8192]{1,0:T(8,128)(2,1)S(1)}, u32[]{:S(2)}, u32[]{:S(2)}) %collective-permute-start.27) | collective-permute-done | bytes 262176 | tf_op jit(solution)/shard_map/ppermute | solution.py:226
  598.9 24.9 %team_backward.15 = (bf16[16,8192]{1,0:T(8,128)(2,1)}, bf16[8,8,16,1152]{3,2,1,0:T(8,128)(2,1)}) custom-call(s32[3]{0:T(128)S(1)} %pad_add_fusion.place, bf16[16,8192]{1,0:T(8,128)(2,1)S(1)} %collective-permute-done.27.c_ref, f32[8,8192]{1,0:T(8,128)S(1)} %bitcast.58, bf16[8192,128]{1,0:T(8,128)(2,1)S(1)} %bitcast.42, ...), custom_call_target="tpu_custom_call", output_to_operand_aliasing={{1}: (21, {})} | custom-call | tf_op jit(solution)/shard_map/team_backward/pallas_call | solution.py:195
  623.8 10.4 %all-to-all-start.2 = ((bf16[64,16,1152]{2,1,0:T(8,128)(2,1)}), bf16[64,16,1152]{2,1,0:T(8,128)(2,1)S(1)}, u32[]{:S(2)}, u32[]{:S(2)}) async-start(bf16[64,16,1152]{2,1,0:T(8,128)(2,1)} %bitcast.79), calls=%async_computation.2 | async-start | bytes 4718592 | tf_op jit(solution)/shard_map/all_to_all | solution.py:234
  634.2 0.7 constant_dynamic-slice_fusion
  634.9 55.6 %all-to-all-done.2 = bf16[64,16,1152]{2,1,0:T(8,128)(2,1)S(1)} async-done(((bf16[64,16,1152]{2,1,0:T(8,128)(2,1)}), bf16[64,16,1152]{2,1,0:T(8,128)(2,1)S(1)}, u32[]{:S(2)}, u32[]{:S(2)}) %all-to-all-start.2) | async-done | bytes 2359328 | tf_op jit(solution)/shard_map/all_to_all | solution.py:234
  690.6 2.1 fusion.19
  692.7 3.1 fusion.22
  (39 shorter events, 1.3 us)
Async XLA Ops:
  0.6 203.1 %copy-start = (bf16[1,8192,128]{2,1,0:T(8,128)(2,1)S(1)}, bf16[1,8192,128]{2,1,0:T(8,128)(2,1)}, u32[]{:S(2)}) copy-start(bf16[1,8192,128]{2,1,0:T(8,128)(2,1)} %param.6) | copy-start | bytes 6291460
  0.6 56.2 %collective-permute-start.8 = (bf16[128,8192]{1,0:T(8,128)(2,1)}, bf16[128,8192]{1,0:T(8,128)(2,1)}, u32[]{:S(2)}, u32[]{:S(2)}) collective-permute-start(bf16[128,8192]{1,0:T(8,128)(2,1)} %bitcast.60), channel_id=1, source_target_pairs={{0,49},{16,0},{32,16},{48,32},{1,48},{17,1},{33,17},{49,33},{2,51}... | collective-permute-start | bytes 6291464 | tf_op jit(solution)/shard_map/ppermute | solution.py:218
  12.3 49.5 %collective-permute-start.3 = (bf16[8192,128]{1,0:T(8,128)(2,1)}, bf16[8192,128]{1,0:T(8,128)(2,1)S(1)}, u32[]{:S(2)}, u32[]{:S(2)}) collective-permute-start(bf16[8192,128]{1,0:T(8,128)(2,1)} %bitcast.24), channel_id=1, source_target_pairs={{0,16},{16,32},{32,48},{48,1},{1,17},{17,33},{33,49},{49,0},{2,18}... | collective-permute-start | bytes 6291464 | tf_op jit(solution)/shard_map/ppermute | solution.py:218
  14.2 92.6 %collective-permute-start.12 = (bf16[128,8192]{1,0:T(8,128)(2,1)}, bf16[128,8192]{1,0:T(8,128)(2,1)}, u32[]{:S(2)}, u32[]{:S(2)}) collective-permute-start(bf16[128,8192]{1,0:T(8,128)(2,1)} %bitcast.61), channel_id=1, source_target_pairs={{0,16},{16,32},{32,48},{48,1},{1,17},{17,33},{33,49},{49,0},{2,18}... | collective-permute-start | bytes 6291464 | tf_op jit(solution)/shard_map/ppermute | solution.py:218
  16.1 92.6 %collective-permute-start.1 = (bf16[8192,128]{1,0:T(8,128)(2,1)}, bf16[8192,128]{1,0:T(8,128)(2,1)}, u32[]{:S(2)}, u32[]{:S(2)}) collective-permute-start(bf16[8192,128]{1,0:T(8,128)(2,1)} %bitcast.25), channel_id=1, source_target_pairs={{0,49},{16,0},{32,16},{48,32},{1,48},{17,1},{33,17},{49,33},{2,51}... | collective-permute-start | bytes 6291464 | tf_op jit(solution)/shard_map/ppermute | solution.py:218
  20.7 91.8 %collective-permute-start = (bf16[8192,128]{1,0:T(8,128)(2,1)}, bf16[8192,128]{1,0:T(8,128)(2,1)S(1)}, u32[]{:S(2)}, u32[]{:S(2)}) collective-permute-start(bf16[8192,128]{1,0:T(8,128)(2,1)} %bitcast.26), channel_id=1, source_target_pairs={{0,8},{8,0},{1,9},{9,1},{2,10},{10,2},{3,11},{11,3},{4,12},{12,4},... | collective-permute-start | bytes 6291464 | tf_op jit(solution)/shard_map/ppermute | solution.py:222
  56.9 58.9 %collective-permute-start.7 = (bf16[128,8192]{1,0:T(8,128)(2,1)}, bf16[128,8192]{1,0:T(8,128)(2,1)S(1)}, u32[]{:S(2)}, u32[]{:S(2)}) collective-permute-start(bf16[128,8192]{1,0:T(8,128)(2,1)} %bitcast.62), channel_id=1, source_target_pairs={{0,8},{8,0},{1,9},{9,1},{2,10},{10,2},{3,11},{11,3},{4,12},{12,4},... | collective-permute-start | bytes 6291464 | tf_op jit(solution)/shard_map/ppermute | solution.py:222
  61.8 50.8 %copy-start.4 = (bf16[8192,128]{1,0:T(8,128)(2,1)}, bf16[8192,128]{1,0:T(8,128)(2,1)S(1)}, u32[]{:S(2)}) copy-start(bf16[8192,128]{1,0:T(8,128)(2,1)S(1)} %collective-permute-done.3.refs_6_) | copy-start | bytes 6291460
  61.8 85.0 %collective-permute-start.10 = (bf16[128,8192]{1,0:T(8,128)(2,1)}, bf16[128,8192]{1,0:T(8,128)(2,1)}, u32[]{:S(2)}, u32[]{:S(2)}) collective-permute-start(bf16[128,8192]{1,0:T(8,128)(2,1)} %collective-permute-done.8.refs_10_), channel_id=1, source_target_pairs={{0,49},{16,0},{32,16},{48,32},{1,48},{17,1},{33,17},{49,33},{2,51}... | collective-permute-start | bytes 6291464 | tf_op jit(solution)/shard_map/ppermute | solution.py:218
  106.8 48.5 %collective-permute-start.4 = (bf16[8192,128]{1,0:T(8,128)(2,1)S(1)}, bf16[8192,128]{1,0:T(8,128)(2,1)}, u32[]{:S(2)}, u32[]{:S(2)}) collective-permute-start(bf16[8192,128]{1,0:T(8,128)(2,1)S(1)} %collective-permute-done.3.refs_6_), channel_id=1, source_target_pairs={{0,16},{16,32},{32,48},{48,1},{1,17},{17,33},{33,49},{49,0},{2,18}... | collective-permute-start | bytes 6291464 | tf_op jit(solution)/shard_map/ppermute | solution.py:218
  108.7 51.2 %collective-permute-start.6 = (bf16[8192,128]{1,0:T(8,128)(2,1)S(1)}, bf16[8192,128]{1,0:T(8,128)(2,1)S(1)}, u32[]{:S(2)}, u32[]{:S(2)}) collective-permute-start(bf16[8192,128]{1,0:T(8,128)(2,1)S(1)} %collective-permute-done.3.refs_6_), channel_id=1, source_target_pairs={{0,8},{8,0},{1,9},{9,1},{2,10},{10,2},{3,11},{11,3},{4,12},{12,4},... | collective-permute-start | bytes 6291464 | tf_op jit(solution)/shard_map/ppermute | solution.py:222
  112.6 1.3 copy-start.1
  113.8 88.3 %collective-permute-start.9 = (bf16[128,8192]{1,0:T(8,128)(2,1)}, bf16[128,8192]{1,0:T(8,128)(2,1)}, u32[]{:S(2)}, u32[]{:S(2)}) collective-permute-start(bf16[128,8192]{1,0:T(8,128)(2,1)} %collective-permute-done.8.refs_10_), channel_id=1, source_target_pairs={{0,8},{8,0},{1,9},{9,1},{2,10},{10,2},{3,11},{11,3},{4,12},{12,4},... | collective-permute-start | bytes 6291464 | tf_op jit(solution)/shard_map/ppermute | solution.py:222
  115.8 44.2 %copy-start.5 = (bf16[128,8192]{1,0:T(8,128)(2,1)}, bf16[128,8192]{1,0:T(8,128)(2,1)S(1)}, u32[]{:S(2)}) copy-start(bf16[128,8192]{1,0:T(8,128)(2,1)S(1)} %collective-permute-done.7.refs_9_) | copy-start | bytes 6291460
  115.8 86.3 %collective-permute-start.13 = (bf16[128,8192]{1,0:T(8,128)(2,1)}, bf16[128,8192]{1,0:T(8,128)(2,1)}, u32[]{:S(2)}, u32[]{:S(2)}) collective-permute-start(bf16[128,8192]{1,0:T(8,128)(2,1)} %collective-permute-done.12.refs_14_), channel_id=1, source_target_pairs={{0,8},{8,0},{1,9},{9,1},{2,10},{10,2},{3,11},{11,3},{4,12},{12,4},... | collective-permute-start | bytes 6291464 | tf_op jit(solution)/shard_map/ppermute | solution.py:222
  146.8 55.4 %collective-permute-start.2 = (bf16[8192,128]{1,0:T(8,128)(2,1)}, bf16[8192,128]{1,0:T(8,128)(2,1)}, u32[]{:S(2)}, u32[]{:S(2)}) collective-permute-start(bf16[8192,128]{1,0:T(8,128)(2,1)} %collective-permute-done.1.refs_2_), channel_id=1, source_target_pairs={{0,8},{8,0},{1,9},{9,1},{2,10},{10,2},{3,11},{11,3},{4,12},{12,4},... | collective-permute-start | bytes 6291464 | tf_op jit(solution)/shard_map/ppermute | solution.py:222
  155.3 46.8 %collective-permute-start.11 = (bf16[128,8192]{1,0:T(8,128)(2,1)}, bf16[128,8192]{1,0:T(8,128)(2,1)}, u32[]{:S(2)}, u32[]{:S(2)}) collective-permute-start(bf16[128,8192]{1,0:T(8,128)(2,1)} %collective-permute-done.10.refs_12_), channel_id=1, source_target_pairs={{0,8},{8,0},{1,9},{9,1},{2,10},{10,2},{3,11},{11,3},{4,12},{12,4},... | collective-permute-start | bytes 6291464 | tf_op jit(solution)/shard_map/ppermute | solution.py:222
  160.0 1.4 copy-start.6
  161.4 40.8 %collective-permute-start.5 = (bf16[8192,128]{1,0:T(8,128)(2,1)}, bf16[8192,128]{1,0:T(8,128)(2,1)}, u32[]{:S(2)}, u32[]{:S(2)}) collective-permute-start(bf16[8192,128]{1,0:T(8,128)(2,1)} %collective-permute-done.4.refs_4_), channel_id=1, source_target_pairs={{0,8},{8,0},{1,9},{9,1},{2,10},{10,2},{3,11},{11,3},{4,12},{12,4},... | collective-permute-start | bytes 6291464 | tf_op jit(solution)/shard_map/ppermute | solution.py:222
  163.3 18.8 %all-to-all-start = ((bf16[8,16,128]{2,1,0:T(8,128)(2,1)}), bf16[8,16,128]{2,1,0:T(8,128)(2,1)S(1)}, u32[]{:S(2)}, u32[]{:S(2)}) async-start(bf16[8,16,128]{2,1,0:T(8,128)(2,1)} %param.4), calls=%async_computation | async-start | bytes 65536 | tf_op jit(solution)/shard_map/all_to_all | solution.py:250
  203.7 1.6 copy-start.2
  217.2 4.6 collective-permute-start.14
  222.5 0.7 collective-permute-start.15
  223.9 0.7 collective-permute-start.16
  225.3 0.7 collective-permute-start.17
  226.7 0.7 collective-permute-start.18
  228.2 0.7 collective-permute-start.19
  229.6 0.7 collective-permute-start.20
  231.2 392.6 %all-to-all-start.1 = ((bf16[64,16,1152]{2,1,0:T(8,128)(2,1)}), bf16[64,16,1152]{2,1,0:T(8,128)(2,1)}, u32[]{:S(2)}, u32[]{:S(2)}) async-start(bf16[64,16,1152]{2,1,0:T(8,128)(2,1)} %bitcast.59), calls=%async_computation.1 | async-start | bytes 4718592 | tf_op jit(solution)/shard_map/all_to_all | solution.py:234
  246.6 2.4 copy-start.3
  249.8 0.7 collective-permute-start.21
  251.3 0.7 collective-permute-start.22
  252.8 0.7 collective-permute-start.23
  254.2 0.7 collective-permute-start.24
  255.7 0.7 collective-permute-start.25
  257.2 0.7 collective-permute-start.26
  258.7 340.1 %collective-permute-start.27 = (bf16[16,8192]{1,0:T(8,128)(2,1)S(1)}, bf16[16,8192]{1,0:T(8,128)(2,1)S(1)}, u32[]{:S(2)}, u32[]{:S(2)}) collective-permute-start(bf16[16,8192]{1,0:T(8,128)(2,1)S(1)} %get-tuple-element.77), channel_id=1, source_target_pairs={{64,0},{65,1},{66,2},{67,3},{68,4},{69,5},{70,6},{71,7},{72,8},{73... | collective-permute-start | bytes 786440 | tf_op jit(solution)/shard_map/ppermute | solution.py:226
  623.8 66.7 %all-to-all-start.2 = ((bf16[64,16,1152]{2,1,0:T(8,128)(2,1)}), bf16[64,16,1152]{2,1,0:T(8,128)(2,1)S(1)}, u32[]{:S(2)}, u32[]{:S(2)}) async-start(bf16[64,16,1152]{2,1,0:T(8,128)(2,1)} %bitcast.79), calls=%async_computation.2 | async-start | bytes 4718592 | tf_op jit(solution)/shard_map/all_to_all | solution.py:234

commit v2 on v1

v2 whole, which is shorter than its diff:
```python
import functools
import math

import jax
import jax.numpy as jnp
from jax import lax
from jax.experimental import pallas as pl
from jax.experimental.pallas import tpu as pltpu
from jax.sharding import Mesh, PartitionSpec as P

epsilon = 1e-05
f32 = jnp.float32
bf16 = jnp.bfloat16

D = 8192
HD = 128
LAYERS = 8
ROWS = 16
PARTS = 8
SLICE = D // PARTS
WIDE = SLICE + HD
LAST = 7
FIRST_EXCHANGE = 7
SLOTS = 4
AHEAD = 3
EARLY = 2


def fetch(place, pieces, held, sems, layer):
    layer = jnp.int32(layer)
    slot = lax.rem(layer, held.shape[0])
    apart = lax.rem(layer // 2 - place[1] + 4, 4)
    other = (lax.rem(layer, 2) != place[2]).astype(jnp.int32)
    which = apart * 2 + other
    for index in range(8):

        @pl.when(which == index)
        def _():
            pltpu.make_async_copy(pieces[index], held.at[slot], sems.at[slot]).start()


def await_fetch(pieces, held, sems, layer):
    slot = lax.rem(jnp.int32(layer), held.shape[0])
    pltpu.make_async_copy(pieces[0], held.at[slot], sems.at[slot]).wait()
    return slot


def forward_pass(refs, fetches, get_in, get_out):
    x_ref, sent_ref, stash_ref, small_ref = refs[:4]
    hidden, narrow, wide, small, out_sems = refs[4:]
    for layer in range(AHEAD):
        fetches(layer)
    hidden[...] = x_ref[...].astype(f32)

    def step(layer, carry):
        @pl.when(layer + AHEAD < LAYERS)
        def _():
            fetches(layer + AHEAD)

        squares = jnp.zeros((ROWS, 128), f32)
        for part in range(PARTS):
            lanes = slice(part * SLICE, (part + 1) * SLICE)
            value = hidden[:, lanes]
            wide[layer, part, :, :SLICE] = value.astype(bf16)
            narrow[:, lanes] = value.astype(bf16)
            square = value * value
            for at in range(0, SLICE, 128):
                squares = squares + square[:, at : at + 128]
        inverse = lax.rsqrt(jnp.sum(squares, axis=-1, keepdims=True) * (1.0 / D) + epsilon)
        weights = get_in(layer)
        project = inverse * jnp.dot(narrow[...], weights[...], preferred_element_type=f32)
        active = (project * jax.nn.sigmoid(project)).astype(bf16)
        small[layer, 0] = project
        small[layer, 1] = jnp.broadcast_to(inverse, (ROWS, HD))
        for part in range(PARTS):
            wide[layer, part, :, SLICE:] = active
        pltpu.make_async_copy(wide.at[layer], stash_ref.at[layer], out_sems.at[layer]).start()
        weights = get_out(layer)
        for at in range(0, D, 512):
            hidden[:, at : at + 512] += jnp.dot(
                active, weights[:, at : at + 512], preferred_element_type=f32
            )
        return carry

    lax.fori_loop(0, LAYERS, step, 0)
    last = pltpu.make_async_copy(small, small_ref, out_sems.at[LAYERS])
    last.start()
    sent_ref[...] = hidden[...].astype(bf16)
    for layer in range(LAYERS):
        pltpu.make_async_copy(wide.at[layer], stash_ref.at[layer], out_sems.at[layer]).wait()
    last.wait()


def early_kernel(tick, place, x_ref, *refs):
    pieces_in, pieces_out = refs[:8], refs[8:16]
    refs = refs[16:] if tick == 0 else refs[18:]
    state, (held_in, held_out, in_sems, held_sems) = refs[3:8], refs[8:]

    @pl.when(place[0] == tick)
    def _():
        def fetches(layer):
            fetch(place, pieces_in, held_in, in_sems, layer)
            fetch(place, pieces_out, held_out, held_sems, layer)

        forward_pass(
            (x_ref,) + tuple(refs[:3]) + tuple(state),
            fetches,
            lambda layer: held_in.at[await_fetch(pieces_in, held_in, in_sems, layer)],
            lambda layer: held_out.at[await_fetch(pieces_out, held_out, held_sems, layer)],
        )


def forward_kernel(tick, place, x_ref, held_out, *refs):
    pieces_in, refs = refs[:8], refs[10:]
    state, (held_in, in_sems) = refs[3:8], refs[8:]

    @pl.when(place[0] == tick)
    def _():
        forward_pass(
            (x_ref,) + tuple(refs[:3]) + tuple(state),
            lambda layer: fetch(place, pieces_in, held_in, in_sems, layer),
            lambda layer: held_in.at[await_fetch(pieces_in, held_in, in_sems, layer)],
            lambda layer: held_out.at[layer],
        )


def load_kernel(place, *refs):
    pieces_out, pieces_in = refs[:8], refs[8:16]
    held_out, turned_out, turned_in = refs[17:20]
    first, second, last, sems, in_sem, out_sems, last_sem = refs[20:]
    for layer in range(LAYERS):
        fetch(place, pieces_out, held_out, sems, layer)
    fetch(place, pieces_in, last, in_sem, LAYERS - 1)

    def step(layer, carry):
        slot = lax.rem(layer, 2)
        copy = pltpu.make_async_copy(first.at[slot], turned_out.at[layer], out_sems.at[slot])

        @pl.when(layer >= 2)
        def _():
            copy.wait()

        await_fetch(pieces_out, held_out, sems, layer)
        for at in range(0, D, HD):
            first[slot, at : at + HD, :] = held_out[layer, :, at : at + HD].T
        copy.start()
        return carry

    lax.fori_loop(0, LAYERS, step, 0)
    await_fetch(pieces_in, last, in_sem, 0)
    for at in range(0, D, HD):
        second[:, at : at + HD] = last[0, at : at + HD, :].T
    copy = pltpu.make_async_copy(second, turned_in, last_sem.at[0])
    copy.start()
    for layer in range(LAYERS - 2, LAYERS):
        pltpu.make_async_copy(
            first.at[layer % 2], turned_out.at[layer], out_sems.at[layer % 2]
        ).wait()
    copy.wait()


def backward_layer(layer, refs, first, second, extra):
    (stash_ref, stash_out, cotangent, rounded, stash, wide, small, in_sems, out_sems) = refs
    for part in range(PARTS):
        lanes = slice(part * SLICE, (part + 1) * SLICE)
        value = cotangent[:, lanes].astype(bf16)
        rounded[:, lanes] = value
        wide[layer, part, :, :SLICE] = value
    pltpu.make_async_copy(stash_ref.at[layer], stash.at[layer], in_sems.at[layer]).wait()
    upper = jnp.dot(rounded[...], first(), preferred_element_type=f32)
    extra()
    project = small[layer, 0]
    inverse = small[layer, 1]
    sigma = jax.nn.sigmoid(project)
    slope = upper * sigma * (1.0 + project * (1.0 - sigma))
    factor = (slope * inverse).astype(bf16)
    for part in range(PARTS):
        wide[layer, part, :, SLICE:] = factor
    inner = jnp.sum(slope * project, axis=-1, keepdims=True) * (1.0 / D)
    inner = inner * inverse[:, :1] * inverse[:, :1]
    for part in range(PARTS):
        for at in range(0, SLICE, 512):
            lanes = slice(part * SLICE + at, part * SLICE + at + 512)
            grad = jnp.dot(factor, second(lanes), preferred_element_type=f32)
            hidden = stash[layer, part, :, at : at + 512].astype(f32)
            cotangent[:, lanes] += grad - hidden * inner
    pltpu.make_async_copy(wide.at[layer], stash_out.at[layer], out_sems.at[layer]).start()


def backward_kernel(tick, place, c_ref, turned_out, turned_in, *refs):
    pieces_in, stash_ref, small_in = refs[:8], refs[8], refs[9]
    refs = refs[10:] if tick == LAST else refs[11:]
    sent_ref, stash_out = refs[:2]
    (cotangent, rounded, stash, wide, small, in_sems, out_sems, held_in, held_sems) = refs[2:11]
    first, first_sems, last_sem = refs[11:14]
    seconds = refs[14:16]
    common = (
        stash_ref, stash_out, cotangent, rounded, stash, wide, small, in_sems, out_sems,
    )

    def fetch_turned(layer):
        slot = lax.rem(layer, SLOTS)
        return pltpu.make_async_copy(turned_out.at[layer], first.at[slot], first_sems.at[slot])

    def turn(layer, second):
        slot = lax.rem(layer, SLOTS)
        for at in range(0, D, HD):
            second[:, at : at + HD] = held_in[slot, at : at + HD, :].T

    def one_layer(layer, now, later):
        @pl.when((layer >= SLOTS - 1) & (layer < LAYERS - 1))
        def _():
            fetch_turned(layer - SLOTS + 1).start()

        @pl.when(layer >= SLOTS)
        def _():
            fetch(place, pieces_in, held_in, held_sems, layer - SLOTS)

        @pl.when(layer > 0)
        def _():
            await_fetch(pieces_in, held_in, held_sems, layer - 1)

        fetch_turned(layer).wait()
        backward_layer(
            layer,
            common,
            lambda: first[lax.rem(layer, SLOTS)],
            lambda lanes: now[:, lanes],
            lambda: turn(jnp.maximum(layer - 1, 0), later),
        )

    @pl.when(place[0] == tick)
    def _():
        start = pltpu.make_async_copy(small_in, small, in_sems.at[LAYERS])
        start.start()
        fetch_turned(jnp.int32(LAYERS - 1)).start()
        last = pltpu.make_async_copy(turned_in, seconds[0], last_sem.at[0])
        last.start()

        def begin(back, carry):
            layer = LAYERS - 1 - back
            pltpu.make_async_copy(stash_ref.at[layer], stash.at[layer], in_sems.at[layer]).start()

            @pl.when((back > 0) & (back < SLOTS))
            def _():
                fetch(place, pieces_in, held_in, held_sems, layer)
                fetch_turned(layer).start()

            return carry

        lax.fori_loop(0, LAYERS, begin, 0)
        cotangent[...] = c_ref[...].astype(f32)
        start.wait()
        last.wait()

        def two_layers(back, carry):
            layer = LAYERS - 1 - 2 * back
            one_layer(layer, seconds[0], seconds[1])
            one_layer(layer - 1, seconds[1], seconds[0])
            return carry

        lax.fori_loop(0, LAYERS // 2, two_layers, 0)
        sent_ref[...] = cotangent[...].astype(bf16)

        def end(layer, carry):
            pltpu.make_async_copy(wide.at[layer], stash_out.at[layer], out_sems.at[layer]).wait()
            return carry

        lax.fori_loop(0, LAYERS, end, 0)


STASH = jax.ShapeDtypeStruct((LAYERS, PARTS, ROWS, WIDE), bf16)
SMALL = jax.ShapeDtypeStruct((LAYERS, 2, ROWS, HD), f32)
SENT = jax.ShapeDtypeStruct((ROWS, D), bf16)
ANY = pl.BlockSpec(memory_space=pl.ANY)
VMEM = pl.BlockSpec(memory_space=pltpu.VMEM)
SMEM = pl.BlockSpec(memory_space=pltpu.SMEM)
STATE = [pltpu.VMEM((ROWS, D), f32), pltpu.VMEM((ROWS, D), bf16)]
PARAMS = pltpu.CompilerParams(vmem_limit_bytes=30 * 2**20)


COST = pl.CostEstimate(flops=4 * LAYERS * ROWS * D * HD, bytes_accessed=36 * 2**20, transcendentals=0)


def in_hbm(value):
    return pltpu.with_memory_space_constraint(value, pltpu.HBM)


def in_vmem(value):
    return pltpu.with_memory_space_constraint(value, pltpu.VMEM)


STREAM_IN = [pltpu.VMEM((SLOTS, D, HD), bf16), pltpu.SemaphoreType.DMA((SLOTS,))]
FORWARD = STATE + [
    pltpu.VMEM(STASH.shape, bf16),
    pltpu.VMEM(SMALL.shape, f32),
    pltpu.SemaphoreType.DMA((LAYERS + 1,)),
]


def run_load(place, pieces_in, pieces_out, after):
    return pl.pallas_call(
        load_kernel,
        in_specs=[SMEM] + [ANY] * 17,
        out_specs=[VMEM, ANY, ANY],
        out_shape=[
            pltpu.VMEM((LAYERS, HD, D), bf16),
            jax.ShapeDtypeStruct((LAYERS, D, HD), bf16),
            jax.ShapeDtypeStruct((HD, D), bf16),
        ],
        scratch_shapes=[
            pltpu.VMEM((2, D, HD), bf16),
            pltpu.VMEM((HD, D), bf16),
            pltpu.VMEM((1, D, HD), bf16),
            pltpu.SemaphoreType.DMA((LAYERS,)),
            pltpu.SemaphoreType.DMA((1,)),
            pltpu.SemaphoreType.DMA((2,)),
            pltpu.SemaphoreType.DMA((1,)),
        ],
        compiler_params=pltpu.CompilerParams(vmem_limit_bytes=10 * 2**20),
        cost_estimate=COST,
        name="team_load",
    )(place, *map(in_hbm, pieces_out), *map(in_hbm, pieces_in), after)


def run_early(tick, place, x, pieces_in, pieces_out, stash, small):
    older = [] if stash is None else [stash, small]
    return pl.pallas_call(
        functools.partial(early_kernel, tick),
        in_specs=[SMEM, VMEM] + [ANY] * (16 + len(older)),
        out_specs=[VMEM, ANY, ANY],
        out_shape=[SENT, STASH, SMALL],
        input_output_aliases={18: 1, 19: 2} if older else {},
        scratch_shapes=FORWARD
        + [
            pltpu.VMEM((SLOTS, D, HD), bf16),
            pltpu.VMEM((SLOTS, HD, D), bf16),
            pltpu.SemaphoreType.DMA((SLOTS,)),
            pltpu.SemaphoreType.DMA((SLOTS,)),
        ],
        compiler_params=PARAMS,
        cost_estimate=COST,
        name="team_early",
    )(place, x, *map(in_hbm, pieces_in), *map(in_hbm, pieces_out), *map(in_hbm, older))


def run_forward(tick, place, x, held_out, pieces_in, stash, small):
    return pl.pallas_call(
        functools.partial(forward_kernel, tick),
        in_specs=[SMEM, VMEM, VMEM] + [ANY] * 10,
        out_specs=[VMEM, ANY, ANY],
        out_shape=[SENT, STASH, SMALL],
        input_output_aliases={11: 1, 12: 2},
        scratch_shapes=FORWARD + STREAM_IN,
        compiler_params=PARAMS,
        cost_estimate=COST,
        name="team_forward",
    )(place, x, in_vmem(held_out), *map(in_hbm, pieces_in), in_hbm(stash), in_hbm(small))


def run_backward(tick, place, c, turned_out, turned_in, pieces_in, stash, small, cots):
    older = [] if cots is None else [cots]
    return pl.pallas_call(
        functools.partial(backward_kernel, tick),
        in_specs=[SMEM, VMEM] + [ANY] * (12 + len(older)),
        out_specs=[VMEM, ANY],
        out_shape=[SENT, STASH],
        input_output_aliases={14: 1} if older else {},
        scratch_shapes=STATE
        + [
            pltpu.VMEM(STASH.shape, bf16),
            pltpu.VMEM(STASH.shape, bf16),
            pltpu.VMEM(SMALL.shape, f32),
            pltpu.SemaphoreType.DMA((LAYERS + 1,)),
            pltpu.SemaphoreType.DMA((LAYERS,)),
        ]
        + STREAM_IN
        + STREAM_IN
        + [pltpu.SemaphoreType.DMA((1,)), pltpu.VMEM((HD, D), bf16), pltpu.VMEM((HD, D), bf16)],
        compiler_params=PARAMS,
        cost_estimate=COST,
        name="team_backward",
    )(place, c, *map(in_hbm, [turned_out, turned_in, *pieces_in, stash, small, *older]))


def along_z(value, steps):
    index = [(z % 4) * 2 + z // 4 for z in range(8)]
    pairs = [(index[z], index[(z + steps) % 8]) for z in range(8)]
    return lax.ppermute(value, ("zl", "zh"), pairs)


def swap_cores(value):
    return lax.ppermute(value, "core", [(0, 1), (1, 0)])


def along_y(value, source, target):
    return lax.ppermute(value, "y", [(source, target)])


PLANE = ("zl", "core", "x", "zh")


def exchange(stash):
    flat = stash.reshape(LAYERS * PARTS, ROWS, WIDE)
    flat = lax.all_to_all(flat, PLANE, 0, 0, tiled=True)
    return flat.reshape(LAYERS * PARTS * ROWS, WIDE)


def local(inputs, gain, w_in, w_out):
    axes = ("y", "zl", "core")
    place = jnp.stack([lax.axis_index(axis) for axis in axes]).astype(jnp.int32)
    own_in, own_out = w_in[0], w_out[0]
    own_in = (own_in.astype(f32) * gain[0][:, None]).astype(bf16)
    before_in, after_out = along_z(own_in, 1), along_z(own_out, -1)
    before_out, after_in = along_z(own_out, 1), along_z(own_in, -1)
    near_in, near_out, inputs = lax.optimization_barrier((before_in, after_out, inputs))
    far_in, far_out = along_z(near_in, 1), along_z(near_out, -1)
    x = jnp.broadcast_to(inputs, (8,) + inputs.shape).reshape(64, ROWS, HD)
    x = lax.all_to_all(x, ("y", "zl", "core"), 0, 0, tiled=True)
    x = x.transpose(1, 0, 2).reshape(ROWS, D)
    (before_out, after_in, x) = lax.optimization_barrier((before_out, after_in, x))
    pieces_in = [own_in, swap_cores(own_in), after_in, swap_cores(after_in)]
    pieces_in += [far_in, swap_cores(far_in), near_in, swap_cores(near_in)]
    pieces_out = [own_out, swap_cores(own_out), near_out, swap_cores(near_out)]
    pieces_out += [far_out, swap_cores(far_out), before_out, swap_cores(before_out)]

    stash = small = cots = None
    for tick in range(8):
        if tick > 0:
            last, x = x, along_y(x, tick - 1, tick)
        if tick < EARLY:
            x, stash, small = run_early(tick, place, x, pieces_in, pieces_out, stash, small)
            continue
        if tick == EARLY:
            held_out, turned_out, turned_in = run_load(place, pieces_in, pieces_out, last)
        x, stash, small = run_forward(tick, place, x, held_out, pieces_in, stash, small)
    for tick in range(LAST, -1, -1):
        if tick < LAST:
            x = along_y(x, tick + 1, tick)
        x, cots = run_backward(
            tick, place, x, turned_out, turned_in, pieces_in, stash, small, cots
        )
        if tick == FIRST_EXCHANGE:
            x, stash_sent = lax.optimization_barrier((x, stash))
            first = exchange(stash_sent)

    second = exchange(cots)
    part = lax.axis_index("x") * 2 + lax.axis_index("zh")
    own_gain = lax.dynamic_slice(gain, (0, part * SLICE), (1, SLICE)).reshape(SLICE, 1)
    scale = 1.0 / math.sqrt(LAYERS * PARTS * ROWS)
    rows = (((0,), (0,)), ((), ()))
    sum_in = lax.dot_general(
        first[:, :SLICE], second[:, SLICE:], rows, preferred_element_type=f32
    )
    sum_out = lax.dot_general(
        first[:, SLICE:], second[:, :SLICE], rows, preferred_element_type=f32
    )
    grad_in = (sum_in * own_gain * scale).astype(bf16)[None]
    grad_out = (sum_out * scale).astype(bf16)[None]
    return (grad_in, grad_out)


def solution(mesh):
    axes = ("y", "zl", "core", "x", "zh")
    split = Mesh(mesh.devices.reshape(8, 4, 2, 4, 2), axes)
    section, replica = ("y", "zl", "core"), ("x", "zh")
    return jax.shard_map(
        local,
        mesh=split,
        in_specs=(
            P(None, replica, section),
            P(section, None),
            P(section, None, None),
            P(section, None, None),
        ),
        out_specs=(P(section, replica, None), P(section, None, replica)),
        check_vma=False,
    )
```

time: 697 us -> 562 us (0.81)
  waiting for transfers between devices: 504 us -> 392 us
  blocking collectives: 34.8 us -> 0 us
  starting transfers between devices: 93.4 us -> 101 us
    ppermute x14, waiting for transfers between devices: 342 us -> 236 us  [along_y(): return lax.ppermute(value, 'y', [(source, target)])]
    all_gather x2 -> x0, blocking collectives: 34.8 us -> none  [the longest x1 20 us: local(): x = lax.all_gather(x, 'y', axis=1, tiled=True)]
    pallas_call x0 -> x3, Pallas kernels: none -> 22.7 us  [the longest x2 13.6 us: run_early(): pl.pallas_call(functools.partial(early_kernel, tick), in_specs=[SMEM, VME...]
    pallas_call x8 -> x6, Pallas kernels: 17 us -> 4.03 us  [run_forward(): pl.pallas_call(functools.partial(forward_kernel, tick), in_specs=[SMEM, V...]
    ppermute x6, waiting for transfers between devices: 107 us -> 96.4 us  [along_z(): return lax.ppermute(value, ('zl', 'zh'), pairs)]
    all_to_all x1, starting transfers between devices: 3.75 us -> 13.8 us  [local(): x = lax.all_to_all(x, ('y', 'zl', 'core'), 0, 0, tiled=True)]
    pallas_call x8, Pallas kernels: 30.4 us -> 21 us  [run_backward(): pl.pallas_call(functools.partial(backward_kernel, tick), in_specs=[SMEM,...]
  transfers between devices with their start and end apart: 31 -> 31, of which waited for: 8 -> 8; matrix products, arithmetic and copies ran while one was open for 0% -> 0% of each run, Pallas kernels for 4% -> 5%
where the time goes in v2:
time: 562 us; the launch traced here: 561 us
  waiting for transfers between devices  392 us (70%)
  starting transfers between devices  101 us (18%)
  Pallas kernels  47.8 us (9%)
  local copies, waits for them, and re-layouts  12.1 us (2%)
    ppermute x14, waiting for transfers between devices, along_y(): return lax.ppermute(value, 'y', [(source, target)])  236 us
    ppermute x6, waiting for transfers between devices, along_z(): return lax.ppermute(value, ('zl', 'zh'), pairs)  96.4 us
    all_to_all x2, waiting for transfers between devices, exchange(): flat = lax.all_to_all(flat, PLANE, 0, 0, tiled=True)  55.6 us
    ppermute x6, starting transfers between devices, along_z(): return lax.ppermute(value, ('zl', 'zh'), pairs)  29.3 us
    all_to_all x2, starting transfers between devices, exchange(): flat = lax.all_to_all(flat, PLANE, 0, 0, tiled=True)  27 us
    pallas_call x8, Pallas kernels, run_backward(): pl.pallas_call(functools.partial(backward_kernel, tick), in_specs=[SMEM,...  21 us
    ppermute x8, starting transfers between devices, swap_cores(): return lax.ppermute(value, 'core', [(0, 1), (1, 0)])  19.9 us
    all_to_all x1, starting transfers between devices, local(): x = lax.all_to_all(x, ('y', 'zl', 'core'), 0, 0, tiled=True)  13.8 us
  transfers between devices with their start and end apart: 31, of which 8 were waited for; matrix products, arithmetic and copies ran while one was open for 0% of the time, Pallas kernels for 5%

profile of v2, /device:TPU:1, one launch (start us, length us, event | category | flops | bytes accessed | tf_op | source)
XLA Modules:
  0.0 561.2 jit_solution(6404110281581036243)
XLA Ops:
  0.6 2.5 fusion.refs_0_.refs_8_
  3.1 4.8 collective-permute-start.2
  8.0 8.6 %collective-permute-start.3 = (bf16[128,8192]{1,0:T(8,128)(2,1)}, bf16[128,8192]{1,0:T(8,128)(2,1)}, u32[]{:S(2)}, u32[]{:S(2)}) collective-permute-start(bf16[128,8192]{1,0:T(8,128)(2,1)} %bitcast.3.refs_8_.refs_0_), channel_id=1, source_target_pairs={{0,49},{16,0},{32,16},{48,32},{1,48},{17,1},{33,17},{49,33},{2,51}... | collective-permute-start | bytes 6291464 | tf_op jit(solution)/shard_map/ppermute | solution.py:389
  16.6 3.4 collective-permute-start.1
  20.0 1.9 collective-permute-start
  21.9 38.1 %collective-permute-done.2.refs_6_.refs_14_ = bf16[8192,128]{1,0:T(8,128)(2,1)S(1)} collective-permute-done((bf16[8192,128]{1,0:T(8,128)(2,1)S(1)}, bf16[8192,128]{1,0:T(8,128)(2,1)S(1)}, u32[]{:S(2)}, u32[]{:S(2)}) %collective-permute-start.2) | collective-permute-done | bytes 2097184 | tf_op jit(solution)/shard_map/ppermute | solution.py:389
  60.0 1.4 copy-done.5
  61.4 0.7 broadcast_in_dim.9
  62.2 13.8 %all-to-all-start = ((bf16[64,16,128]{2,1,0:T(8,128)(2,1)}), bf16[64,16,128]{2,1,0:T(8,128)(2,1)S(1)}, u32[]{:S(2)}, u32[]{:S(2)}) async-start(bf16[64,16,128]{2,1,0:T(8,128)(2,1)} %bitcast.6), calls=%async_computation | async-start | bytes 524288 | tf_op jit(solution)/shard_map/all_to_all | solution.py:419
  76.0 2.4 collective-permute-start.4
  78.3 2.0 collective-permute-start.9
  80.3 3.3 collective-permute-start.6
  83.6 22.4 %collective-permute-done.1.refs_2_.refs_10_ = bf16[8192,128]{1,0:T(8,128)(2,1)} collective-permute-done((bf16[8192,128]{1,0:T(8,128)(2,1)S(1)}, bf16[8192,128]{1,0:T(8,128)(2,1)}, u32[]{:S(2)}, u32[]{:S(2)}) %collective-permute-start.1) | collective-permute-done | bytes 2097184 | tf_op jit(solution)/shard_map/ppermute | solution.py:389
  106.0 3.5 collective-permute-start.8
  109.5 7.3 %collective-permute-start.11 = (bf16[128,8192]{1,0:T(8,128)(2,1)}, bf16[128,8192]{1,0:T(8,128)(2,1)}, u32[]{:S(2)}, u32[]{:S(2)}) collective-permute-start(bf16[128,8192]{1,0:T(8,128)(2,1)} %collective-permute-done.3.refs_10_.refs_2_), channel_id=1, source_target_pairs={{0,49},{16,0},{32,16},{48,32},{1,48},{17,1},{33,17},{49,33},{2,51}... | collective-permute-start | bytes 6291464 | tf_op jit(solution)/shard_map/ppermute | solution.py:389
  116.8 2.2 collective-permute-start.10
  119.1 2.1 collective-permute-start.5
  121.2 28.8 %collective-permute-done.6.refs_4_.refs_12_ = bf16[8192,128]{1,0:T(8,128)(2,1)} collective-permute-done((bf16[8192,128]{1,0:T(8,128)(2,1)}, bf16[8192,128]{1,0:T(8,128)(2,1)}, u32[]{:S(2)}, u32[]{:S(2)}) %collective-permute-start.6) | collective-permute-done | bytes 2097184 | tf_op jit(solution)/shard_map/ppermute | solution.py:389
  150.0 3.1 collective-permute-start.13
  153.1 1.9 collective-permute-start.7
  155.1 7.1 %collective-permute-done.11.refs_12_.refs_4_ = bf16[128,8192]{1,0:T(8,128)(2,1)} collective-permute-done((bf16[128,8192]{1,0:T(8,128)(2,1)}, bf16[128,8192]{1,0:T(8,128)(2,1)}, u32[]{:S(2)}, u32[]{:S(2)}) %collective-permute-start.11) | collective-permute-done | bytes 2097184 | tf_op jit(solution)/shard_map/ppermute | solution.py:389
  162.1 2.7 collective-permute-start.12
  164.9 4.0 collective-permute-done.12.refs_13_.refs_5_
  168.9 12.9 %team_early.2 = (bf16[16,8192]{1,0:T(8,128)(2,1)S(1)}, bf16[8,8,16,1152]{3,2,1,0:T(8,128)(2,1)}, f32[8,2,16,128]{3,2,1,0:T(8,128)S(1)}) custom-call(s32[3]{0:T(128)S(1)} %pad_add_fusion.place, bf16[16,8192]{1,0:T(8,128)(2,1)S(1)} %copy_bitcast_fusion.x_ref, bf16[8192,128]{1,0:T(8,128)(2,1)} %copy-done.4, ...), custom_call_target="tpu_custom_call" | custom-call | flops 536870912 | bytes 37748736 | tf_op jit(solution)/shard_map/team_early/pallas_call | solution.py:328
  182.5 1.3 collective-permute-start.14
  183.8 5.6 collective-permute-done.14.x_ref
  189.4 0.7 team_early.3
  190.1 0.7 collective-permute-start.15
  190.8 9.1 %team_load.1 = (bf16[8,128,8192]{2,1,0:T(8,128)(2,1)S(1)}, bf16[8,8192,128]{2,1,0:T(8,128)(2,1)S(1)}, bf16[128,8192]{1,0:T(8,128)(2,1)S(1)}) custom-call(s32[3]{0:T(128)S(1)} %pad_add_fusion.place, bf16[128,8192]{1,0:T(8,128)(2,1)} %bitcast.3.refs_8_.refs_0_, bf16[128,8192]{1,0:T(8,128)(2,1)} %collective-permute-done.9.refs_9_.refs_1_, ...), custom_call_target="tpu_custom_call" | custom-call | flops 536870912 | bytes 37748736 | tf_op jit(solution)/shard_map/team_load/pallas_call | solution.py:302
  200.0 5.8 %copy-done = bf16[8,8192,128]{2,1,0:T(8,128)(2,1)} copy-done((bf16[8,8192,128]{2,1,0:T(8,128)(2,1)}, bf16[8,8192,128]{2,1,0:T(8,128)(2,1)S(1)}, u32[]{:S(2)}) %copy-start) | copy-done | bytes 16777240
  205.7 1.3 copy-done.2
  207.7 0.7 collective-permute-start.16
  208.4 0.7 team_forward.7
  209.1 0.7 collective-permute-start.17
  209.8 0.7 team_forward.8
  210.5 0.7 collective-permute-start.18
  211.2 0.7 team_forward.9
  211.8 0.7 collective-permute-start.19
  212.5 0.7 team_forward.10
  213.2 0.7 collective-permute-start.20
  213.9 0.7 team_forward.11
  214.6 1.0 team_backward.8
  215.6 1.5 copy-done.1
  217.1 11.2 %all-to-all-start.1 = ((bf16[64,16,1152]{2,1,0:T(8,128)(2,1)}), bf16[64,16,1152]{2,1,0:T(8,128)(2,1)S(1)}, u32[]{:S(2)}, u32[]{:S(2)}) async-start(bf16[64,16,1152]{2,1,0:T(8,128)(2,1)} %bitcast.8), calls=%async_computation.1 | async-start | bytes 4718592 | tf_op jit(solution)/shard_map/all_to_all | solution.py:405
  228.2 0.7 collective-permute-start.21
  228.9 0.8 team_backward.9
  229.7 0.7 collective-permute-start.22
  230.4 0.8 team_backward.10
  231.2 0.7 collective-permute-start.23
  231.9 0.8 team_backward.11
  232.7 0.7 collective-permute-start.24
  233.4 0.8 team_backward.12
  234.2 0.7 collective-permute-start.25
  234.9 1.0 team_backward.13
  235.9 0.7 collective-permute-start.26
  236.6 0.8 team_backward.14
  237.4 1.3 collective-permute-start.27
  238.7 230.1 %collective-permute-done.27.c_ref = bf16[16,8192]{1,0:T(8,128)(2,1)S(1)} collective-permute-done((bf16[16,8192]{1,0:T(8,128)(2,1)S(1)}, bf16[16,8192]{1,0:T(8,128)(2,1)S(1)}, u32[]{:S(2)}, u32[]{:S(2)}) %collective-permute-start.27) | collective-permute-done | bytes 262176 | tf_op jit(solution)/shard_map/ppermute | solution.py:397
  468.8 15.1 %team_backward.15 = (bf16[16,8192]{1,0:T(8,128)(2,1)}, bf16[8,8,16,1152]{3,2,1,0:T(8,128)(2,1)}) custom-call(s32[3]{0:T(128)S(1)} %pad_add_fusion.place, bf16[16,8192]{1,0:T(8,128)(2,1)S(1)} %collective-permute-done.27.c_ref, bf16[8,8192,128]{2,1,0:T(8,128)(2,1)} %copy-done, bf16[128,8192]{1,0:T(8,128)(2,1)} %copy-done.2, ...), custom_call_target="tpu_custom_call", output_to_operand_aliasing={{1}: (14, {})} | custom-call | flops 536870912 | bytes 37748736 | tf_op jit(solution)/shard_map/team_backward/pallas_call | solution.py:363
  483.9 15.8 %all-to-all-start.2 = ((bf16[64,16,1152]{2,1,0:T(8,128)(2,1)}), bf16[64,16,1152]{2,1,0:T(8,128)(2,1)}, u32[]{:S(2)}, u32[]{:S(2)}) async-start(bf16[64,16,1152]{2,1,0:T(8,128)(2,1)} %bitcast.24), calls=%async_computation.2 | async-start | bytes 4718592 | tf_op jit(solution)/shard_map/all_to_all | solution.py:405
  499.7 0.7 constant_dynamic-slice_fusion
  500.4 55.6 %all-to-all-done.2 = bf16[64,16,1152]{2,1,0:T(8,128)(2,1)} async-done(((bf16[64,16,1152]{2,1,0:T(8,128)(2,1)}), bf16[64,16,1152]{2,1,0:T(8,128)(2,1)}, u32[]{:S(2)}, u32[]{:S(2)}) %all-to-all-start.2) | async-done | bytes 2359328 | tf_op jit(solution)/shard_map/all_to_all | solution.py:405
  556.0 2.8 fusion.20
  558.7 2.4 fusion.23
  (36 shorter events, 1.5 us)
Async XLA Ops:
  0.6 60.8 %copy-start.6 = (bf16[8,16,128]{2,1,0:T(8,128)(2,1)S(1)}, bf16[8,16,128]{2,1,0:T(8,128)(2,1)}, u32[]{:S(2)}) copy-start(bf16[8,16,128]{2,1,0:T(8,128)(2,1)} %param.4) | copy-start | bytes 98308
  3.1 165.8 %copy-start.4 = (bf16[8192,128]{1,0:T(8,128)(2,1)}, bf16[8192,128]{1,0:T(8,128)(2,1)S(1)}, u32[]{:S(2)}) copy-start(bf16[8192,128]{1,0:T(8,128)(2,1)S(1)} %fusion.refs_0_.refs_8_) | copy-start | bytes 6291460
  3.1 56.8 %collective-permute-start.2 = (bf16[8192,128]{1,0:T(8,128)(2,1)S(1)}, bf16[8192,128]{1,0:T(8,128)(2,1)S(1)}, u32[]{:S(2)}, u32[]{:S(2)}) collective-permute-start(bf16[8192,128]{1,0:T(8,128)(2,1)S(1)} %fusion.refs_0_.refs_8_), channel_id=1, source_target_pairs={{0,16},{16,32},{32,48},{48,1},{1,17},{17,33},{33,49},{49,0},{2,18}... | collective-permute-start | bytes 6291464 | tf_op jit(solution)/shard_map/ppermute | solution.py:389
  8.0 53.4 %collective-permute-start.3 = (bf16[128,8192]{1,0:T(8,128)(2,1)}, bf16[128,8192]{1,0:T(8,128)(2,1)}, u32[]{:S(2)}, u32[]{:S(2)}) collective-permute-start(bf16[128,8192]{1,0:T(8,128)(2,1)} %bitcast.3.refs_8_.refs_0_), channel_id=1, source_target_pairs={{0,49},{16,0},{32,16},{48,32},{1,48},{17,1},{33,17},{49,33},{2,51}... | collective-permute-start | bytes 6291464 | tf_op jit(solution)/shard_map/ppermute | solution.py:389
  16.6 89.4 %collective-permute-start.1 = (bf16[8192,128]{1,0:T(8,128)(2,1)S(1)}, bf16[8192,128]{1,0:T(8,128)(2,1)}, u32[]{:S(2)}, u32[]{:S(2)}) collective-permute-start(bf16[8192,128]{1,0:T(8,128)(2,1)S(1)} %fusion.refs_0_.refs_8_), channel_id=1, source_target_pairs={{0,49},{16,0},{32,16},{48,32},{1,48},{17,1},{33,17},{49,33},{2,51}... | collective-permute-start | bytes 6291464 | tf_op jit(solution)/shard_map/ppermute | solution.py:389
  20.0 89.6 %collective-permute-start = (bf16[128,8192]{1,0:T(8,128)(2,1)}, bf16[128,8192]{1,0:T(8,128)(2,1)}, u32[]{:S(2)}, u32[]{:S(2)}) collective-permute-start(bf16[128,8192]{1,0:T(8,128)(2,1)} %bitcast.3.refs_8_.refs_0_), channel_id=1, source_target_pairs={{0,16},{16,32},{32,48},{48,1},{1,17},{17,33},{33,49},{49,0},{2,18}... | collective-permute-start | bytes 6291464 | tf_op jit(solution)/shard_map/ppermute | solution.py:389
  60.0 1.4 copy-start.5
  62.2 54.6 %all-to-all-start = ((bf16[64,16,128]{2,1,0:T(8,128)(2,1)}), bf16[64,16,128]{2,1,0:T(8,128)(2,1)S(1)}, u32[]{:S(2)}, u32[]{:S(2)}) async-start(bf16[64,16,128]{2,1,0:T(8,128)(2,1)} %bitcast.6), calls=%async_computation | async-start | bytes 524288 | tf_op jit(solution)/shard_map/all_to_all | solution.py:419
  76.0 40.9 %collective-permute-start.4 = (bf16[8192,128]{1,0:T(8,128)(2,1)S(1)}, bf16[8192,128]{1,0:T(8,128)(2,1)}, u32[]{:S(2)}, u32[]{:S(2)}) collective-permute-start(bf16[8192,128]{1,0:T(8,128)(2,1)S(1)} %fusion.refs_0_.refs_8_), channel_id=1, source_target_pairs={{0,8},{8,0},{1,9},{9,1},{2,10},{10,2},{3,11},{11,3},{4,12},{12,4},... | collective-permute-start | bytes 6291464 | tf_op jit(solution)/shard_map/ppermute | solution.py:393
  78.3 40.7 %collective-permute-start.9 = (bf16[128,8192]{1,0:T(8,128)(2,1)}, bf16[128,8192]{1,0:T(8,128)(2,1)}, u32[]{:S(2)}, u32[]{:S(2)}) collective-permute-start(bf16[128,8192]{1,0:T(8,128)(2,1)} %bitcast.3.refs_8_.refs_0_), channel_id=1, source_target_pairs={{0,8},{8,0},{1,9},{9,1},{2,10},{10,2},{3,11},{11,3},{4,12},{12,4},... | collective-permute-start | bytes 6291464 | tf_op jit(solution)/shard_map/ppermute | solution.py:393
  80.3 69.7 %collective-permute-start.6 = (bf16[8192,128]{1,0:T(8,128)(2,1)}, bf16[8192,128]{1,0:T(8,128)(2,1)}, u32[]{:S(2)}, u32[]{:S(2)}) collective-permute-start(bf16[8192,128]{1,0:T(8,128)(2,1)} %copy-done.5), channel_id=1, source_target_pairs={{0,16},{16,32},{32,48},{48,1},{1,17},{17,33},{33,49},{49,0},{2,18}... | collective-permute-start | bytes 6291464 | tf_op jit(solution)/shard_map/ppermute | solution.py:389
  106.0 47.1 %collective-permute-start.8 = (bf16[8192,128]{1,0:T(8,128)(2,1)}, bf16[8192,128]{1,0:T(8,128)(2,1)}, u32[]{:S(2)}, u32[]{:S(2)}) collective-permute-start(bf16[8192,128]{1,0:T(8,128)(2,1)} %copy-done.5), channel_id=1, source_target_pairs={{0,8},{8,0},{1,9},{9,1},{2,10},{10,2},{3,11},{11,3},{4,12},{12,4},... | collective-permute-start | bytes 6291464 | tf_op jit(solution)/shard_map/ppermute | solution.py:393
  109.5 52.6 %collective-permute-start.11 = (bf16[128,8192]{1,0:T(8,128)(2,1)}, bf16[128,8192]{1,0:T(8,128)(2,1)}, u32[]{:S(2)}, u32[]{:S(2)}) collective-permute-start(bf16[128,8192]{1,0:T(8,128)(2,1)} %collective-permute-done.3.refs_10_.refs_2_), channel_id=1, source_target_pairs={{0,49},{16,0},{32,16},{48,32},{1,48},{17,1},{33,17},{49,33},{2,51}... | collective-permute-start | bytes 6291464 | tf_op jit(solution)/shard_map/ppermute | solution.py:389
  116.8 48.1 %collective-permute-start.10 = (bf16[128,8192]{1,0:T(8,128)(2,1)}, bf16[128,8192]{1,0:T(8,128)(2,1)}, u32[]{:S(2)}, u32[]{:S(2)}) collective-permute-start(bf16[128,8192]{1,0:T(8,128)(2,1)} %collective-permute-done.3.refs_10_.refs_2_), channel_id=1, source_target_pairs={{0,8},{8,0},{1,9},{9,1},{2,10},{10,2},{3,11},{11,3},{4,12},{12,4},... | collective-permute-start | bytes 6291464 | tf_op jit(solution)/shard_map/ppermute | solution.py:393
  119.1 45.9 %collective-permute-start.5 = (bf16[8192,128]{1,0:T(8,128)(2,1)}, bf16[8192,128]{1,0:T(8,128)(2,1)}, u32[]{:S(2)}, u32[]{:S(2)}) collective-permute-start(bf16[8192,128]{1,0:T(8,128)(2,1)} %collective-permute-done.1.refs_2_.refs_10_), channel_id=1, source_target_pairs={{0,8},{8,0},{1,9},{9,1},{2,10},{10,2},{3,11},{11,3},{4,12},{12,4},... | collective-permute-start | bytes 6291464 | tf_op jit(solution)/shard_map/ppermute | solution.py:393
  150.0 14.9 %collective-permute-start.13 = (bf16[128,8192]{1,0:T(8,128)(2,1)}, bf16[128,8192]{1,0:T(8,128)(2,1)}, u32[]{:S(2)}, u32[]{:S(2)}) collective-permute-start(bf16[128,8192]{1,0:T(8,128)(2,1)} %collective-permute-done.refs_14_.refs_6_), channel_id=1, source_target_pairs={{0,8},{8,0},{1,9},{9,1},{2,10},{10,2},{3,11},{11,3},{4,12},{12,4},... | collective-permute-start | bytes 6291464 | tf_op jit(solution)/shard_map/ppermute | solution.py:393
  153.1 11.8 %collective-permute-start.7 = (bf16[8192,128]{1,0:T(8,128)(2,1)}, bf16[8192,128]{1,0:T(8,128)(2,1)}, u32[]{:S(2)}, u32[]{:S(2)}) collective-permute-start(bf16[8192,128]{1,0:T(8,128)(2,1)} %collective-permute-done.6.refs_4_.refs_12_), channel_id=1, source_target_pairs={{0,8},{8,0},{1,9},{9,1},{2,10},{10,2},{3,11},{11,3},{4,12},{12,4},... | collective-permute-start | bytes 6291464 | tf_op jit(solution)/shard_map/ppermute | solution.py:393
  162.1 6.8 %collective-permute-start.12 = (bf16[128,8192]{1,0:T(8,128)(2,1)}, bf16[128,8192]{1,0:T(8,128)(2,1)}, u32[]{:S(2)}, u32[]{:S(2)}) collective-permute-start(bf16[128,8192]{1,0:T(8,128)(2,1)} %collective-permute-done.11.refs_12_.refs_4_), channel_id=1, source_target_pairs={{0,8},{8,0},{1,9},{9,1},{2,10},{10,2},{3,11},{11,3},{4,12},{12,4},... | collective-permute-start | bytes 6291464 | tf_op jit(solution)/shard_map/ppermute | solution.py:393
  181.8 0.7 copy-start.3
  182.5 6.9 %collective-permute-start.14 = (bf16[16,8192]{1,0:T(8,128)(2,1)S(1)}, bf16[16,8192]{1,0:T(8,128)(2,1)S(1)}, u32[]{:S(2)}, u32[]{:S(2)}) collective-permute-start(bf16[16,8192]{1,0:T(8,128)(2,1)S(1)} %get-tuple-element.58), channel_id=1, source_target_pairs={{0,64},{1,65},{2,66},{3,67},{4,68},{5,69},{6,70},{7,71},{8,72},{9,... | collective-permute-start | bytes 786440 | tf_op jit(solution)/shard_map/ppermute | solution.py:397
  190.1 16.9 %collective-permute-start.15 = (bf16[16,8192]{1,0:T(8,128)(2,1)S(1)}, bf16[16,8192]{1,0:T(8,128)(2,1)S(1)}, u32[]{:S(2)}, u32[]{:S(2)}) collective-permute-start(bf16[16,8192]{1,0:T(8,128)(2,1)S(1)} %get-tuple-element.61.refs_16_), channel_id=1, source_target_pairs={{64,128},{65,129},{66,130},{67,131},{68,132},{69,133},{70,134},{71... | collective-permute-start | bytes 786440 | tf_op jit(solution)/shard_map/ppermute | solution.py:397
  199.9 5.8 %copy-start = (bf16[8,8192,128]{2,1,0:T(8,128)(2,1)}, bf16[8,8192,128]{2,1,0:T(8,128)(2,1)S(1)}, u32[]{:S(2)}) copy-start(bf16[8,8192,128]{2,1,0:T(8,128)(2,1)S(1)} %get-tuple-element.81.turned_out) | copy-start | bytes 50331652
  205.7 1.3 copy-start.2
  207.7 0.7 collective-permute-start.16
  209.1 0.7 collective-permute-start.17
  210.5 0.7 collective-permute-start.18
  211.8 0.7 collective-permute-start.19
  213.2 0.7 collective-permute-start.20
  215.6 1.5 copy-start.1
  217.1 266.8 %all-to-all-start.1 = ((bf16[64,16,1152]{2,1,0:T(8,128)(2,1)}), bf16[64,16,1152]{2,1,0:T(8,128)(2,1)S(1)}, u32[]{:S(2)}, u32[]{:S(2)}) async-start(bf16[64,16,1152]{2,1,0:T(8,128)(2,1)} %bitcast.8), calls=%async_computation.1 | async-start | bytes 4718592 | tf_op jit(solution)/shard_map/all_to_all | solution.py:405
  228.2 0.7 collective-permute-start.21
  229.7 0.7 collective-permute-start.22
  231.2 0.7 collective-permute-start.23
  232.7 0.7 collective-permute-start.24
  234.2 0.7 collective-permute-start.25
  235.9 0.7 collective-permute-start.26
  237.4 231.4 %collective-permute-start.27 = (bf16[16,8192]{1,0:T(8,128)(2,1)S(1)}, bf16[16,8192]{1,0:T(8,128)(2,1)S(1)}, u32[]{:S(2)}, u32[]{:S(2)}) collective-permute-start(bf16[16,8192]{1,0:T(8,128)(2,1)S(1)} %get-tuple-element.99), channel_id=1, source_target_pairs={{64,0},{65,1},{66,2},{67,3},{68,4},{69,5},{70,6},{71,7},{72,8},{73... | collective-permute-start | bytes 786440 | tf_op jit(solution)/shard_map/ppermute | solution.py:397
  483.9 72.1 %all-to-all-start.2 = ((bf16[64,16,1152]{2,1,0:T(8,128)(2,1)}), bf16[64,16,1152]{2,1,0:T(8,128)(2,1)}, u32[]{:S(2)}, u32[]{:S(2)}) async-start(bf16[64,16,1152]{2,1,0:T(8,128)(2,1)} %bitcast.24), calls=%async_computation.2 | async-start | bytes 4718592 | tf_op jit(solution)/shard_map/all_to_all | solution.py:405

commit v3 on v2

--- a/solution.py
+++ b/solution.py
@@ -20,10 +20,9 @@
 SLICE = D // PARTS
 WIDE = SLICE + HD
 LAST = 7
-FIRST_EXCHANGE = 7
 SLOTS = 4
 AHEAD = 3
-EARLY = 2
+EARLY = 1
 
 
 def fetch(place, pieces, held, sems, layer):
@@ -57,6 +56,7 @@
         def _():
             fetches(layer + AHEAD)
 
+        weights = get_in(layer)
         squares = jnp.zeros((ROWS, 128), f32)
         for part in range(PARTS):
             lanes = slice(part * SLICE, (part + 1) * SLICE)
@@ -67,7 +67,6 @@
             for at in range(0, SLICE, 128):
                 squares = squares + square[:, at : at + 128]
         inverse = lax.rsqrt(jnp.sum(squares, axis=-1, keepdims=True) * (1.0 / D) + epsilon)
-        weights = get_in(layer)
         project = inverse * jnp.dot(narrow[...], weights[...], preferred_element_type=f32)
         active = (project * jax.nn.sigmoid(project)).astype(bf16)
         small[layer, 0] = project
@@ -166,7 +165,6 @@
         value = cotangent[:, lanes].astype(bf16)
         rounded[:, lanes] = value
         wide[layer, part, :, :SLICE] = value
-    pltpu.make_async_copy(stash_ref.at[layer], stash.at[layer], in_sems.at[layer]).wait()
     upper = jnp.dot(rounded[...], first(), preferred_element_type=f32)
     extra()
     project = small[layer, 0]
@@ -192,15 +190,10 @@
     refs = refs[10:] if tick == LAST else refs[11:]
     sent_ref, stash_out = refs[:2]
     (cotangent, rounded, stash, wide, small, in_sems, out_sems, held_in, held_sems) = refs[2:11]
-    first, first_sems, last_sem = refs[11:14]
-    seconds = refs[14:16]
+    last_sem, *seconds = refs[11:14]
     common = (
         stash_ref, stash_out, cotangent, rounded, stash, wide, small, in_sems, out_sems,
     )
-
-    def fetch_turned(layer):
-        slot = lax.rem(layer, SLOTS)
-        return pltpu.make_async_copy(turned_out.at[layer], first.at[slot], first_sems.at[slot])
 
     def turn(layer, second):
         slot = lax.rem(layer, SLOTS)
@@ -208,10 +201,6 @@
             second[:, at : at + HD] = held_in[slot, at : at + HD, :].T
 
     def one_layer(layer, now, later):
-        @pl.when((layer >= SLOTS - 1) & (layer < LAYERS - 1))
-        def _():
-            fetch_turned(layer - SLOTS + 1).start()
-
         @pl.when(layer >= SLOTS)
         def _():
             fetch(place, pieces_in, held_in, held_sems, layer - SLOTS)
@@ -220,11 +209,11 @@
         def _():
             await_fetch(pieces_in, held_in, held_sems, layer - 1)
 
-        fetch_turned(layer).wait()
+        pltpu.make_async_copy(stash_ref.at[layer], stash.at[layer], in_sems.at[layer]).wait()
         backward_layer(
             layer,
             common,
-            lambda: first[lax.rem(layer, SLOTS)],
+            lambda: turned_out[layer],
             lambda lanes: now[:, lanes],
             lambda: turn(jnp.maximum(layer - 1, 0), later),
         )
@@ -233,7 +222,6 @@
     def _():
         start = pltpu.make_async_copy(small_in, small, in_sems.at[LAYERS])
         start.start()
-        fetch_turned(jnp.int32(LAYERS - 1)).start()
         last = pltpu.make_async_copy(turned_in, seconds[0], last_sem.at[0])
         last.start()
 
@@ -244,7 +232,6 @@
             @pl.when((back > 0) & (back < SLOTS))
             def _():
                 fetch(place, pieces_in, held_in, held_sems, layer)
-                fetch_turned(layer).start()
 
             return carry
 
@@ -269,14 +256,14 @@
         lax.fori_loop(0, LAYERS, end, 0)
 
 
-STASH = jax.ShapeDtypeStruct((LAYERS, PARTS, ROWS, WIDE), bf16)
-SMALL = jax.ShapeDtypeStruct((LAYERS, 2, ROWS, HD), f32)
+STASH = pltpu.HBM((LAYERS, PARTS, ROWS, WIDE), bf16)
+SMALL = pltpu.HBM((LAYERS, 2, ROWS, HD), f32)
 SENT = jax.ShapeDtypeStruct((ROWS, D), bf16)
 ANY = pl.BlockSpec(memory_space=pl.ANY)
 VMEM = pl.BlockSpec(memory_space=pltpu.VMEM)
 SMEM = pl.BlockSpec(memory_space=pltpu.SMEM)
 STATE = [pltpu.VMEM((ROWS, D), f32), pltpu.VMEM((ROWS, D), bf16)]
-PARAMS = pltpu.CompilerParams(vmem_limit_bytes=30 * 2**20)
+PARAMS = pltpu.CompilerParams(vmem_limit_bytes=20 * 2**20)
 
 
 COST = pl.CostEstimate(flops=4 * LAYERS * ROWS * D * HD, bytes_accessed=36 * 2**20, transcendentals=0)
@@ -306,7 +293,7 @@
         out_shape=[
             pltpu.VMEM((LAYERS, HD, D), bf16),
             jax.ShapeDtypeStruct((LAYERS, D, HD), bf16),
-            jax.ShapeDtypeStruct((HD, D), bf16),
+            pltpu.HBM((HD, D), bf16),
         ],
         scratch_shapes=[
             pltpu.VMEM((2, D, HD), bf16),
@@ -352,7 +339,7 @@
         out_shape=[SENT, STASH, SMALL],
         input_output_aliases={11: 1, 12: 2},
         scratch_shapes=FORWARD + STREAM_IN,
-        compiler_params=PARAMS,
+        compiler_params=pltpu.CompilerParams(vmem_limit_bytes=14 * 2**20),
         cost_estimate=COST,
         name="team_forward",
     )(place, x, in_vmem(held_out), *map(in_hbm, pieces_in), in_hbm(stash), in_hbm(small))
@@ -362,7 +349,7 @@
     older = [] if cots is None else [cots]
     return pl.pallas_call(
         functools.partial(backward_kernel, tick),
-        in_specs=[SMEM, VMEM] + [ANY] * (12 + len(older)),
+        in_specs=[SMEM, VMEM, VMEM] + [ANY] * (11 + len(older)),
         out_specs=[VMEM, ANY],
         out_shape=[SENT, STASH],
         input_output_aliases={14: 1} if older else {},
@@ -375,12 +362,11 @@
             pltpu.SemaphoreType.DMA((LAYERS,)),
         ]
         + STREAM_IN
-        + STREAM_IN
         + [pltpu.SemaphoreType.DMA((1,)), pltpu.VMEM((HD, D), bf16), pltpu.VMEM((HD, D), bf16)],
         compiler_params=PARAMS,
         cost_estimate=COST,
         name="team_backward",
-    )(place, c, *map(in_hbm, [turned_out, turned_in, *pieces_in, stash, small, *older]))
+    )(place, c, in_vmem(turned_out), *map(in_hbm, [turned_in, *pieces_in, stash, small, *older]))
 
 
 def along_z(value, steps):
@@ -419,6 +405,7 @@
     x = lax.all_to_all(x, ("y", "zl", "core"), 0, 0, tiled=True)
     x = x.transpose(1, 0, 2).reshape(ROWS, D)
     (before_out, after_in, x) = lax.optimization_barrier((before_out, after_in, x))
+    far_in, far_out = lax.optimization_barrier((far_in, far_out))
     pieces_in = [own_in, swap_cores(own_in), after_in, swap_cores(after_in)]
     pieces_in += [far_in, swap_cores(far_in), near_in, swap_cores(near_in)]
     pieces_out = [own_out, swap_cores(own_out), near_out, swap_cores(near_out)]
@@ -434,15 +421,14 @@
         if tick == EARLY:
             held_out, turned_out, turned_in = run_load(place, pieces_in, pieces_out, last)
         x, stash, small = run_forward(tick, place, x, held_out, pieces_in, stash, small)
+    x, stash_sent = lax.optimization_barrier((x, stash))
+    first = exchange(stash_sent)
     for tick in range(LAST, -1, -1):
         if tick < LAST:
             x = along_y(x, tick + 1, tick)
         x, cots = run_backward(
             tick, place, x, turned_out, turned_in, pieces_in, stash, small, cots
         )
-        if tick == FIRST_EXCHANGE:
-            x, stash_sent = lax.optimization_barrier((x, stash))
-            first = exchange(stash_sent)
 
     second = exchange(cots)
     part = lax.axis_index("x") * 2 + lax.axis_index("zh")

time: 562 us -> 528 us (0.940)
  waiting for transfers between devices: 392 us -> 357 us
    ppermute x14, waiting for transfers between devices: 236 us -> 200 us  [along_y(): return lax.ppermute(value, 'y', [(source, target)])]
    unnamed x14 -> x10, local copies, waits for them, and re-layouts: 10.7 us -> 12.9 us
    pallas_call x2 -> x1, Pallas kernels: 13.6 us -> 12.9 us  [run_early(): pl.pallas_call(functools.partial(early_kernel, tick), in_specs=[SMEM, VME...]
where the time goes in v3:
time: 528 us; the launch traced here: 527 us
  waiting for transfers between devices  357 us (68%)
  starting transfers between devices  102 us (19%)
  Pallas kernels  44.9 us (9%)
  local copies, waits for them, and re-layouts  14.4 us (3%)
    ppermute x14, waiting for transfers between devices, along_y(): return lax.ppermute(value, 'y', [(source, target)])  200 us
    ppermute x6, waiting for transfers between devices, along_z(): return lax.ppermute(value, ('zl', 'zh'), pairs)  93.3 us
    all_to_all x2, waiting for transfers between devices, exchange(): flat = lax.all_to_all(flat, PLANE, 0, 0, tiled=True)  55.6 us
    all_to_all x2, starting transfers between devices, exchange(): flat = lax.all_to_all(flat, PLANE, 0, 0, tiled=True)  28.1 us
    ppermute x6, starting transfers between devices, along_z(): return lax.ppermute(value, ('zl', 'zh'), pairs)  25.2 us
    ppermute x8, starting transfers between devices, swap_cores(): return lax.ppermute(value, 'core', [(0, 1), (1, 0)])  24 us
    pallas_call x8, Pallas kernels, run_backward(): pl.pallas_call(functools.partial(backward_kernel, tick), in_specs=[SMEM,...  16.9 us
    all_to_all x1, starting transfers between devices, local(): x = lax.all_to_all(x, ('y', 'zl', 'core'), 0, 0, tiled=True)  13.8 us
  transfers between devices with their start and end apart: 31, of which 8 were waited for; matrix products, arithmetic and copies ran while one was open for 0% of the time, Pallas kernels for 5%

profile of v3, /device:TPU:1, one launch (start us, length us, event | category | flops | bytes accessed | tf_op | source)
XLA Modules:
  0.0 526.9 jit_solution(675017997538165807)
XLA Ops:
  0.6 2.5 fusion.refs_0_.refs_8_
  3.1 4.8 collective-permute-start.2
  8.0 8.6 %collective-permute-start.3 = (bf16[128,8192]{1,0:T(8,128)(2,1)}, bf16[128,8192]{1,0:T(8,128)(2,1)}, u32[]{:S(2)}, u32[]{:S(2)}) collective-permute-start(bf16[128,8192]{1,0:T(8,128)(2,1)} %bitcast.3.refs_8_.refs_0_), channel_id=1, source_target_pairs={{0,49},{16,0},{32,16},{48,32},{1,48},{17,1},{33,17},{49,33},{2,51}... | collective-permute-start | bytes 6291464 | tf_op jit(solution)/shard_map/ppermute | solution.py:375
  16.6 3.4 collective-permute-start.1
  20.0 1.9 collective-permute-start
  21.9 38.1 %collective-permute-done.2.refs_6_.refs_14_ = bf16[8192,128]{1,0:T(8,128)(2,1)S(1)} collective-permute-done((bf16[8192,128]{1,0:T(8,128)(2,1)S(1)}, bf16[8192,128]{1,0:T(8,128)(2,1)S(1)}, u32[]{:S(2)}, u32[]{:S(2)}) %collective-permute-start.2) | collective-permute-done | bytes 2097184 | tf_op jit(solution)/shard_map/ppermute | solution.py:375
  60.0 1.4 copy-done.3
  61.4 0.7 broadcast_in_dim.9
  62.1 13.8 %all-to-all-start = ((bf16[64,16,128]{2,1,0:T(8,128)(2,1)}), bf16[64,16,128]{2,1,0:T(8,128)(2,1)S(1)}, u32[]{:S(2)}, u32[]{:S(2)}) async-start(bf16[64,16,128]{2,1,0:T(8,128)(2,1)} %bitcast.6), calls=%async_computation | async-start | bytes 524288 | tf_op jit(solution)/shard_map/all_to_all | solution.py:405
  76.0 3.3 collective-permute-start.6
  79.3 3.2 collective-permute-start.7
  82.5 2.9 collective-permute-start.4
  85.4 20.6 %collective-permute-done.1.refs_2_.refs_10_ = bf16[8192,128]{1,0:T(8,128)(2,1)} collective-permute-done((bf16[8192,128]{1,0:T(8,128)(2,1)S(1)}, bf16[8192,128]{1,0:T(8,128)(2,1)}, u32[]{:S(2)}, u32[]{:S(2)}) %collective-permute-start.1) | collective-permute-done | bytes 2097184 | tf_op jit(solution)/shard_map/ppermute | solution.py:375
  106.0 7.4 %collective-permute-start.10 = (bf16[128,8192]{1,0:T(8,128)(2,1)}, bf16[128,8192]{1,0:T(8,128)(2,1)}, u32[]{:S(2)}, u32[]{:S(2)}) collective-permute-start(bf16[128,8192]{1,0:T(8,128)(2,1)} %bitcast.3.refs_8_.refs_0_), channel_id=1, source_target_pairs={{0,8},{8,0},{1,9},{9,1},{2,10},{10,2},{3,11},{11,3},{4,12},{12,4},... | collective-permute-start | bytes 6291464 | tf_op jit(solution)/shard_map/ppermute | solution.py:379
  113.4 1.9 collective-permute-start.9
  115.4 34.6 %collective-permute-done.6.refs_4_.refs_12_ = bf16[8192,128]{1,0:T(8,128)(2,1)} collective-permute-done((bf16[8192,128]{1,0:T(8,128)(2,1)}, bf16[8192,128]{1,0:T(8,128)(2,1)}, u32[]{:S(2)}, u32[]{:S(2)}) %collective-permute-start.6) | collective-permute-done | bytes 2097184 | tf_op jit(solution)/shard_map/ppermute | solution.py:375
  150.0 3.1 collective-permute-start.11
  153.1 1.9 collective-permute-start.5
  155.1 2.4 collective-permute-start.13
  157.5 1.9 collective-permute-start.8
  159.4 2.4 collective-permute-start.12
  161.9 1.3 collective-permute-done.13.refs_15_.refs_7_
  163.2 3.0 collective-permute-done.8.refs_5_.refs_13_
  166.2 3.0 collective-permute-done.12.refs_13_.refs_5_
  169.2 12.9 %team_early.1 = (bf16[16,8192]{1,0:T(8,128)(2,1)S(1)}, bf16[8,8,16,1152]{3,2,1,0:T(8,128)(2,1)}, f32[8,2,16,128]{3,2,1,0:T(8,128)}) custom-call(s32[3]{0:T(128)S(1)} %pad_add_fusion.place, bf16[16,8192]{1,0:T(8,128)(2,1)S(1)} %copy_bitcast_fusion.x_ref, bf16[8192,128]{1,0:T(8,128)(2,1)} %copy-done.2, ...), custom_call_target="tpu_custom_call" | custom-call | flops 536870912 | bytes 37748736 | tf_op jit(solution)/shard_map/team_early/pallas_call | solution.py:315
  182.2 1.3 collective-permute-start.14
  183.5 10.3 %team_load.1 = (bf16[8,128,8192]{2,1,0:T(8,128)(2,1)S(1)}, bf16[8,8192,128]{2,1,0:T(8,128)(2,1)S(1)}, bf16[128,8192]{1,0:T(8,128)(2,1)}) custom-call(s32[3]{0:T(128)S(1)} %pad_add_fusion.place, bf16[128,8192]{1,0:T(8,128)(2,1)} %bitcast.3.refs_8_.refs_0_, bf16[128,8192]{1,0:T(8,128)(2,1)} %collective-permute-done.10.refs_9_.refs_1_, ...), custom_call_target="tpu_custom_call" | custom-call | flops 536870912 | bytes 37748736 | tf_op jit(solution)/shard_map/team_load/pallas_call | solution.py:289
  193.8 5.8 %copy-done = bf16[8,8192,128]{2,1,0:T(8,128)(2,1)} copy-done((bf16[8,8192,128]{2,1,0:T(8,128)(2,1)}, bf16[8,8192,128]{2,1,0:T(8,128)(2,1)S(1)}, u32[]{:S(2)}) %copy-start) | copy-done | bytes 16777240
  199.6 0.7 team_forward.7
  200.3 0.7 collective-permute-start.15
  201.0 0.7 team_forward.8
  201.6 0.7 collective-permute-start.16
  202.3 0.7 team_forward.9
  203.0 0.7 collective-permute-start.17
  203.7 0.7 team_forward.10
  204.4 0.7 collective-permute-start.18
  205.1 0.7 team_forward.11
  205.8 0.7 collective-permute-start.19
  206.5 0.7 team_forward.12
  207.1 0.7 collective-permute-start.20
  207.8 0.7 team_forward.13
  208.5 12.3 %all-to-all-start.1 = ((bf16[64,16,1152]{2,1,0:T(8,128)(2,1)}), bf16[64,16,1152]{2,1,0:T(8,128)(2,1)S(1)}, u32[]{:S(2)}, u32[]{:S(2)}) async-start(bf16[64,16,1152]{2,1,0:T(8,128)(2,1)} %bitcast.24), calls=%async_computation.1 | async-start | bytes 4718592 | tf_op jit(solution)/shard_map/all_to_all | solution.py:391
  220.9 5.8 %copy-done.1 = bf16[8,8192,128]{2,1,0:T(8,128)(2,1)S(1)} copy-done((bf16[8,8192,128]{2,1,0:T(8,128)(2,1)S(1)}, bf16[8,8192,128]{2,1,0:T(8,128)(2,1)}, u32[]{:S(2)}) %copy-start.1) | copy-done | bytes 16777240
  226.6 0.7 team_backward.8
  227.4 0.7 collective-permute-start.21
  228.1 0.8 team_backward.9
  228.9 0.7 collective-permute-start.22
  229.5 0.8 team_backward.10
  230.3 0.7 collective-permute-start.23
  231.0 0.8 team_backward.11
  231.8 0.7 collective-permute-start.24
  232.5 0.8 team_backward.12
  233.2 0.7 collective-permute-start.25
  233.9 1.0 team_backward.13
  234.9 0.7 collective-permute-start.26
  235.6 0.8 team_backward.14
  236.4 1.3 collective-permute-start.27
  237.7 200.4 %collective-permute-done.27.c_ref = bf16[16,8192]{1,0:T(8,128)(2,1)S(1)} collective-permute-done((bf16[16,8192]{1,0:T(8,128)(2,1)S(1)}, bf16[16,8192]{1,0:T(8,128)(2,1)S(1)}, u32[]{:S(2)}, u32[]{:S(2)}) %collective-permute-start.27) | collective-permute-done | bytes 262176 | tf_op jit(solution)/shard_map/ppermute | solution.py:383
  438.1 11.4 %team_backward.15 = (bf16[16,8192]{1,0:T(8,128)(2,1)}, bf16[8,8,16,1152]{3,2,1,0:T(8,128)(2,1)}) custom-call(s32[3]{0:T(128)S(1)} %pad_add_fusion.place, bf16[16,8192]{1,0:T(8,128)(2,1)S(1)} %collective-permute-done.27.c_ref, bf16[8,8192,128]{2,1,0:T(8,128)(2,1)S(1)} %copy-done.1, ...), custom_call_target="tpu_custom_call", output_to_operand_aliasing={{1}: (14, {})} | custom-call | flops 536870912 | bytes 37748736 | tf_op jit(solution)/shard_map/team_backward/pallas_call | solution.py:350
  449.6 15.8 %all-to-all-start.2 = ((bf16[64,16,1152]{2,1,0:T(8,128)(2,1)}), bf16[64,16,1152]{2,1,0:T(8,128)(2,1)}, u32[]{:S(2)}, u32[]{:S(2)}) async-start(bf16[64,16,1152]{2,1,0:T(8,128)(2,1)} %bitcast.25), calls=%async_computation.2 | async-start | bytes 4718592 | tf_op jit(solution)/shard_map/all_to_all | solution.py:391
  465.4 0.7 constant_dynamic-slice_fusion
  466.1 55.6 %all-to-all-done.2 = bf16[64,16,1152]{2,1,0:T(8,128)(2,1)} async-done(((bf16[64,16,1152]{2,1,0:T(8,128)(2,1)}), bf16[64,16,1152]{2,1,0:T(8,128)(2,1)}, u32[]{:S(2)}, u32[]{:S(2)}) %all-to-all-start.2) | async-done | bytes 2359328 | tf_op jit(solution)/shard_map/all_to_all | solution.py:391
  521.6 2.8 fusion.20
  524.4 2.4 fusion.23
  (32 shorter events, 0.2 us)
Async XLA Ops:
  0.6 60.7 %copy-start.4 = (bf16[8,16,128]{2,1,0:T(8,128)(2,1)S(1)}, bf16[8,16,128]{2,1,0:T(8,128)(2,1)}, u32[]{:S(2)}) copy-start(bf16[8,16,128]{2,1,0:T(8,128)(2,1)} %param.4) | copy-start | bytes 98308
  3.1 166.1 %copy-start.2 = (bf16[8192,128]{1,0:T(8,128)(2,1)}, bf16[8192,128]{1,0:T(8,128)(2,1)S(1)}, u32[]{:S(2)}) copy-start(bf16[8192,128]{1,0:T(8,128)(2,1)S(1)} %fusion.refs_0_.refs_8_) | copy-start | bytes 6291460
  3.1 56.8 %collective-permute-start.2 = (bf16[8192,128]{1,0:T(8,128)(2,1)S(1)}, bf16[8192,128]{1,0:T(8,128)(2,1)S(1)}, u32[]{:S(2)}, u32[]{:S(2)}) collective-permute-start(bf16[8192,128]{1,0:T(8,128)(2,1)S(1)} %fusion.refs_0_.refs_8_), channel_id=1, source_target_pairs={{0,16},{16,32},{32,48},{48,1},{1,17},{17,33},{33,49},{49,0},{2,18}... | collective-permute-start | bytes 6291464 | tf_op jit(solution)/shard_map/ppermute | solution.py:375
  8.0 53.4 %collective-permute-start.3 = (bf16[128,8192]{1,0:T(8,128)(2,1)}, bf16[128,8192]{1,0:T(8,128)(2,1)}, u32[]{:S(2)}, u32[]{:S(2)}) collective-permute-start(bf16[128,8192]{1,0:T(8,128)(2,1)} %bitcast.3.refs_8_.refs_0_), channel_id=1, source_target_pairs={{0,49},{16,0},{32,16},{48,32},{1,48},{17,1},{33,17},{49,33},{2,51}... | collective-permute-start | bytes 6291464 | tf_op jit(solution)/shard_map/ppermute | solution.py:375
  16.6 89.4 %collective-permute-start.1 = (bf16[8192,128]{1,0:T(8,128)(2,1)S(1)}, bf16[8192,128]{1,0:T(8,128)(2,1)}, u32[]{:S(2)}, u32[]{:S(2)}) collective-permute-start(bf16[8192,128]{1,0:T(8,128)(2,1)S(1)} %fusion.refs_0_.refs_8_), channel_id=1, source_target_pairs={{0,49},{16,0},{32,16},{48,32},{1,48},{17,1},{33,17},{49,33},{2,51}... | collective-permute-start | bytes 6291464 | tf_op jit(solution)/shard_map/ppermute | solution.py:375
  20.0 93.4 %collective-permute-start = (bf16[128,8192]{1,0:T(8,128)(2,1)}, bf16[128,8192]{1,0:T(8,128)(2,1)}, u32[]{:S(2)}, u32[]{:S(2)}) collective-permute-start(bf16[128,8192]{1,0:T(8,128)(2,1)} %bitcast.3.refs_8_.refs_0_), channel_id=1, source_target_pairs={{0,16},{16,32},{32,48},{48,1},{1,17},{17,33},{33,49},{49,0},{2,18}... | collective-permute-start | bytes 6291464 | tf_op jit(solution)/shard_map/ppermute | solution.py:375
  60.0 1.4 copy-start.3
  62.1 53.2 %all-to-all-start = ((bf16[64,16,128]{2,1,0:T(8,128)(2,1)}), bf16[64,16,128]{2,1,0:T(8,128)(2,1)S(1)}, u32[]{:S(2)}, u32[]{:S(2)}) async-start(bf16[64,16,128]{2,1,0:T(8,128)(2,1)} %bitcast.6), calls=%async_computation | async-start | bytes 524288 | tf_op jit(solution)/shard_map/all_to_all | solution.py:405
  76.0 74.0 %collective-permute-start.6 = (bf16[8192,128]{1,0:T(8,128)(2,1)}, bf16[8192,128]{1,0:T(8,128)(2,1)}, u32[]{:S(2)}, u32[]{:S(2)}) collective-permute-start(bf16[8192,128]{1,0:T(8,128)(2,1)} %copy-done.3), channel_id=1, source_target_pairs={{0,16},{16,32},{32,48},{48,1},{1,17},{17,33},{33,49},{49,0},{2,18}... | collective-permute-start | bytes 6291464 | tf_op jit(solution)/shard_map/ppermute | solution.py:375
  79.3 73.9 %collective-permute-start.7 = (bf16[128,8192]{1,0:T(8,128)(2,1)}, bf16[128,8192]{1,0:T(8,128)(2,1)}, u32[]{:S(2)}, u32[]{:S(2)}) collective-permute-start(bf16[128,8192]{1,0:T(8,128)(2,1)} %collective-permute-done.3.refs_10_.refs_2_), channel_id=1, source_target_pairs={{0,49},{16,0},{32,16},{48,32},{1,48},{17,1},{33,17},{49,33},{2,51}... | collective-permute-start | bytes 6291464 | tf_op jit(solution)/shard_map/ppermute | solution.py:375
  82.5 72.6 %collective-permute-start.4 = (bf16[8192,128]{1,0:T(8,128)(2,1)S(1)}, bf16[8192,128]{1,0:T(8,128)(2,1)}, u32[]{:S(2)}, u32[]{:S(2)}) collective-permute-start(bf16[8192,128]{1,0:T(8,128)(2,1)S(1)} %fusion.refs_0_.refs_8_), channel_id=1, source_target_pairs={{0,8},{8,0},{1,9},{9,1},{2,10},{10,2},{3,11},{11,3},{4,12},{12,4},... | collective-permute-start | bytes 6291464 | tf_op jit(solution)/shard_map/ppermute | solution.py:379
  106.0 51.5 %collective-permute-start.10 = (bf16[128,8192]{1,0:T(8,128)(2,1)}, bf16[128,8192]{1,0:T(8,128)(2,1)}, u32[]{:S(2)}, u32[]{:S(2)}) collective-permute-start(bf16[128,8192]{1,0:T(8,128)(2,1)} %bitcast.3.refs_8_.refs_0_), channel_id=1, source_target_pairs={{0,8},{8,0},{1,9},{9,1},{2,10},{10,2},{3,11},{11,3},{4,12},{12,4},... | collective-permute-start | bytes 6291464 | tf_op jit(solution)/shard_map/ppermute | solution.py:379
  113.4 46.0 %collective-permute-start.9 = (bf16[8192,128]{1,0:T(8,128)(2,1)}, bf16[8192,128]{1,0:T(8,128)(2,1)}, u32[]{:S(2)}, u32[]{:S(2)}) collective-permute-start(bf16[8192,128]{1,0:T(8,128)(2,1)} %copy-done.3), channel_id=1, source_target_pairs={{0,8},{8,0},{1,9},{9,1},{2,10},{10,2},{3,11},{11,3},{4,12},{12,4},... | collective-permute-start | bytes 6291464 | tf_op jit(solution)/shard_map/ppermute | solution.py:379
  150.0 12.0 %collective-permute-start.11 = (bf16[128,8192]{1,0:T(8,128)(2,1)}, bf16[128,8192]{1,0:T(8,128)(2,1)}, u32[]{:S(2)}, u32[]{:S(2)}) collective-permute-start(bf16[128,8192]{1,0:T(8,128)(2,1)} %collective-permute-done.3.refs_10_.refs_2_), channel_id=1, source_target_pairs={{0,8},{8,0},{1,9},{9,1},{2,10},{10,2},{3,11},{11,3},{4,12},{12,4},... | collective-permute-start | bytes 6291464 | tf_op jit(solution)/shard_map/ppermute | solution.py:379
  153.1 8.8 %collective-permute-start.5 = (bf16[8192,128]{1,0:T(8,128)(2,1)}, bf16[8192,128]{1,0:T(8,128)(2,1)}, u32[]{:S(2)}, u32[]{:S(2)}) collective-permute-start(bf16[8192,128]{1,0:T(8,128)(2,1)} %collective-permute-done.1.refs_2_.refs_10_), channel_id=1, source_target_pairs={{0,8},{8,0},{1,9},{9,1},{2,10},{10,2},{3,11},{11,3},{4,12},{12,4},... | collective-permute-start | bytes 6291464 | tf_op jit(solution)/shard_map/ppermute | solution.py:379
  155.1 8.2 %collective-permute-start.13 = (bf16[128,8192]{1,0:T(8,128)(2,1)}, bf16[128,8192]{1,0:T(8,128)(2,1)}, u32[]{:S(2)}, u32[]{:S(2)}) collective-permute-start(bf16[128,8192]{1,0:T(8,128)(2,1)} %collective-permute-done.refs_14_.refs_6_), channel_id=1, source_target_pairs={{0,8},{8,0},{1,9},{9,1},{2,10},{10,2},{3,11},{11,3},{4,12},{12,4},... | collective-permute-start | bytes 6291464 | tf_op jit(solution)/shard_map/ppermute | solution.py:379
  157.5 8.7 %collective-permute-start.8 = (bf16[8192,128]{1,0:T(8,128)(2,1)}, bf16[8192,128]{1,0:T(8,128)(2,1)}, u32[]{:S(2)}, u32[]{:S(2)}) collective-permute-start(bf16[8192,128]{1,0:T(8,128)(2,1)} %collective-permute-done.6.refs_4_.refs_12_), channel_id=1, source_target_pairs={{0,8},{8,0},{1,9},{9,1},{2,10},{10,2},{3,11},{11,3},{4,12},{12,4},... | collective-permute-start | bytes 6291464 | tf_op jit(solution)/shard_map/ppermute | solution.py:379
  159.4 9.8 %collective-permute-start.12 = (bf16[128,8192]{1,0:T(8,128)(2,1)}, bf16[128,8192]{1,0:T(8,128)(2,1)}, u32[]{:S(2)}, u32[]{:S(2)}) collective-permute-start(bf16[128,8192]{1,0:T(8,128)(2,1)} %collective-permute-done.7.refs_12_.refs_4_), channel_id=1, source_target_pairs={{0,8},{8,0},{1,9},{9,1},{2,10},{10,2},{3,11},{11,3},{4,12},{12,4},... | collective-permute-start | bytes 6291464 | tf_op jit(solution)/shard_map/ppermute | solution.py:379
  182.2 17.4 %collective-permute-start.14 = (bf16[16,8192]{1,0:T(8,128)(2,1)S(1)}, bf16[16,8192]{1,0:T(8,128)(2,1)S(1)}, u32[]{:S(2)}, u32[]{:S(2)}) collective-permute-start(bf16[16,8192]{1,0:T(8,128)(2,1)S(1)} %get-tuple-element.62.refs_16_), channel_id=1, source_target_pairs={{0,64},{1,65},{2,66},{3,67},{4,68},{5,69},{6,70},{7,71},{8,72},{9,... | collective-permute-start | bytes 786440 | tf_op jit(solution)/shard_map/ppermute | solution.py:383
  193.8 5.8 %copy-start = (bf16[8,8192,128]{2,1,0:T(8,128)(2,1)}, bf16[8,8192,128]{2,1,0:T(8,128)(2,1)S(1)}, u32[]{:S(2)}) copy-start(bf16[8,8192,128]{2,1,0:T(8,128)(2,1)S(1)} %get-tuple-element.88.turned_out) | copy-start | bytes 50331652
  200.3 0.7 collective-permute-start.15
  201.6 0.7 collective-permute-start.16
  203.0 0.7 collective-permute-start.17
  204.4 0.7 collective-permute-start.18
  205.8 0.7 collective-permute-start.19
  207.1 0.7 collective-permute-start.20
  208.5 241.0 %all-to-all-start.1 = ((bf16[64,16,1152]{2,1,0:T(8,128)(2,1)}), bf16[64,16,1152]{2,1,0:T(8,128)(2,1)S(1)}, u32[]{:S(2)}, u32[]{:S(2)}) async-start(bf16[64,16,1152]{2,1,0:T(8,128)(2,1)} %bitcast.24), calls=%async_computation.1 | async-start | bytes 4718592 | tf_op jit(solution)/shard_map/all_to_all | solution.py:391
  220.9 5.8 %copy-start.1 = (bf16[8,8192,128]{2,1,0:T(8,128)(2,1)S(1)}, bf16[8,8192,128]{2,1,0:T(8,128)(2,1)}, u32[]{:S(2)}) copy-start(bf16[8,8192,128]{2,1,0:T(8,128)(2,1)} %copy-done) | copy-start | bytes 50331652
  227.4 0.7 collective-permute-start.21
  228.9 0.7 collective-permute-start.22
  230.3 0.7 collective-permute-start.23
  231.8 0.7 collective-permute-start.24
  233.2 0.7 collective-permute-start.25
  234.9 0.7 collective-permute-start.26
  236.4 201.7 %collective-permute-start.27 = (bf16[16,8192]{1,0:T(8,128)(2,1)S(1)}, bf16[16,8192]{1,0:T(8,128)(2,1)S(1)}, u32[]{:S(2)}, u32[]{:S(2)}) collective-permute-start(bf16[16,8192]{1,0:T(8,128)(2,1)S(1)} %get-tuple-element.103), channel_id=1, source_target_pairs={{64,0},{65,1},{66,2},{67,3},{68,4},{69,5},{70,6},{71,7},{72,8},{73... | collective-permute-start | bytes 786440 | tf_op jit(solution)/shard_map/ppermute | solution.py:383
  449.6 72.1 %all-to-all-start.2 = ((bf16[64,16,1152]{2,1,0:T(8,128)(2,1)}), bf16[64,16,1152]{2,1,0:T(8,128)(2,1)}, u32[]{:S(2)}, u32[]{:S(2)}) async-start(bf16[64,16,1152]{2,1,0:T(8,128)(2,1)} %bitcast.25), calls=%async_computation.2 | async-start | bytes 4718592 | tf_op jit(solution)/shard_map/all_to_all | solution.py:391

commit v4 on v3

--- a/solution.py
+++ b/solution.py
@@ -123,42 +123,42 @@
         )
 
 
-def load_kernel(place, *refs):
-    pieces_out, pieces_in = refs[:8], refs[8:16]
-    held_out, turned_out, turned_in = refs[17:20]
-    first, second, last, sems, in_sem, out_sems, last_sem = refs[20:]
-    for layer in range(LAYERS):
-        fetch(place, pieces_out, held_out, sems, layer)
-    fetch(place, pieces_in, last, in_sem, LAYERS - 1)
+def turn_kernel(keep, place, *refs):
+    pieces, refs = refs[:8], refs[9:]
+    turned, held, turn, sems, out_sems = (refs[1], refs[0], *refs[2:]) if keep else refs
+
+    def begin(layer, carry):
+        fetch(place, pieces, held, sems, layer)
+        return carry
+
+    lax.fori_loop(0, LAYERS, begin, 0)
 
     def step(layer, carry):
         slot = lax.rem(layer, 2)
-        copy = pltpu.make_async_copy(first.at[slot], turned_out.at[layer], out_sems.at[slot])
+        copy = pltpu.make_async_copy(turn.at[slot], turned.at[layer], out_sems.at[slot])
 
         @pl.when(layer >= 2)
         def _():
             copy.wait()
 
-        await_fetch(pieces_out, held_out, sems, layer)
+        await_fetch(pieces, held, sems, layer)
         for at in range(0, D, HD):
-            first[slot, at : at + HD, :] = held_out[layer, :, at : at + HD].T
+            block = slice(at, at + HD)
+            if keep:
+                turn[slot, block, :] = held[layer, :, block].T
+            else:
+                turn[slot, :, block] = held[layer, block, :].T
         copy.start()
         return carry
 
     lax.fori_loop(0, LAYERS, step, 0)
-    await_fetch(pieces_in, last, in_sem, 0)
-    for at in range(0, D, HD):
-        second[:, at : at + HD] = last[0, at : at + HD, :].T
-    copy = pltpu.make_async_copy(second, turned_in, last_sem.at[0])
-    copy.start()
     for layer in range(LAYERS - 2, LAYERS):
         pltpu.make_async_copy(
-            first.at[layer % 2], turned_out.at[layer], out_sems.at[layer % 2]
+            turn.at[layer % 2], turned.at[layer], out_sems.at[layer % 2]
         ).wait()
-    copy.wait()
-
-
-def backward_layer(layer, refs, first, second, extra):
+
+
+def backward_layer(layer, refs, first, second):
     (stash_ref, stash_out, cotangent, rounded, stash, wide, small, in_sems, out_sems) = refs
     for part in range(PARTS):
         lanes = slice(part * SLICE, (part + 1) * SLICE)
@@ -166,7 +166,6 @@
         rounded[:, lanes] = value
         wide[layer, part, :, :SLICE] = value
     upper = jnp.dot(rounded[...], first(), preferred_element_type=f32)
-    extra()
     project = small[layer, 0]
     inverse = small[layer, 1]
     sigma = jax.nn.sigmoid(project)
@@ -186,67 +185,53 @@
 
 
 def backward_kernel(tick, place, c_ref, turned_out, turned_in, *refs):
-    pieces_in, stash_ref, small_in = refs[:8], refs[8], refs[9]
-    refs = refs[10:] if tick == LAST else refs[11:]
+    stash_ref, small_in = refs[:2]
+    refs = refs[2:] if tick == LAST else refs[3:]
     sent_ref, stash_out = refs[:2]
-    (cotangent, rounded, stash, wide, small, in_sems, out_sems, held_in, held_sems) = refs[2:11]
-    last_sem, *seconds = refs[11:14]
+    (cotangent, rounded, stash, wide, small, in_sems, out_sems, second, sems) = refs[2:]
     common = (
         stash_ref, stash_out, cotangent, rounded, stash, wide, small, in_sems, out_sems,
     )
 
-    def turn(layer, second):
+    def fetch_turned(layer):
         slot = lax.rem(layer, SLOTS)
-        for at in range(0, D, HD):
-            second[:, at : at + HD] = held_in[slot, at : at + HD, :].T
-
-    def one_layer(layer, now, later):
-        @pl.when(layer >= SLOTS)
-        def _():
-            fetch(place, pieces_in, held_in, held_sems, layer - SLOTS)
-
-        @pl.when(layer > 0)
-        def _():
-            await_fetch(pieces_in, held_in, held_sems, layer - 1)
-
-        pltpu.make_async_copy(stash_ref.at[layer], stash.at[layer], in_sems.at[layer]).wait()
-        backward_layer(
-            layer,
-            common,
-            lambda: turned_out[layer],
-            lambda lanes: now[:, lanes],
-            lambda: turn(jnp.maximum(layer - 1, 0), later),
-        )
+        return pltpu.make_async_copy(turned_in.at[layer], second.at[slot], sems.at[slot])
 
     @pl.when(place[0] == tick)
     def _():
         start = pltpu.make_async_copy(small_in, small, in_sems.at[LAYERS])
         start.start()
-        last = pltpu.make_async_copy(turned_in, seconds[0], last_sem.at[0])
-        last.start()
 
         def begin(back, carry):
             layer = LAYERS - 1 - back
             pltpu.make_async_copy(stash_ref.at[layer], stash.at[layer], in_sems.at[layer]).start()
 
-            @pl.when((back > 0) & (back < SLOTS))
+            @pl.when(back < AHEAD)
             def _():
-                fetch(place, pieces_in, held_in, held_sems, layer)
+                fetch_turned(layer).start()
 
             return carry
 
         lax.fori_loop(0, LAYERS, begin, 0)
         cotangent[...] = c_ref[...].astype(f32)
         start.wait()
-        last.wait()
-
-        def two_layers(back, carry):
-            layer = LAYERS - 1 - 2 * back
-            one_layer(layer, seconds[0], seconds[1])
-            one_layer(layer - 1, seconds[1], seconds[0])
+
+        def step(back, carry):
+            layer = LAYERS - 1 - back
+            slot = lax.rem(layer, SLOTS)
+
+            @pl.when(layer >= AHEAD)
+            def _():
+                fetch_turned(layer - AHEAD).start()
+
+            fetch_turned(layer).wait()
+            pltpu.make_async_copy(stash_ref.at[layer], stash.at[layer], in_sems.at[layer]).wait()
+            backward_layer(
+                layer, common, lambda: turned_out[layer], lambda lanes: second[slot, :, lanes]
+            )
             return carry
 
-        lax.fori_loop(0, LAYERS // 2, two_layers, 0)
+        lax.fori_loop(0, LAYERS, step, 0)
         sent_ref[...] = cotangent[...].astype(bf16)
 
         def end(layer, carry):
@@ -285,29 +270,25 @@
 ]
 
 
-def run_load(place, pieces_in, pieces_out, after):
+def run_turn(keep, place, pieces, after):
+    tall, flat = (LAYERS, D, HD), (LAYERS, HD, D)
+    turned = tall if keep else flat
+    held = pltpu.VMEM(flat if keep else tall, bf16)
     return pl.pallas_call(
-        load_kernel,
-        in_specs=[SMEM] + [ANY] * 17,
-        out_specs=[VMEM, ANY, ANY],
-        out_shape=[
-            pltpu.VMEM((LAYERS, HD, D), bf16),
-            jax.ShapeDtypeStruct((LAYERS, D, HD), bf16),
-            pltpu.HBM((HD, D), bf16),
+        functools.partial(turn_kernel, keep),
+        in_specs=[SMEM] + [ANY] * 9,
+        out_specs=[VMEM, ANY] if keep else ANY,
+        out_shape=[held, pltpu.HBM(turned, bf16)] if keep else pltpu.HBM(turned, bf16),
+        scratch_shapes=([] if keep else [held])
+        + [
+            pltpu.VMEM((2,) + turned[1:], bf16),
+            pltpu.SemaphoreType.DMA((LAYERS,)),
+            pltpu.SemaphoreType.DMA((2,)),
         ],
-        scratch_shapes=[
-            pltpu.VMEM((2, D, HD), bf16),
-            pltpu.VMEM((HD, D), bf16),
-            pltpu.VMEM((1, D, HD), bf16),
-            pltpu.SemaphoreType.DMA((LAYERS,)),
-            pltpu.SemaphoreType.DMA((1,)),
-            pltpu.SemaphoreType.DMA((2,)),
-            pltpu.SemaphoreType.DMA((1,)),
-        ],
-        compiler_params=pltpu.CompilerParams(vmem_limit_bytes=10 * 2**20),
+        compiler_params=pltpu.CompilerParams(vmem_limit_bytes=(6 if keep else 22) * 2**20),
         cost_estimate=COST,
-        name="team_load",
-    )(place, *map(in_hbm, pieces_out), *map(in_hbm, pieces_in), after)
+        name="team_turn",
+    )(place, *map(in_hbm, pieces), after)
 
 
 def run_early(tick, place, x, pieces_in, pieces_out, stash, small):
@@ -345,14 +326,14 @@
     )(place, x, in_vmem(held_out), *map(in_hbm, pieces_in), in_hbm(stash), in_hbm(small))
 
 
-def run_backward(tick, place, c, turned_out, turned_in, pieces_in, stash, small, cots):
+def run_backward(tick, place, c, turned_out, turned_in, stash, small, cots):
     older = [] if cots is None else [cots]
     return pl.pallas_call(
         functools.partial(backward_kernel, tick),
-        in_specs=[SMEM, VMEM, VMEM] + [ANY] * (11 + len(older)),
+        in_specs=[SMEM, VMEM, VMEM] + [ANY] * (3 + len(older)),
         out_specs=[VMEM, ANY],
         out_shape=[SENT, STASH],
-        input_output_aliases={14: 1} if older else {},
+        input_output_aliases={6: 1} if older else {},
         scratch_shapes=STATE
         + [
             pltpu.VMEM(STASH.shape, bf16),
@@ -360,13 +341,13 @@
             pltpu.VMEM(SMALL.shape, f32),
             pltpu.SemaphoreType.DMA((LAYERS + 1,)),
             pltpu.SemaphoreType.DMA((LAYERS,)),
-        ]
-        + STREAM_IN
-        + [pltpu.SemaphoreType.DMA((1,)), pltpu.VMEM((HD, D), bf16), pltpu.VMEM((HD, D), bf16)],
-        compiler_params=PARAMS,
+            pltpu.VMEM((SLOTS, HD, D), bf16),
+            pltpu.SemaphoreType.DMA((SLOTS,)),
+        ],
+        compiler_params=pltpu.CompilerParams(vmem_limit_bytes=16 * 2**20),
         cost_estimate=COST,
         name="team_backward",
-    )(place, c, in_vmem(turned_out), *map(in_hbm, [turned_in, *pieces_in, stash, small, *older]))
+    )(place, c, in_vmem(turned_out), *map(in_hbm, [turned_in, stash, small, *older]))
 
 
 def along_z(value, steps):
@@ -419,16 +400,17 @@
             x, stash, small = run_early(tick, place, x, pieces_in, pieces_out, stash, small)
             continue
         if tick == EARLY:
-            held_out, turned_out, turned_in = run_load(place, pieces_in, pieces_out, last)
+            held_out, turned_out = run_turn(True, place, pieces_out, last)
+        if tick == EARLY + 1:
+            turned_in = run_turn(False, place, pieces_in, last)
+            x, turned_in = lax.optimization_barrier((x, turned_in))
         x, stash, small = run_forward(tick, place, x, held_out, pieces_in, stash, small)
     x, stash_sent = lax.optimization_barrier((x, stash))
     first = exchange(stash_sent)
     for tick in range(LAST, -1, -1):
         if tick < LAST:
             x = along_y(x, tick + 1, tick)
-        x, cots = run_backward(
-            tick, place, x, turned_out, turned_in, pieces_in, stash, small, cots
-        )
+        x, cots = run_backward(tick, place, x, turned_out, turned_in, stash, small, cots)
 
     second = exchange(cots)
     part = lax.axis_index("x") * 2 + lax.axis_index("zh")

time: 528 us -> 519 us (0.983)
  waiting for transfers between devices: 357 us -> 339 us
  Pallas kernels: 44.9 us -> 58.9 us
  local copies, waits for them, and re-layouts: 14.4 us -> 8.56 us
    ppermute x14, waiting for transfers between devices: 200 us -> 183 us  [along_y(): return lax.ppermute(value, 'y', [(source, target)])]
    pallas_call x1 -> x2, Pallas kernels: 10.3 us -> 25.7 us  [run_turn(): pl.pallas_call(functools.partial(turn_kernel, keep), in_specs=[SMEM] + [A...]
    unnamed x10 -> x8, local copies, waits for them, and re-layouts: 12.9 us -> 7.11 us
  transfers between devices with their start and end apart: 31 -> 31, of which waited for: 8 -> 8; matrix products, arithmetic and copies ran while one was open for 0% -> 0% of each run, Pallas kernels for 5% -> 8%
where the time goes in v4:
time: 519 us; the launch traced here: 518 us
  waiting for transfers between devices  339 us (65%)
  starting transfers between devices  102 us (20%)
  Pallas kernels  58.9 us (11%)
  local copies, waits for them, and re-layouts  8.56 us (2%)
  matrix products  5.19 us (1%)
    ppermute x14, waiting for transfers between devices, along_y(): return lax.ppermute(value, 'y', [(source, target)])  183 us
    ppermute x6, waiting for transfers between devices, along_z(): return lax.ppermute(value, ('zl', 'zh'), pairs)  93.3 us
    all_to_all x2, waiting for transfers between devices, exchange(): flat = lax.all_to_all(flat, PLANE, 0, 0, tiled=True)  55.6 us
    all_to_all x2, starting transfers between devices, exchange(): flat = lax.all_to_all(flat, PLANE, 0, 0, tiled=True)  28.1 us
    pallas_call x2, Pallas kernels, run_turn(): pl.pallas_call(functools.partial(turn_kernel, keep), in_specs=[SMEM] + [A...  25.7 us
    ppermute x6, starting transfers between devices, along_z(): return lax.ppermute(value, ('zl', 'zh'), pairs)  25.2 us
    ppermute x8, starting transfers between devices, swap_cores(): return lax.ppermute(value, 'core', [(0, 1), (1, 0)])  24 us
    pallas_call x8, Pallas kernels, run_backward(): pl.pallas_call(functools.partial(backward_kernel, tick), in_specs=[SMEM,...  15.5 us
  transfers between devices with their start and end apart: 31, of which 8 were waited for; matrix products, arithmetic and copies ran while one was open for 0% of the time, Pallas kernels for 8%

profile of v4, /device:TPU:1, one launch (start us, length us, event | category | flops | bytes accessed | tf_op | source)
XLA Modules:
  0.0 517.8 jit_solution(10039247707582595177)
XLA Ops:
  0.6 2.5 fusion.refs_0_
  3.1 4.8 collective-permute-start.2
  8.0 8.6 %collective-permute-start.3 = (bf16[128,8192]{1,0:T(8,128)(2,1)}, bf16[128,8192]{1,0:T(8,128)(2,1)}, u32[]{:S(2)}, u32[]{:S(2)}) collective-permute-start(bf16[128,8192]{1,0:T(8,128)(2,1)} %bitcast.3.refs_8_.refs_0_), channel_id=1, source_target_pairs={{0,49},{16,0},{32,16},{48,32},{1,48},{17,1},{33,17},{49,33},{2,51}... | collective-permute-start | bytes 6291464 | tf_op jit(solution)/shard_map/ppermute | solution.py:356
  16.6 3.4 collective-permute-start.1
  20.0 1.9 collective-permute-start
  21.9 38.1 %collective-permute-done.2.refs_6_ = bf16[8192,128]{1,0:T(8,128)(2,1)S(1)} collective-permute-done((bf16[8192,128]{1,0:T(8,128)(2,1)S(1)}, bf16[8192,128]{1,0:T(8,128)(2,1)S(1)}, u32[]{:S(2)}, u32[]{:S(2)}) %collective-permute-start.2) | collective-permute-done | bytes 2097184 | tf_op jit(solution)/shard_map/ppermute | solution.py:356
  60.0 1.3 copy-done.2
  61.3 0.7 broadcast_in_dim.9
  62.1 13.9 %all-to-all-start = ((bf16[64,16,128]{2,1,0:T(8,128)(2,1)}), bf16[64,16,128]{2,1,0:T(8,128)(2,1)S(1)}, u32[]{:S(2)}, u32[]{:S(2)}) async-start(bf16[64,16,128]{2,1,0:T(8,128)(2,1)} %bitcast.6), calls=%async_computation | async-start | bytes 524288 | tf_op jit(solution)/shard_map/all_to_all | solution.py:386
  76.0 3.3 collective-permute-start.6
  79.3 3.2 collective-permute-start.7
  82.5 2.9 collective-permute-start.4
  85.4 20.6 %collective-permute-done.1.refs_2_ = bf16[8192,128]{1,0:T(8,128)(2,1)} collective-permute-done((bf16[8192,128]{1,0:T(8,128)(2,1)S(1)}, bf16[8192,128]{1,0:T(8,128)(2,1)}, u32[]{:S(2)}, u32[]{:S(2)}) %collective-permute-start.1) | collective-permute-done | bytes 2097184 | tf_op jit(solution)/shard_map/ppermute | solution.py:356
  106.0 7.4 %collective-permute-start.10 = (bf16[128,8192]{1,0:T(8,128)(2,1)}, bf16[128,8192]{1,0:T(8,128)(2,1)}, u32[]{:S(2)}, u32[]{:S(2)}) collective-permute-start(bf16[128,8192]{1,0:T(8,128)(2,1)} %bitcast.3.refs_8_.refs_0_), channel_id=1, source_target_pairs={{0,8},{8,0},{1,9},{9,1},{2,10},{10,2},{3,11},{11,3},{4,12},{12,4},... | collective-permute-start | bytes 6291464 | tf_op jit(solution)/shard_map/ppermute | solution.py:360
  113.4 1.9 collective-permute-start.9
  115.4 34.6 %collective-permute-done.6.refs_4_ = bf16[8192,128]{1,0:T(8,128)(2,1)} collective-permute-done((bf16[8192,128]{1,0:T(8,128)(2,1)}, bf16[8192,128]{1,0:T(8,128)(2,1)}, u32[]{:S(2)}, u32[]{:S(2)}) %collective-permute-start.6) | collective-permute-done | bytes 2097184 | tf_op jit(solution)/shard_map/ppermute | solution.py:356
  150.0 3.1 collective-permute-start.11
  153.1 1.9 collective-permute-start.5
  155.1 2.4 collective-permute-start.13
  157.5 1.9 collective-permute-start.8
  159.4 2.4 collective-permute-start.12
  161.9 1.3 collective-permute-done.13.refs_15_.refs_7_
  163.2 3.0 collective-permute-done.8.refs_5_
  166.2 3.0 collective-permute-done.12.refs_13_.refs_5_
  169.2 12.9 %team_early.1 = (bf16[16,8192]{1,0:T(8,128)(2,1)S(1)}, bf16[8,8,16,1152]{3,2,1,0:T(8,128)(2,1)}, f32[8,2,16,128]{3,2,1,0:T(8,128)}) custom-call(s32[3]{0:T(128)S(1)} %pad_add_fusion.place, bf16[16,8192]{1,0:T(8,128)(2,1)S(1)} %copy_bitcast_fusion.x_ref, bf16[8192,128]{1,0:T(8,128)(2,1)} %copy-done.1, bf16[8192,128]{1,0:T(8,128)(2,1)} %collective-permute-done.4.refs_1_, ...), custom_call_target="tpu_custom_call" | custom-call | flops 536870912 | bytes 37748736 | tf_op jit(solution)/shard_map/team_early/pallas_call | solution.py:296
  182.2 1.3 collective-permute-start.14
  183.5 12.9 %team_turn.2 = (bf16[8,128,8192]{2,1,0:T(8,128)(2,1)S(1)}, bf16[8,8192,128]{2,1,0:T(8,128)(2,1)}) custom-call(s32[3]{0:T(128)S(1)} %pad_add_fusion.place, bf16[128,8192]{1,0:T(8,128)(2,1)} %bitcast.3.refs_8_.refs_0_, bf16[128,8192]{1,0:T(8,128)(2,1)} %collective-permute-done.10.refs_9_.refs_1_, bf16[128,8192]{1,0:T(8,128)(2,1)} %collective-permute-done.3.refs_10_.refs_2_, ...), custom_call_target="tpu_custom_call" | custom-call | flops 536870912 | bytes 37748736 | tf_op jit(solution)/shard_map/team_turn/pallas_call | solution.py:277
  196.4 0.7 team_forward.7
  197.0 0.7 collective-permute-start.15
  197.7 12.9 %team_turn.3.turned_in = bf16[8,128,8192]{2,1,0:T(8,128)(2,1)} custom-call(s32[3]{0:T(128)S(1)} %pad_add_fusion.place, bf16[8192,128]{1,0:T(8,128)(2,1)} %copy-done.1, bf16[8192,128]{1,0:T(8,128)(2,1)} %collective-permute-done.4.refs_1_, bf16[8192,128]{1,0:T(8,128)(2,1)} %collective-permute-done.1.refs_2_, bf16[8192,128]{1,0:T(8,128)(2,1)} %collective-permute-done.5.refs_3_, ...), custom_call_target="tpu_custom_call" | custom-call | flops 536870912 | bytes 37748736 | tf_op jit(solution)/shard_map/team_turn/pallas_call | solution.py:277
  210.6 0.7 team_forward.8
  211.3 0.7 collective-permute-start.16
  212.0 0.7 team_forward.9
  212.7 0.7 collective-permute-start.17
  213.4 0.7 team_forward.10
  214.0 0.7 collective-permute-start.18
  214.7 0.7 team_forward.11
  215.4 0.7 collective-permute-start.19
  216.1 0.7 team_forward.12
  216.8 0.7 collective-permute-start.20
  217.5 0.7 team_forward.13
  218.2 12.3 %all-to-all-start.1 = ((bf16[64,16,1152]{2,1,0:T(8,128)(2,1)}), bf16[64,16,1152]{2,1,0:T(8,128)(2,1)S(1)}, u32[]{:S(2)}, u32[]{:S(2)}) async-start(bf16[64,16,1152]{2,1,0:T(8,128)(2,1)} %bitcast.24), calls=%async_computation.1 | async-start | bytes 4718592 | tf_op jit(solution)/shard_map/all_to_all | solution.py:372
  230.5 5.8 %copy-done = bf16[8,8192,128]{2,1,0:T(8,128)(2,1)S(1)} copy-done((bf16[8,8192,128]{2,1,0:T(8,128)(2,1)S(1)}, bf16[8,8192,128]{2,1,0:T(8,128)(2,1)}, u32[]{:S(2)}) %copy-start) | copy-done | bytes 16777240
  236.3 0.7 team_backward.8
  237.0 0.7 collective-permute-start.21
  237.7 0.7 team_backward.9
  238.5 0.7 collective-permute-start.22
  239.2 0.7 team_backward.10
  239.9 0.7 collective-permute-start.23
  240.6 0.7 team_backward.11
  241.4 0.7 collective-permute-start.24
  242.1 0.7 team_backward.12
  242.8 0.7 collective-permute-start.25
  243.5 0.7 team_backward.13
  244.3 0.7 collective-permute-start.26
  245.0 0.7 team_backward.14
  245.7 1.3 collective-permute-start.27
  247.0 183.2 %collective-permute-done.27.c_ref = bf16[16,8192]{1,0:T(8,128)(2,1)S(1)} collective-permute-done((bf16[16,8192]{1,0:T(8,128)(2,1)S(1)}, bf16[16,8192]{1,0:T(8,128)(2,1)S(1)}, u32[]{:S(2)}, u32[]{:S(2)}) %collective-permute-start.27) | collective-permute-done | bytes 262176 | tf_op jit(solution)/shard_map/ppermute | solution.py:364
  430.2 10.3 %team_backward.15 = (bf16[16,8192]{1,0:T(8,128)(2,1)}, bf16[8,8,16,1152]{3,2,1,0:T(8,128)(2,1)}) custom-call(s32[3]{0:T(128)S(1)} %pad_add_fusion.place, bf16[16,8192]{1,0:T(8,128)(2,1)S(1)} %collective-permute-done.27.c_ref, bf16[8,8192,128]{2,1,0:T(8,128)(2,1)S(1)} %copy-done, ...), custom_call_target="tpu_custom_call", output_to_operand_aliasing={{1}: (6, {})} | custom-call | flops 536870912 | bytes 37748736 | tf_op jit(solution)/shard_map/team_backward/pallas_call | solution.py:331
  440.5 15.8 %all-to-all-start.2 = ((bf16[64,16,1152]{2,1,0:T(8,128)(2,1)}), bf16[64,16,1152]{2,1,0:T(8,128)(2,1)}, u32[]{:S(2)}, u32[]{:S(2)}) async-start(bf16[64,16,1152]{2,1,0:T(8,128)(2,1)} %bitcast.25), calls=%async_computation.2 | async-start | bytes 4718592 | tf_op jit(solution)/shard_map/all_to_all | solution.py:372
  456.4 0.7 constant_dynamic-slice_fusion
  457.0 55.6 %all-to-all-done.2 = bf16[64,16,1152]{2,1,0:T(8,128)(2,1)} async-done(((bf16[64,16,1152]{2,1,0:T(8,128)(2,1)}), bf16[64,16,1152]{2,1,0:T(8,128)(2,1)}, u32[]{:S(2)}, u32[]{:S(2)}) %all-to-all-start.2) | async-done | bytes 2359328 | tf_op jit(solution)/shard_map/all_to_all | solution.py:372
  512.6 2.8 fusion.20
  515.4 2.4 fusion.23
  (31 shorter events, 0.2 us)
Async XLA Ops:
  0.6 60.7 %copy-start.3 = (bf16[8,16,128]{2,1,0:T(8,128)(2,1)S(1)}, bf16[8,16,128]{2,1,0:T(8,128)(2,1)}, u32[]{:S(2)}) copy-start(bf16[8,16,128]{2,1,0:T(8,128)(2,1)} %param.4) | copy-start | bytes 98308
  3.1 166.1 %copy-start.1 = (bf16[8192,128]{1,0:T(8,128)(2,1)}, bf16[8192,128]{1,0:T(8,128)(2,1)S(1)}, u32[]{:S(2)}) copy-start(bf16[8192,128]{1,0:T(8,128)(2,1)S(1)} %fusion.refs_0_) | copy-start | bytes 6291460
  3.1 56.8 %collective-permute-start.2 = (bf16[8192,128]{1,0:T(8,128)(2,1)S(1)}, bf16[8192,128]{1,0:T(8,128)(2,1)S(1)}, u32[]{:S(2)}, u32[]{:S(2)}) collective-permute-start(bf16[8192,128]{1,0:T(8,128)(2,1)S(1)} %fusion.refs_0_), channel_id=1, source_target_pairs={{0,16},{16,32},{32,48},{48,1},{1,17},{17,33},{33,49},{49,0},{2,18}... | collective-permute-start | bytes 6291464 | tf_op jit(solution)/shard_map/ppermute | solution.py:356
  8.0 53.4 %collective-permute-start.3 = (bf16[128,8192]{1,0:T(8,128)(2,1)}, bf16[128,8192]{1,0:T(8,128)(2,1)}, u32[]{:S(2)}, u32[]{:S(2)}) collective-permute-start(bf16[128,8192]{1,0:T(8,128)(2,1)} %bitcast.3.refs_8_.refs_0_), channel_id=1, source_target_pairs={{0,49},{16,0},{32,16},{48,32},{1,48},{17,1},{33,17},{49,33},{2,51}... | collective-permute-start | bytes 6291464 | tf_op jit(solution)/shard_map/ppermute | solution.py:356
  16.6 89.4 %collective-permute-start.1 = (bf16[8192,128]{1,0:T(8,128)(2,1)S(1)}, bf16[8192,128]{1,0:T(8,128)(2,1)}, u32[]{:S(2)}, u32[]{:S(2)}) collective-permute-start(bf16[8192,128]{1,0:T(8,128)(2,1)S(1)} %fusion.refs_0_), channel_id=1, source_target_pairs={{0,49},{16,0},{32,16},{48,32},{1,48},{17,1},{33,17},{49,33},{2,51}... | collective-permute-start | bytes 6291464 | tf_op jit(solution)/shard_map/ppermute | solution.py:356
  20.0 93.4 %collective-permute-start = (bf16[128,8192]{1,0:T(8,128)(2,1)}, bf16[128,8192]{1,0:T(8,128)(2,1)}, u32[]{:S(2)}, u32[]{:S(2)}) collective-permute-start(bf16[128,8192]{1,0:T(8,128)(2,1)} %bitcast.3.refs_8_.refs_0_), channel_id=1, source_target_pairs={{0,16},{16,32},{32,48},{48,1},{1,17},{17,33},{33,49},{49,0},{2,18}... | collective-permute-start | bytes 6291464 | tf_op jit(solution)/shard_map/ppermute | solution.py:356
  60.0 1.3 copy-start.2
  62.1 53.3 %all-to-all-start = ((bf16[64,16,128]{2,1,0:T(8,128)(2,1)}), bf16[64,16,128]{2,1,0:T(8,128)(2,1)S(1)}, u32[]{:S(2)}, u32[]{:S(2)}) async-start(bf16[64,16,128]{2,1,0:T(8,128)(2,1)} %bitcast.6), calls=%async_computation | async-start | bytes 524288 | tf_op jit(solution)/shard_map/all_to_all | solution.py:386
  76.0 74.0 %collective-permute-start.6 = (bf16[8192,128]{1,0:T(8,128)(2,1)}, bf16[8192,128]{1,0:T(8,128)(2,1)}, u32[]{:S(2)}, u32[]{:S(2)}) collective-permute-start(bf16[8192,128]{1,0:T(8,128)(2,1)} %copy-done.2), channel_id=1, source_target_pairs={{0,16},{16,32},{32,48},{48,1},{1,17},{17,33},{33,49},{49,0},{2,18}... | collective-permute-start | bytes 6291464 | tf_op jit(solution)/shard_map/ppermute | solution.py:356
  79.3 73.9 %collective-permute-start.7 = (bf16[128,8192]{1,0:T(8,128)(2,1)}, bf16[128,8192]{1,0:T(8,128)(2,1)}, u32[]{:S(2)}, u32[]{:S(2)}) collective-permute-start(bf16[128,8192]{1,0:T(8,128)(2,1)} %collective-permute-done.3.refs_10_.refs_2_), channel_id=1, source_target_pairs={{0,49},{16,0},{32,16},{48,32},{1,48},{17,1},{33,17},{49,33},{2,51}... | collective-permute-start | bytes 6291464 | tf_op jit(solution)/shard_map/ppermute | solution.py:356
  82.5 72.6 %collective-permute-start.4 = (bf16[8192,128]{1,0:T(8,128)(2,1)S(1)}, bf16[8192,128]{1,0:T(8,128)(2,1)}, u32[]{:S(2)}, u32[]{:S(2)}) collective-permute-start(bf16[8192,128]{1,0:T(8,128)(2,1)S(1)} %fusion.refs_0_), channel_id=1, source_target_pairs={{0,8},{8,0},{1,9},{9,1},{2,10},{10,2},{3,11},{11,3},{4,12},{12,4},... | collective-permute-start | bytes 6291464 | tf_op jit(solution)/shard_map/ppermute | solution.py:360
  106.0 51.5 %collective-permute-start.10 = (bf16[128,8192]{1,0:T(8,128)(2,1)}, bf16[128,8192]{1,0:T(8,128)(2,1)}, u32[]{:S(2)}, u32[]{:S(2)}) collective-permute-start(bf16[128,8192]{1,0:T(8,128)(2,1)} %bitcast.3.refs_8_.refs_0_), channel_id=1, source_target_pairs={{0,8},{8,0},{1,9},{9,1},{2,10},{10,2},{3,11},{11,3},{4,12},{12,4},... | collective-permute-start | bytes 6291464 | tf_op jit(solution)/shard_map/ppermute | solution.py:360
  113.4 46.0 %collective-permute-start.9 = (bf16[8192,128]{1,0:T(8,128)(2,1)}, bf16[8192,128]{1,0:T(8,128)(2,1)}, u32[]{:S(2)}, u32[]{:S(2)}) collective-permute-start(bf16[8192,128]{1,0:T(8,128)(2,1)} %copy-done.2), channel_id=1, source_target_pairs={{0,8},{8,0},{1,9},{9,1},{2,10},{10,2},{3,11},{11,3},{4,12},{12,4},... | collective-permute-start | bytes 6291464 | tf_op jit(solution)/shard_map/ppermute | solution.py:360
  150.0 12.0 %collective-permute-start.11 = (bf16[128,8192]{1,0:T(8,128)(2,1)}, bf16[128,8192]{1,0:T(8,128)(2,1)}, u32[]{:S(2)}, u32[]{:S(2)}) collective-permute-start(bf16[128,8192]{1,0:T(8,128)(2,1)} %collective-permute-done.3.refs_10_.refs_2_), channel_id=1, source_target_pairs={{0,8},{8,0},{1,9},{9,1},{2,10},{10,2},{3,11},{11,3},{4,12},{12,4},... | collective-permute-start | bytes 6291464 | tf_op jit(solution)/shard_map/ppermute | solution.py:360
  153.1 8.8 %collective-permute-start.5 = (bf16[8192,128]{1,0:T(8,128)(2,1)}, bf16[8192,128]{1,0:T(8,128)(2,1)}, u32[]{:S(2)}, u32[]{:S(2)}) collective-permute-start(bf16[8192,128]{1,0:T(8,128)(2,1)} %collective-permute-done.1.refs_2_), channel_id=1, source_target_pairs={{0,8},{8,0},{1,9},{9,1},{2,10},{10,2},{3,11},{11,3},{4,12},{12,4},... | collective-permute-start | bytes 6291464 | tf_op jit(solution)/shard_map/ppermute | solution.py:360
  155.1 8.2 %collective-permute-start.13 = (bf16[128,8192]{1,0:T(8,128)(2,1)}, bf16[128,8192]{1,0:T(8,128)(2,1)}, u32[]{:S(2)}, u32[]{:S(2)}) collective-permute-start(bf16[128,8192]{1,0:T(8,128)(2,1)} %collective-permute-done.refs_14_.refs_6_), channel_id=1, source_target_pairs={{0,8},{8,0},{1,9},{9,1},{2,10},{10,2},{3,11},{11,3},{4,12},{12,4},... | collective-permute-start | bytes 6291464 | tf_op jit(solution)/shard_map/ppermute | solution.py:360
  157.5 8.7 %collective-permute-start.8 = (bf16[8192,128]{1,0:T(8,128)(2,1)}, bf16[8192,128]{1,0:T(8,128)(2,1)}, u32[]{:S(2)}, u32[]{:S(2)}) collective-permute-start(bf16[8192,128]{1,0:T(8,128)(2,1)} %collective-permute-done.6.refs_4_), channel_id=1, source_target_pairs={{0,8},{8,0},{1,9},{9,1},{2,10},{10,2},{3,11},{11,3},{4,12},{12,4},... | collective-permute-start | bytes 6291464 | tf_op jit(solution)/shard_map/ppermute | solution.py:360
  159.4 9.8 %collective-permute-start.12 = (bf16[128,8192]{1,0:T(8,128)(2,1)}, bf16[128,8192]{1,0:T(8,128)(2,1)}, u32[]{:S(2)}, u32[]{:S(2)}) collective-permute-start(bf16[128,8192]{1,0:T(8,128)(2,1)} %collective-permute-done.7.refs_12_.refs_4_), channel_id=1, source_target_pairs={{0,8},{8,0},{1,9},{9,1},{2,10},{10,2},{3,11},{11,3},{4,12},{12,4},... | collective-permute-start | bytes 6291464 | tf_op jit(solution)/shard_map/ppermute | solution.py:360
  182.2 14.2 %collective-permute-start.14 = (bf16[16,8192]{1,0:T(8,128)(2,1)S(1)}, bf16[16,8192]{1,0:T(8,128)(2,1)S(1)}, u32[]{:S(2)}, u32[]{:S(2)}) collective-permute-start(bf16[16,8192]{1,0:T(8,128)(2,1)S(1)} %get-tuple-element.63.refs_8_), channel_id=1, source_target_pairs={{0,64},{1,65},{2,66},{3,67},{4,68},{5,69},{6,70},{7,71},{8,72},{9,... | collective-permute-start | bytes 786440 | tf_op jit(solution)/shard_map/ppermute | solution.py:364
  197.0 13.6 %collective-permute-start.15 = (bf16[16,8192]{1,0:T(8,128)(2,1)S(1)}, bf16[16,8192]{1,0:T(8,128)(2,1)S(1)}, u32[]{:S(2)}, u32[]{:S(2)}) collective-permute-start(bf16[16,8192]{1,0:T(8,128)(2,1)S(1)} %get-tuple-element.67.refs_8_), channel_id=1, source_target_pairs={{64,128},{65,129},{66,130},{67,131},{68,132},{69,133},{70,134},{71... | collective-permute-start | bytes 786440 | tf_op jit(solution)/shard_map/ppermute | solution.py:364
  211.3 0.7 collective-permute-start.16
  212.7 0.7 collective-permute-start.17
  214.0 0.7 collective-permute-start.18
  215.4 0.7 collective-permute-start.19
  216.8 0.7 collective-permute-start.20
  218.2 222.4 %all-to-all-start.1 = ((bf16[64,16,1152]{2,1,0:T(8,128)(2,1)}), bf16[64,16,1152]{2,1,0:T(8,128)(2,1)S(1)}, u32[]{:S(2)}, u32[]{:S(2)}) async-start(bf16[64,16,1152]{2,1,0:T(8,128)(2,1)} %bitcast.24), calls=%async_computation.1 | async-start | bytes 4718592 | tf_op jit(solution)/shard_map/all_to_all | solution.py:372
  230.5 5.8 %copy-start = (bf16[8,8192,128]{2,1,0:T(8,128)(2,1)S(1)}, bf16[8,8192,128]{2,1,0:T(8,128)(2,1)}, u32[]{:S(2)}) copy-start(bf16[8,8192,128]{2,1,0:T(8,128)(2,1)} %get-tuple-element.90.turned_out) | copy-start | bytes 50331652
  237.0 0.7 collective-permute-start.21
  238.5 0.7 collective-permute-start.22
  239.9 0.7 collective-permute-start.23
  241.4 0.7 collective-permute-start.24
  242.8 0.7 collective-permute-start.25
  244.3 0.7 collective-permute-start.26
  245.7 184.5 %collective-permute-start.27 = (bf16[16,8192]{1,0:T(8,128)(2,1)S(1)}, bf16[16,8192]{1,0:T(8,128)(2,1)S(1)}, u32[]{:S(2)}, u32[]{:S(2)}) collective-permute-start(bf16[16,8192]{1,0:T(8,128)(2,1)S(1)} %get-tuple-element.105), channel_id=1, source_target_pairs={{64,0},{65,1},{66,2},{67,3},{68,4},{69,5},{70,6},{71,7},{72,8},{73... | collective-permute-start | bytes 786440 | tf_op jit(solution)/shard_map/ppermute | solution.py:364
  440.5 72.1 %all-to-all-start.2 = ((bf16[64,16,1152]{2,1,0:T(8,128)(2,1)}), bf16[64,16,1152]{2,1,0:T(8,128)(2,1)}, u32[]{:S(2)}, u32[]{:S(2)}) async-start(bf16[64,16,1152]{2,1,0:T(8,128)(2,1)} %bitcast.25), calls=%async_computation.2 | async-start | bytes 4718592 | tf_op jit(solution)/shard_map/all_to_all | solution.py:372

commit v5 on v4

--- a/solution.py
+++ b/solution.py
@@ -47,14 +47,16 @@
 def forward_pass(refs, fetches, get_in, get_out):
     x_ref, sent_ref, stash_ref, small_ref = refs[:4]
     hidden, narrow, wide, small, out_sems = refs[4:]
-    for layer in range(AHEAD):
+    for layer in range(AHEAD if fetches else 0):
         fetches(layer)
     hidden[...] = x_ref[...].astype(f32)
 
     def step(layer, carry):
-        @pl.when(layer + AHEAD < LAYERS)
-        def _():
-            fetches(layer + AHEAD)
+        if fetches:
+
+            @pl.when(layer + AHEAD < LAYERS)
+            def _():
+                fetches(layer + AHEAD)
 
         weights = get_in(layer)
         squares = jnp.zeros((ROWS, 128), f32)
@@ -110,22 +112,31 @@
 
 
 def forward_kernel(tick, place, x_ref, held_out, *refs):
-    pieces_in, refs = refs[:8], refs[10:]
-    state, (held_in, in_sems) = refs[3:8], refs[8:]
+    if tick == EARLY:
+        pieces_in, refs = refs[:8], refs[10:]
+        state, (held_in, in_sems) = refs[3:8], refs[8:]
+    else:
+        held_in, refs = refs[0], refs[3:]
+        state = refs[3:8]
 
     @pl.when(place[0] == tick)
     def _():
+        if tick == EARLY:
+            fetches = lambda layer: fetch(place, pieces_in, held_in, in_sems, layer)
+            get_in = lambda layer: held_in.at[await_fetch(pieces_in, held_in, in_sems, layer)]
+        else:
+            fetches, get_in = None, lambda layer: held_in.at[layer]
         forward_pass(
             (x_ref,) + tuple(refs[:3]) + tuple(state),
-            lambda layer: fetch(place, pieces_in, held_in, in_sems, layer),
-            lambda layer: held_in.at[await_fetch(pieces_in, held_in, in_sems, layer)],
+            fetches,
+            get_in,
             lambda layer: held_out.at[layer],
         )
 
 
-def turn_kernel(keep, place, *refs):
+def turn_kernel(tall, place, *refs):
     pieces, refs = refs[:8], refs[9:]
-    turned, held, turn, sems, out_sems = (refs[1], refs[0], *refs[2:]) if keep else refs
+    held, turned, turn, sems, out_sems = refs
 
     def begin(layer, carry):
         fetch(place, pieces, held, sems, layer)
@@ -144,10 +155,10 @@
         await_fetch(pieces, held, sems, layer)
         for at in range(0, D, HD):
             block = slice(at, at + HD)
-            if keep:
+            if tall:
+                turn[slot, :, block] = held[layer, block, :].T
+            else:
                 turn[slot, block, :] = held[layer, :, block].T
-            else:
-                turn[slot, :, block] = held[layer, block, :].T
         copy.start()
         return carry
 
@@ -270,22 +281,22 @@
 ]
 
 
-def run_turn(keep, place, pieces, after):
-    tall, flat = (LAYERS, D, HD), (LAYERS, HD, D)
-    turned = tall if keep else flat
-    held = pltpu.VMEM(flat if keep else tall, bf16)
+def run_turn(place, pieces, after):
+    rows, columns = pieces[0].shape
     return pl.pallas_call(
-        functools.partial(turn_kernel, keep),
+        functools.partial(turn_kernel, rows > columns),
         in_specs=[SMEM] + [ANY] * 9,
-        out_specs=[VMEM, ANY] if keep else ANY,
-        out_shape=[held, pltpu.HBM(turned, bf16)] if keep else pltpu.HBM(turned, bf16),
-        scratch_shapes=([] if keep else [held])
-        + [
-            pltpu.VMEM((2,) + turned[1:], bf16),
+        out_specs=[VMEM, ANY],
+        out_shape=[
+            pltpu.VMEM((LAYERS, rows, columns), bf16),
+            pltpu.HBM((LAYERS, columns, rows), bf16),
+        ],
+        scratch_shapes=[
+            pltpu.VMEM((2, columns, rows), bf16),
             pltpu.SemaphoreType.DMA((LAYERS,)),
             pltpu.SemaphoreType.DMA((2,)),
         ],
-        compiler_params=pltpu.CompilerParams(vmem_limit_bytes=(6 if keep else 22) * 2**20),
+        compiler_params=pltpu.CompilerParams(vmem_limit_bytes=6 * 2**20),
         cost_estimate=COST,
         name="team_turn",
     )(place, *map(in_hbm, pieces), after)
@@ -312,18 +323,21 @@
     )(place, x, *map(in_hbm, pieces_in), *map(in_hbm, pieces_out), *map(in_hbm, older))
 
 
-def run_forward(tick, place, x, held_out, pieces_in, stash, small):
+def run_forward(tick, place, x, held_out, weights_in, stash, small):
+    resident = tick > EARLY
+    weights_in = [in_vmem(weights_in)] if resident else [*map(in_hbm, weights_in)]
+    count = len(weights_in)
     return pl.pallas_call(
         functools.partial(forward_kernel, tick),
-        in_specs=[SMEM, VMEM, VMEM] + [ANY] * 10,
+        in_specs=[SMEM, VMEM, VMEM] + [VMEM if resident else ANY] * count + [ANY] * 2,
         out_specs=[VMEM, ANY, ANY],
         out_shape=[SENT, STASH, SMALL],
-        input_output_aliases={11: 1, 12: 2},
-        scratch_shapes=FORWARD + STREAM_IN,
-        compiler_params=pltpu.CompilerParams(vmem_limit_bytes=14 * 2**20),
+        input_output_aliases={3 + count: 1, 4 + count: 2},
+        scratch_shapes=FORWARD + ([] if resident else STREAM_IN),
+        compiler_params=pltpu.CompilerParams(vmem_limit_bytes=(6 if resident else 14) * 2**20),
         cost_estimate=COST,
         name="team_forward",
-    )(place, x, in_vmem(held_out), *map(in_hbm, pieces_in), in_hbm(stash), in_hbm(small))
+    )(place, x, in_vmem(held_out), *weights_in, in_hbm(stash), in_hbm(small))
 
 
 def run_backward(tick, place, c, turned_out, turned_in, stash, small, cots):
@@ -400,11 +414,12 @@
             x, stash, small = run_early(tick, place, x, pieces_in, pieces_out, stash, small)
             continue
         if tick == EARLY:
-            held_out, turned_out = run_turn(True, place, pieces_out, last)
+            held_out, turned_out = run_turn(place, pieces_out, last)
+            weights_in = pieces_in
         if tick == EARLY + 1:
-            turned_in = run_turn(False, place, pieces_in, last)
+            weights_in, turned_in = run_turn(place, pieces_in, last)
             x, turned_in = lax.optimization_barrier((x, turned_in))
-        x, stash, small = run_forward(tick, place, x, held_out, pieces_in, stash, small)
+        x, stash, small = run_forward(tick, place, x, held_out, weights_in, stash, small)
     x, stash_sent = lax.optimization_barrier((x, stash))
     first = exchange(stash_sent)
     for tick in range(LAST, -1, -1):

time: 519 us -> 511 us (0.985)
  waiting for transfers between devices: 339 us -> 332 us
    ppermute x14, waiting for transfers between devices: 183 us -> 176 us  [along_y(): return lax.ppermute(value, 'y', [(source, target)])]
where the time goes in v5:
time: 511 us; the launch traced here: 510 us
  waiting for transfers between devices  332 us (65%)
  starting transfers between devices  102 us (20%)
  Pallas kernels  58.9 us (12%)
  local copies, waits for them, and re-layouts  8.56 us (2%)
  matrix products  5.2 us (1%)
    ppermute x14, waiting for transfers between devices, along_y(): return lax.ppermute(value, 'y', [(source, target)])  176 us
    ppermute x6, waiting for transfers between devices, along_z(): return lax.ppermute(value, ('zl', 'zh'), pairs)  93.3 us
    all_to_all x2, waiting for transfers between devices, exchange(): flat = lax.all_to_all(flat, PLANE, 0, 0, tiled=True)  55.6 us
    all_to_all x2, starting transfers between devices, exchange(): flat = lax.all_to_all(flat, PLANE, 0, 0, tiled=True)  28.1 us
    pallas_call x2, Pallas kernels, run_turn(): pl.pallas_call(functools.partial(turn_kernel, rows > columns), in_specs=[...  25.7 us
    ppermute x6, starting transfers between devices, along_z(): return lax.ppermute(value, ('zl', 'zh'), pairs)  25.2 us
    ppermute x8, starting transfers between devices, swap_cores(): return lax.ppermute(value, 'core', [(0, 1), (1, 0)])  24 us
    pallas_call x8, Pallas kernels, run_backward(): pl.pallas_call(functools.partial(backward_kernel, tick), in_specs=[SMEM,...  15.7 us
  transfers between devices with their start and end apart: 31, of which 8 were waited for; matrix products, arithmetic and copies ran while one was open for 0% of the time, Pallas kernels for 8%

profile of v5, /device:TPU:1, one launch (start us, length us, event | category | flops | bytes accessed | tf_op | source)
XLA Modules:
  0.0 510.2 jit_solution(979822476514422580)
XLA Ops:
  0.6 2.5 fusion.refs_0_
  3.1 4.8 collective-permute-start.2
  8.0 8.6 %collective-permute-start.3 = (bf16[128,8192]{1,0:T(8,128)(2,1)}, bf16[128,8192]{1,0:T(8,128)(2,1)}, u32[]{:S(2)}, u32[]{:S(2)}) collective-permute-start(bf16[128,8192]{1,0:T(8,128)(2,1)} %bitcast.3.refs_8_.refs_0_), channel_id=1, source_target_pairs={{0,49},{16,0},{32,16},{48,32},{1,48},{17,1},{33,17},{49,33},{2,51}... | collective-permute-start | bytes 6291464 | tf_op jit(solution)/shard_map/ppermute | solution.py:370
  16.6 3.4 collective-permute-start.1
  20.0 1.9 collective-permute-start
  21.9 38.1 %collective-permute-done.2.refs_6_ = bf16[8192,128]{1,0:T(8,128)(2,1)S(1)} collective-permute-done((bf16[8192,128]{1,0:T(8,128)(2,1)S(1)}, bf16[8192,128]{1,0:T(8,128)(2,1)S(1)}, u32[]{:S(2)}, u32[]{:S(2)}) %collective-permute-start.2) | collective-permute-done | bytes 2097184 | tf_op jit(solution)/shard_map/ppermute | solution.py:370
  60.0 1.3 copy-done.2
  61.3 0.7 broadcast_in_dim.9
  62.1 13.9 %all-to-all-start = ((bf16[64,16,128]{2,1,0:T(8,128)(2,1)}), bf16[64,16,128]{2,1,0:T(8,128)(2,1)S(1)}, u32[]{:S(2)}, u32[]{:S(2)}) async-start(bf16[64,16,128]{2,1,0:T(8,128)(2,1)} %bitcast.6), calls=%async_computation | async-start | bytes 524288 | tf_op jit(solution)/shard_map/all_to_all | solution.py:400
  76.0 3.3 collective-permute-start.6
  79.3 3.2 collective-permute-start.7
  82.5 2.9 collective-permute-start.4
  85.4 20.6 %collective-permute-done.1.refs_2_ = bf16[8192,128]{1,0:T(8,128)(2,1)} collective-permute-done((bf16[8192,128]{1,0:T(8,128)(2,1)S(1)}, bf16[8192,128]{1,0:T(8,128)(2,1)}, u32[]{:S(2)}, u32[]{:S(2)}) %collective-permute-start.1) | collective-permute-done | bytes 2097184 | tf_op jit(solution)/shard_map/ppermute | solution.py:370
  106.0 7.4 %collective-permute-start.10 = (bf16[128,8192]{1,0:T(8,128)(2,1)}, bf16[128,8192]{1,0:T(8,128)(2,1)}, u32[]{:S(2)}, u32[]{:S(2)}) collective-permute-start(bf16[128,8192]{1,0:T(8,128)(2,1)} %bitcast.3.refs_8_.refs_0_), channel_id=1, source_target_pairs={{0,8},{8,0},{1,9},{9,1},{2,10},{10,2},{3,11},{11,3},{4,12},{12,4},... | collective-permute-start | bytes 6291464 | tf_op jit(solution)/shard_map/ppermute | solution.py:374
  113.4 1.9 collective-permute-start.9
  115.4 34.6 %collective-permute-done.6.refs_4_ = bf16[8192,128]{1,0:T(8,128)(2,1)} collective-permute-done((bf16[8192,128]{1,0:T(8,128)(2,1)}, bf16[8192,128]{1,0:T(8,128)(2,1)}, u32[]{:S(2)}, u32[]{:S(2)}) %collective-permute-start.6) | collective-permute-done | bytes 2097184 | tf_op jit(solution)/shard_map/ppermute | solution.py:370
  150.0 3.1 collective-permute-start.11
  153.1 1.9 collective-permute-start.5
  155.1 2.4 collective-permute-start.13
  157.5 1.9 collective-permute-start.8
  159.4 2.4 collective-permute-start.12
  161.9 1.3 collective-permute-done.13.refs_15_.refs_7_
  163.2 3.0 collective-permute-done.8.refs_5_
  166.2 3.0 collective-permute-done.12.refs_13_.refs_5_
  169.2 12.9 %team_early.1 = (bf16[16,8192]{1,0:T(8,128)(2,1)S(1)}, bf16[8,8,16,1152]{3,2,1,0:T(8,128)(2,1)}, f32[8,2,16,128]{3,2,1,0:T(8,128)}) custom-call(s32[3]{0:T(128)S(1)} %pad_add_fusion.place, bf16[16,8192]{1,0:T(8,128)(2,1)S(1)} %copy_bitcast_fusion.x_ref, bf16[8192,128]{1,0:T(8,128)(2,1)} %copy-done.1, bf16[8192,128]{1,0:T(8,128)(2,1)} %collective-permute-done.4.refs_1_, ...), custom_call_target="tpu_custom_call" | custom-call | flops 536870912 | bytes 37748736 | tf_op jit(solution)/shard_map/team_early/pallas_call | solution.py:307
  182.2 1.3 collective-permute-start.14
  183.5 12.9 %team_turn.2 = (bf16[8,128,8192]{2,1,0:T(8,128)(2,1)S(1)}, bf16[8,8192,128]{2,1,0:T(8,128)(2,1)}) custom-call(s32[3]{0:T(128)S(1)} %pad_add_fusion.place, bf16[128,8192]{1,0:T(8,128)(2,1)} %bitcast.3.refs_8_.refs_0_, bf16[128,8192]{1,0:T(8,128)(2,1)} %collective-permute-done.10.refs_9_.refs_1_, bf16[128,8192]{1,0:T(8,128)(2,1)} %collective-permute-done.3.refs_10_.refs_2_, ...), custom_call_target="tpu_custom_call" | custom-call | flops 536870912 | bytes 37748736 | tf_op jit(solution)/shard_map/team_turn/pallas_call | solution.py:286
  196.4 0.7 team_forward.7
  197.0 0.7 collective-permute-start.15
  197.7 12.9 %team_turn.3 = (bf16[8,8192,128]{2,1,0:T(8,128)(2,1)S(1)}, bf16[8,128,8192]{2,1,0:T(8,128)(2,1)}) custom-call(s32[3]{0:T(128)S(1)} %pad_add_fusion.place, bf16[8192,128]{1,0:T(8,128)(2,1)} %copy-done.1, bf16[8192,128]{1,0:T(8,128)(2,1)} %collective-permute-done.4.refs_1_, bf16[8192,128]{1,0:T(8,128)(2,1)} %collective-permute-done.1.refs_2_, ...), custom_call_target="tpu_custom_call" | custom-call | flops 536870912 | bytes 37748736 | tf_op jit(solution)/shard_map/team_turn/pallas_call | solution.py:286
  210.6 0.6 team_forward.8
  211.2 0.7 collective-permute-start.16
  211.9 0.6 team_forward.9
  212.6 0.7 collective-permute-start.17
  213.3 0.6 team_forward.10
  213.9 0.7 collective-permute-start.18
  214.6 0.6 team_forward.11
  215.3 0.7 collective-permute-start.19
  216.0 0.6 team_forward.12
  216.6 0.7 collective-permute-start.20
  217.3 0.6 team_forward.13
  217.9 12.3 %all-to-all-start.1 = ((bf16[64,16,1152]{2,1,0:T(8,128)(2,1)}), bf16[64,16,1152]{2,1,0:T(8,128)(2,1)S(1)}, u32[]{:S(2)}, u32[]{:S(2)}) async-start(bf16[64,16,1152]{2,1,0:T(8,128)(2,1)} %bitcast.24), calls=%async_computation.1 | async-start | bytes 4718592 | tf_op jit(solution)/shard_map/all_to_all | solution.py:386
  230.3 5.8 %copy-done = bf16[8,8192,128]{2,1,0:T(8,128)(2,1)S(1)} copy-done((bf16[8,8192,128]{2,1,0:T(8,128)(2,1)S(1)}, bf16[8,8192,128]{2,1,0:T(8,128)(2,1)}, u32[]{:S(2)}) %copy-start) | copy-done | bytes 16777240
  236.1 0.9 team_backward.8
  237.0 0.7 collective-permute-start.21
  237.7 0.7 team_backward.9
  238.4 0.7 collective-permute-start.22
  239.1 0.7 team_backward.10
  239.9 0.7 collective-permute-start.23
  240.6 0.7 team_backward.11
  241.3 0.7 collective-permute-start.24
  242.0 0.7 team_backward.12
  242.8 0.7 collective-permute-start.25
  243.5 0.7 team_backward.13
  244.2 0.7 collective-permute-start.26
  244.9 0.7 team_backward.14
  245.6 1.3 collective-permute-start.27
  246.9 175.6 %collective-permute-done.27.c_ref = bf16[16,8192]{1,0:T(8,128)(2,1)S(1)} collective-permute-done((bf16[16,8192]{1,0:T(8,128)(2,1)S(1)}, bf16[16,8192]{1,0:T(8,128)(2,1)S(1)}, u32[]{:S(2)}, u32[]{:S(2)}) %collective-permute-start.27) | collective-permute-done | bytes 262176 | tf_op jit(solution)/shard_map/ppermute | solution.py:378
  422.5 10.4 %team_backward.15 = (bf16[16,8192]{1,0:T(8,128)(2,1)}, bf16[8,8,16,1152]{3,2,1,0:T(8,128)(2,1)}) custom-call(s32[3]{0:T(128)S(1)} %pad_add_fusion.place, bf16[16,8192]{1,0:T(8,128)(2,1)S(1)} %collective-permute-done.27.c_ref, bf16[8,8192,128]{2,1,0:T(8,128)(2,1)S(1)} %copy-done, ...), custom_call_target="tpu_custom_call", output_to_operand_aliasing={{1}: (6, {})} | custom-call | flops 536870912 | bytes 37748736 | tf_op jit(solution)/shard_map/team_backward/pallas_call | solution.py:345
  432.9 15.8 %all-to-all-start.2 = ((bf16[64,16,1152]{2,1,0:T(8,128)(2,1)}), bf16[64,16,1152]{2,1,0:T(8,128)(2,1)}, u32[]{:S(2)}, u32[]{:S(2)}) async-start(bf16[64,16,1152]{2,1,0:T(8,128)(2,1)} %bitcast.25), calls=%async_computation.2 | async-start | bytes 4718592 | tf_op jit(solution)/shard_map/all_to_all | solution.py:386
  448.7 0.7 constant_dynamic-slice_fusion
  449.4 55.6 %all-to-all-done.2 = bf16[64,16,1152]{2,1,0:T(8,128)(2,1)} async-done(((bf16[64,16,1152]{2,1,0:T(8,128)(2,1)}), bf16[64,16,1152]{2,1,0:T(8,128)(2,1)}, u32[]{:S(2)}, u32[]{:S(2)}) %all-to-all-start.2) | async-done | bytes 2359328 | tf_op jit(solution)/shard_map/all_to_all | solution.py:386
  505.0 2.8 fusion.20
  507.8 2.4 fusion.23
  (31 shorter events, 0.2 us)
Async XLA Ops:
  0.6 60.7 %copy-start.3 = (bf16[8,16,128]{2,1,0:T(8,128)(2,1)S(1)}, bf16[8,16,128]{2,1,0:T(8,128)(2,1)}, u32[]{:S(2)}) copy-start(bf16[8,16,128]{2,1,0:T(8,128)(2,1)} %param.4) | copy-start | bytes 98308
  3.1 166.1 %copy-start.1 = (bf16[8192,128]{1,0:T(8,128)(2,1)}, bf16[8192,128]{1,0:T(8,128)(2,1)S(1)}, u32[]{:S(2)}) copy-start(bf16[8192,128]{1,0:T(8,128)(2,1)S(1)} %fusion.refs_0_) | copy-start | bytes 6291460
  3.1 56.8 %collective-permute-start.2 = (bf16[8192,128]{1,0:T(8,128)(2,1)S(1)}, bf16[8192,128]{1,0:T(8,128)(2,1)S(1)}, u32[]{:S(2)}, u32[]{:S(2)}) collective-permute-start(bf16[8192,128]{1,0:T(8,128)(2,1)S(1)} %fusion.refs_0_), channel_id=1, source_target_pairs={{0,16},{16,32},{32,48},{48,1},{1,17},{17,33},{33,49},{49,0},{2,18}... | collective-permute-start | bytes 6291464 | tf_op jit(solution)/shard_map/ppermute | solution.py:370
  8.0 53.4 %collective-permute-start.3 = (bf16[128,8192]{1,0:T(8,128)(2,1)}, bf16[128,8192]{1,0:T(8,128)(2,1)}, u32[]{:S(2)}, u32[]{:S(2)}) collective-permute-start(bf16[128,8192]{1,0:T(8,128)(2,1)} %bitcast.3.refs_8_.refs_0_), channel_id=1, source_target_pairs={{0,49},{16,0},{32,16},{48,32},{1,48},{17,1},{33,17},{49,33},{2,51}... | collective-permute-start | bytes 6291464 | tf_op jit(solution)/shard_map/ppermute | solution.py:370
  16.6 89.4 %collective-permute-start.1 = (bf16[8192,128]{1,0:T(8,128)(2,1)S(1)}, bf16[8192,128]{1,0:T(8,128)(2,1)}, u32[]{:S(2)}, u32[]{:S(2)}) collective-permute-start(bf16[8192,128]{1,0:T(8,128)(2,1)S(1)} %fusion.refs_0_), channel_id=1, source_target_pairs={{0,49},{16,0},{32,16},{48,32},{1,48},{17,1},{33,17},{49,33},{2,51}... | collective-permute-start | bytes 6291464 | tf_op jit(solution)/shard_map/ppermute | solution.py:370
  20.0 93.4 %collective-permute-start = (bf16[128,8192]{1,0:T(8,128)(2,1)}, bf16[128,8192]{1,0:T(8,128)(2,1)}, u32[]{:S(2)}, u32[]{:S(2)}) collective-permute-start(bf16[128,8192]{1,0:T(8,128)(2,1)} %bitcast.3.refs_8_.refs_0_), channel_id=1, source_target_pairs={{0,16},{16,32},{32,48},{48,1},{1,17},{17,33},{33,49},{49,0},{2,18}... | collective-permute-start | bytes 6291464 | tf_op jit(solution)/shard_map/ppermute | solution.py:370
  60.0 1.3 copy-start.2
  62.1 53.3 %all-to-all-start = ((bf16[64,16,128]{2,1,0:T(8,128)(2,1)}), bf16[64,16,128]{2,1,0:T(8,128)(2,1)S(1)}, u32[]{:S(2)}, u32[]{:S(2)}) async-start(bf16[64,16,128]{2,1,0:T(8,128)(2,1)} %bitcast.6), calls=%async_computation | async-start | bytes 524288 | tf_op jit(solution)/shard_map/all_to_all | solution.py:400
  76.0 74.0 %collective-permute-start.6 = (bf16[8192,128]{1,0:T(8,128)(2,1)}, bf16[8192,128]{1,0:T(8,128)(2,1)}, u32[]{:S(2)}, u32[]{:S(2)}) collective-permute-start(bf16[8192,128]{1,0:T(8,128)(2,1)} %copy-done.2), channel_id=1, source_target_pairs={{0,16},{16,32},{32,48},{48,1},{1,17},{17,33},{33,49},{49,0},{2,18}... | collective-permute-start | bytes 6291464 | tf_op jit(solution)/shard_map/ppermute | solution.py:370
  79.3 73.9 %collective-permute-start.7 = (bf16[128,8192]{1,0:T(8,128)(2,1)}, bf16[128,8192]{1,0:T(8,128)(2,1)}, u32[]{:S(2)}, u32[]{:S(2)}) collective-permute-start(bf16[128,8192]{1,0:T(8,128)(2,1)} %collective-permute-done.3.refs_10_.refs_2_), channel_id=1, source_target_pairs={{0,49},{16,0},{32,16},{48,32},{1,48},{17,1},{33,17},{49,33},{2,51}... | collective-permute-start | bytes 6291464 | tf_op jit(solution)/shard_map/ppermute | solution.py:370
  82.5 72.6 %collective-permute-start.4 = (bf16[8192,128]{1,0:T(8,128)(2,1)S(1)}, bf16[8192,128]{1,0:T(8,128)(2,1)}, u32[]{:S(2)}, u32[]{:S(2)}) collective-permute-start(bf16[8192,128]{1,0:T(8,128)(2,1)S(1)} %fusion.refs_0_), channel_id=1, source_target_pairs={{0,8},{8,0},{1,9},{9,1},{2,10},{10,2},{3,11},{11,3},{4,12},{12,4},... | collective-permute-start | bytes 6291464 | tf_op jit(solution)/shard_map/ppermute | solution.py:374
  106.0 51.5 %collective-permute-start.10 = (bf16[128,8192]{1,0:T(8,128)(2,1)}, bf16[128,8192]{1,0:T(8,128)(2,1)}, u32[]{:S(2)}, u32[]{:S(2)}) collective-permute-start(bf16[128,8192]{1,0:T(8,128)(2,1)} %bitcast.3.refs_8_.refs_0_), channel_id=1, source_target_pairs={{0,8},{8,0},{1,9},{9,1},{2,10},{10,2},{3,11},{11,3},{4,12},{12,4},... | collective-permute-start | bytes 6291464 | tf_op jit(solution)/shard_map/ppermute | solution.py:374
  113.4 46.0 %collective-permute-start.9 = (bf16[8192,128]{1,0:T(8,128)(2,1)}, bf16[8192,128]{1,0:T(8,128)(2,1)}, u32[]{:S(2)}, u32[]{:S(2)}) collective-permute-start(bf16[8192,128]{1,0:T(8,128)(2,1)} %copy-done.2), channel_id=1, source_target_pairs={{0,8},{8,0},{1,9},{9,1},{2,10},{10,2},{3,11},{11,3},{4,12},{12,4},... | collective-permute-start | bytes 6291464 | tf_op jit(solution)/shard_map/ppermute | solution.py:374
  150.0 12.0 %collective-permute-start.11 = (bf16[128,8192]{1,0:T(8,128)(2,1)}, bf16[128,8192]{1,0:T(8,128)(2,1)}, u32[]{:S(2)}, u32[]{:S(2)}) collective-permute-start(bf16[128,8192]{1,0:T(8,128)(2,1)} %collective-permute-done.3.refs_10_.refs_2_), channel_id=1, source_target_pairs={{0,8},{8,0},{1,9},{9,1},{2,10},{10,2},{3,11},{11,3},{4,12},{12,4},... | collective-permute-start | bytes 6291464 | tf_op jit(solution)/shard_map/ppermute | solution.py:374
  153.1 8.8 %collective-permute-start.5 = (bf16[8192,128]{1,0:T(8,128)(2,1)}, bf16[8192,128]{1,0:T(8,128)(2,1)}, u32[]{:S(2)}, u32[]{:S(2)}) collective-permute-start(bf16[8192,128]{1,0:T(8,128)(2,1)} %collective-permute-done.1.refs_2_), channel_id=1, source_target_pairs={{0,8},{8,0},{1,9},{9,1},{2,10},{10,2},{3,11},{11,3},{4,12},{12,4},... | collective-permute-start | bytes 6291464 | tf_op jit(solution)/shard_map/ppermute | solution.py:374
  155.1 8.2 %collective-permute-start.13 = (bf16[128,8192]{1,0:T(8,128)(2,1)}, bf16[128,8192]{1,0:T(8,128)(2,1)}, u32[]{:S(2)}, u32[]{:S(2)}) collective-permute-start(bf16[128,8192]{1,0:T(8,128)(2,1)} %collective-permute-done.refs_14_.refs_6_), channel_id=1, source_target_pairs={{0,8},{8,0},{1,9},{9,1},{2,10},{10,2},{3,11},{11,3},{4,12},{12,4},... | collective-permute-start | bytes 6291464 | tf_op jit(solution)/shard_map/ppermute | solution.py:374
  157.5 8.7 %collective-permute-start.8 = (bf16[8192,128]{1,0:T(8,128)(2,1)}, bf16[8192,128]{1,0:T(8,128)(2,1)}, u32[]{:S(2)}, u32[]{:S(2)}) collective-permute-start(bf16[8192,128]{1,0:T(8,128)(2,1)} %collective-permute-done.6.refs_4_), channel_id=1, source_target_pairs={{0,8},{8,0},{1,9},{9,1},{2,10},{10,2},{3,11},{11,3},{4,12},{12,4},... | collective-permute-start | bytes 6291464 | tf_op jit(solution)/shard_map/ppermute | solution.py:374
  159.4 9.8 %collective-permute-start.12 = (bf16[128,8192]{1,0:T(8,128)(2,1)}, bf16[128,8192]{1,0:T(8,128)(2,1)}, u32[]{:S(2)}, u32[]{:S(2)}) collective-permute-start(bf16[128,8192]{1,0:T(8,128)(2,1)} %collective-permute-done.7.refs_12_.refs_4_), channel_id=1, source_target_pairs={{0,8},{8,0},{1,9},{9,1},{2,10},{10,2},{3,11},{11,3},{4,12},{12,4},... | collective-permute-start | bytes 6291464 | tf_op jit(solution)/shard_map/ppermute | solution.py:374
  182.2 14.2 %collective-permute-start.14 = (bf16[16,8192]{1,0:T(8,128)(2,1)S(1)}, bf16[16,8192]{1,0:T(8,128)(2,1)S(1)}, u32[]{:S(2)}, u32[]{:S(2)}) collective-permute-start(bf16[16,8192]{1,0:T(8,128)(2,1)S(1)} %get-tuple-element.65.refs_8_), channel_id=1, source_target_pairs={{0,64},{1,65},{2,66},{3,67},{4,68},{5,69},{6,70},{7,71},{8,72},{9,... | collective-permute-start | bytes 786440 | tf_op jit(solution)/shard_map/ppermute | solution.py:378
  197.0 13.6 %collective-permute-start.15 = (bf16[16,8192]{1,0:T(8,128)(2,1)S(1)}, bf16[16,8192]{1,0:T(8,128)(2,1)S(1)}, u32[]{:S(2)}, u32[]{:S(2)}) collective-permute-start(bf16[16,8192]{1,0:T(8,128)(2,1)S(1)} %get-tuple-element.69.refs_8_), channel_id=1, source_target_pairs={{64,128},{65,129},{66,130},{67,131},{68,132},{69,133},{70,134},{71... | collective-permute-start | bytes 786440 | tf_op jit(solution)/shard_map/ppermute | solution.py:378
  211.2 0.7 collective-permute-start.16
  212.6 0.7 collective-permute-start.17
  213.9 0.7 collective-permute-start.18
  215.3 0.7 collective-permute-start.19
  216.6 0.7 collective-permute-start.20
  217.9 215.0 %all-to-all-start.1 = ((bf16[64,16,1152]{2,1,0:T(8,128)(2,1)}), bf16[64,16,1152]{2,1,0:T(8,128)(2,1)S(1)}, u32[]{:S(2)}, u32[]{:S(2)}) async-start(bf16[64,16,1152]{2,1,0:T(8,128)(2,1)} %bitcast.24), calls=%async_computation.1 | async-start | bytes 4718592 | tf_op jit(solution)/shard_map/all_to_all | solution.py:386
  230.3 5.8 %copy-start = (bf16[8,8192,128]{2,1,0:T(8,128)(2,1)S(1)}, bf16[8,8192,128]{2,1,0:T(8,128)(2,1)}, u32[]{:S(2)}) copy-start(bf16[8,8192,128]{2,1,0:T(8,128)(2,1)} %get-tuple-element.94.turned_out) | copy-start | bytes 50331652
  237.0 0.7 collective-permute-start.21
  238.4 0.7 collective-permute-start.22
  239.9 0.7 collective-permute-start.23
  241.3 0.7 collective-permute-start.24
  242.8 0.7 collective-permute-start.25
  244.2 0.7 collective-permute-start.26
  245.6 176.9 %collective-permute-start.27 = (bf16[16,8192]{1,0:T(8,128)(2,1)S(1)}, bf16[16,8192]{1,0:T(8,128)(2,1)S(1)}, u32[]{:S(2)}, u32[]{:S(2)}) collective-permute-start(bf16[16,8192]{1,0:T(8,128)(2,1)S(1)} %get-tuple-element.109), channel_id=1, source_target_pairs={{64,0},{65,1},{66,2},{67,3},{68,4},{69,5},{70,6},{71,7},{72,8},{73... | collective-permute-start | bytes 786440 | tf_op jit(solution)/shard_map/ppermute | solution.py:378
  432.9 72.1 %all-to-all-start.2 = ((bf16[64,16,1152]{2,1,0:T(8,128)(2,1)}), bf16[64,16,1152]{2,1,0:T(8,128)(2,1)}, u32[]{:S(2)}, u32[]{:S(2)}) async-start(bf16[64,16,1152]{2,1,0:T(8,128)(2,1)} %bitcast.25), calls=%async_computation.2 | async-start | bytes 4718592 | tf_op jit(solution)/shard_map/all_to_all | solution.py:386

commit v6 on v5

--- a/solution.py
+++ b/solution.py
@@ -199,14 +199,20 @@
     stash_ref, small_in = refs[:2]
     refs = refs[2:] if tick == LAST else refs[3:]
     sent_ref, stash_out = refs[:2]
-    (cotangent, rounded, stash, wide, small, in_sems, out_sems, second, sems) = refs[2:]
+    (cotangent, rounded, stash, wide, small, in_sems, out_sems, second, sems, *extra) = refs[2:]
     common = (
         stash_ref, stash_out, cotangent, rounded, stash, wide, small, in_sems, out_sems,
     )
 
     def fetch_turned(layer):
         slot = lax.rem(layer, SLOTS)
-        return pltpu.make_async_copy(turned_in.at[layer], second.at[slot], sems.at[slot])
+        copies = [pltpu.make_async_copy(turned_in.at[layer], second.at[slot], sems.at[slot])]
+        if extra:
+            first, first_sems = extra
+            copies = [
+                pltpu.make_async_copy(turned_out.at[layer], first.at[slot], first_sems.at[slot])
+            ] + copies
+        return copies
 
     @pl.when(place[0] == tick)
     def _():
@@ -219,7 +225,8 @@
 
             @pl.when(back < AHEAD)
             def _():
-                fetch_turned(layer).start()
+                for copy in fetch_turned(layer):
+                    copy.start()
 
             return carry
 
@@ -233,12 +240,17 @@
 
             @pl.when(layer >= AHEAD)
             def _():
-                fetch_turned(layer - AHEAD).start()
-
-            fetch_turned(layer).wait()
+                for copy in fetch_turned(layer - AHEAD):
+                    copy.start()
+
+            for copy in fetch_turned(layer):
+                copy.wait()
             pltpu.make_async_copy(stash_ref.at[layer], stash.at[layer], in_sems.at[layer]).wait()
             backward_layer(
-                layer, common, lambda: turned_out[layer], lambda lanes: second[slot, :, lanes]
+                layer,
+                common,
+                lambda: extra[0][slot] if extra else turned_out[layer],
+                lambda lanes: second[slot, :, lanes],
             )
             return carry
 
@@ -342,9 +354,11 @@
 
 def run_backward(tick, place, c, turned_out, turned_in, stash, small, cots):
     older = [] if cots is None else [cots]
+    streams = tick == LAST
+    turned_out = in_hbm(turned_out) if streams else in_vmem(turned_out)
     return pl.pallas_call(
         functools.partial(backward_kernel, tick),
-        in_specs=[SMEM, VMEM, VMEM] + [ANY] * (3 + len(older)),
+        in_specs=[SMEM, VMEM, ANY if streams else VMEM] + [ANY] * (3 + len(older)),
         out_specs=[VMEM, ANY],
         out_shape=[SENT, STASH],
         input_output_aliases={6: 1} if older else {},
@@ -357,11 +371,12 @@
             pltpu.SemaphoreType.DMA((LAYERS,)),
             pltpu.VMEM((SLOTS, HD, D), bf16),
             pltpu.SemaphoreType.DMA((SLOTS,)),
-        ],
-        compiler_params=pltpu.CompilerParams(vmem_limit_bytes=16 * 2**20),
+        ]
+        + (STREAM_IN if streams else []),
+        compiler_params=pltpu.CompilerParams(vmem_limit_bytes=(24 if streams else 16) * 2**20),
         cost_estimate=COST,
         name="team_backward",
-    )(place, c, in_vmem(turned_out), *map(in_hbm, [turned_in, stash, small, *older]))
+    )(place, c, turned_out, *map(in_hbm, [turned_in, stash, small, *older]))
 
 
 def along_z(value, steps):

time: 511 us -> 511 us (level)
  no operation moved by 1% of the time
where the time goes in v6:
time: 511 us; the launch traced here: 510 us
  waiting for transfers between devices  333 us (65%)
  starting transfers between devices  102 us (20%)
  Pallas kernels  58.9 us (12%)
  local copies, waits for them, and re-layouts  6.85 us (1%)
  matrix products  5.2 us (1%)
    ppermute x14, waiting for transfers between devices, along_y(): return lax.ppermute(value, 'y', [(source, target)])  177 us
    ppermute x6, waiting for transfers between devices, along_z(): return lax.ppermute(value, ('zl', 'zh'), pairs)  93.3 us
    all_to_all x2, waiting for transfers between devices, exchange(): flat = lax.all_to_all(flat, PLANE, 0, 0, tiled=True)  55.6 us
    all_to_all x2, starting transfers between devices, exchange(): flat = lax.all_to_all(flat, PLANE, 0, 0, tiled=True)  28.1 us
    pallas_call x2, Pallas kernels, run_turn(): pl.pallas_call(functools.partial(turn_kernel, rows > columns), in_specs=[...  25.7 us
    ppermute x6, starting transfers between devices, along_z(): return lax.ppermute(value, ('zl', 'zh'), pairs)  25.2 us
    ppermute x8, starting transfers between devices, swap_cores(): return lax.ppermute(value, 'core', [(0, 1), (1, 0)])  24 us
    pallas_call x8, Pallas kernels, run_backward(): pl.pallas_call(functools.partial(backward_kernel, tick), in_specs=[SMEM,...  15.8 us
  transfers between devices with their start and end apart: 31, of which 8 were waited for; matrix products, arithmetic and copies ran while one was open for 0% of the time, Pallas kernels for 8%

profile of v6, /device:TPU:1, one launch (start us, length us, event | category | flops | bytes accessed | tf_op | source)
XLA Modules:
  0.0 509.6 jit_solution(3259513474245206086)
XLA Ops:
  0.6 2.5 fusion.refs_0_
  3.1 4.8 collective-permute-start.2
  8.0 8.6 %collective-permute-start.3 = (bf16[128,8192]{1,0:T(8,128)(2,1)}, bf16[128,8192]{1,0:T(8,128)(2,1)}, u32[]{:S(2)}, u32[]{:S(2)}) collective-permute-start(bf16[128,8192]{1,0:T(8,128)(2,1)} %bitcast.3.refs_8_.refs_0_), channel_id=1, source_target_pairs={{0,49},{16,0},{32,16},{48,32},{1,48},{17,1},{33,17},{49,33},{2,51}... | collective-permute-start | bytes 6291464 | tf_op jit(solution)/shard_map/ppermute | solution.py:385
  16.6 3.4 collective-permute-start.1
  20.0 1.9 collective-permute-start
  21.9 38.1 %collective-permute-done.2.refs_6_ = bf16[8192,128]{1,0:T(8,128)(2,1)S(1)} collective-permute-done((bf16[8192,128]{1,0:T(8,128)(2,1)S(1)}, bf16[8192,128]{1,0:T(8,128)(2,1)S(1)}, u32[]{:S(2)}, u32[]{:S(2)}) %collective-permute-start.2) | collective-permute-done | bytes 2097184 | tf_op jit(solution)/shard_map/ppermute | solution.py:385
  60.0 1.4 copy-done.1
  61.3 0.7 broadcast_in_dim.9
  62.1 13.9 %all-to-all-start = ((bf16[64,16,128]{2,1,0:T(8,128)(2,1)}), bf16[64,16,128]{2,1,0:T(8,128)(2,1)S(1)}, u32[]{:S(2)}, u32[]{:S(2)}) async-start(bf16[64,16,128]{2,1,0:T(8,128)(2,1)} %bitcast.6), calls=%async_computation | async-start | bytes 524288 | tf_op jit(solution)/shard_map/all_to_all | solution.py:415
  76.0 3.3 collective-permute-start.6
  79.3 3.2 collective-permute-start.7
  82.5 2.9 collective-permute-start.4
  85.4 20.6 %collective-permute-done.1.refs_2_ = bf16[8192,128]{1,0:T(8,128)(2,1)} collective-permute-done((bf16[8192,128]{1,0:T(8,128)(2,1)S(1)}, bf16[8192,128]{1,0:T(8,128)(2,1)}, u32[]{:S(2)}, u32[]{:S(2)}) %collective-permute-start.1) | collective-permute-done | bytes 2097184 | tf_op jit(solution)/shard_map/ppermute | solution.py:385
  106.0 7.4 %collective-permute-start.10 = (bf16[128,8192]{1,0:T(8,128)(2,1)}, bf16[128,8192]{1,0:T(8,128)(2,1)}, u32[]{:S(2)}, u32[]{:S(2)}) collective-permute-start(bf16[128,8192]{1,0:T(8,128)(2,1)} %bitcast.3.refs_8_.refs_0_), channel_id=1, source_target_pairs={{0,8},{8,0},{1,9},{9,1},{2,10},{10,2},{3,11},{11,3},{4,12},{12,4},... | collective-permute-start | bytes 6291464 | tf_op jit(solution)/shard_map/ppermute | solution.py:389
  113.4 1.9 collective-permute-start.9
  115.4 34.6 %collective-permute-done.6.refs_4_ = bf16[8192,128]{1,0:T(8,128)(2,1)} collective-permute-done((bf16[8192,128]{1,0:T(8,128)(2,1)}, bf16[8192,128]{1,0:T(8,128)(2,1)}, u32[]{:S(2)}, u32[]{:S(2)}) %collective-permute-start.6) | collective-permute-done | bytes 2097184 | tf_op jit(solution)/shard_map/ppermute | solution.py:385
  150.0 3.1 collective-permute-start.11
  153.1 1.9 collective-permute-start.5
  155.1 2.4 collective-permute-start.13
  157.5 1.9 collective-permute-start.8
  159.4 2.4 collective-permute-start.12
  161.9 1.3 collective-permute-done.13.refs_15_.refs_7_
  163.2 3.0 collective-permute-done.8.refs_5_
  166.2 3.0 collective-permute-done.12.refs_13_.refs_5_
  169.2 12.9 %team_early.1 = (bf16[16,8192]{1,0:T(8,128)(2,1)S(1)}, bf16[8,8,16,1152]{3,2,1,0:T(8,128)(2,1)}, f32[8,2,16,128]{3,2,1,0:T(8,128)}) custom-call(s32[3]{0:T(128)S(1)} %pad_add_fusion.place, bf16[16,8192]{1,0:T(8,128)(2,1)S(1)} %copy_bitcast_fusion.x_ref, bf16[8192,128]{1,0:T(8,128)(2,1)} %copy-done, bf16[8192,128]{1,0:T(8,128)(2,1)} %collective-permute-done.4.refs_1_, ...), custom_call_target="tpu_custom_call" | custom-call | flops 536870912 | bytes 37748736 | tf_op jit(solution)/shard_map/team_early/pallas_call | solution.py:319
  182.2 1.3 collective-permute-start.14
  183.5 12.9 %team_turn.2 = (bf16[8,128,8192]{2,1,0:T(8,128)(2,1)S(1)}, bf16[8,8192,128]{2,1,0:T(8,128)(2,1)}) custom-call(s32[3]{0:T(128)S(1)} %pad_add_fusion.place, bf16[128,8192]{1,0:T(8,128)(2,1)} %bitcast.3.refs_8_.refs_0_, bf16[128,8192]{1,0:T(8,128)(2,1)} %collective-permute-done.10.refs_9_.refs_1_, bf16[128,8192]{1,0:T(8,128)(2,1)} %collective-permute-done.3.refs_10_.refs_2_, ...), custom_call_target="tpu_custom_call" | custom-call | flops 536870912 | bytes 37748736 | tf_op jit(solution)/shard_map/team_turn/pallas_call | solution.py:298
  196.4 0.7 team_forward.7
  197.0 0.7 collective-permute-start.15
  197.7 12.9 %team_turn.3 = (bf16[8,8192,128]{2,1,0:T(8,128)(2,1)S(1)}, bf16[8,128,8192]{2,1,0:T(8,128)(2,1)}) custom-call(s32[3]{0:T(128)S(1)} %pad_add_fusion.place, bf16[8192,128]{1,0:T(8,128)(2,1)} %copy-done, bf16[8192,128]{1,0:T(8,128)(2,1)} %collective-permute-done.4.refs_1_, bf16[8192,128]{1,0:T(8,128)(2,1)} %collective-permute-done.1.refs_2_, ...), custom_call_target="tpu_custom_call" | custom-call | flops 536870912 | bytes 37748736 | tf_op jit(solution)/shard_map/team_turn/pallas_call | solution.py:298
  210.6 0.6 team_forward.8
  211.3 0.7 collective-permute-start.16
  211.9 0.6 team_forward.9
  212.6 0.7 collective-permute-start.17
  213.3 0.6 team_forward.10
  213.9 0.7 collective-permute-start.18
  215.3 0.7 collective-permute-start.19
  216.6 0.7 collective-permute-start.20
  217.3 0.6 team_forward.13
  217.9 12.3 %all-to-all-start.1 = ((bf16[64,16,1152]{2,1,0:T(8,128)(2,1)}), bf16[64,16,1152]{2,1,0:T(8,128)(2,1)S(1)}, u32[]{:S(2)}, u32[]{:S(2)}) async-start(bf16[64,16,1152]{2,1,0:T(8,128)(2,1)} %bitcast.26), calls=%async_computation.1 | async-start | bytes 4718592 | tf_op jit(solution)/shard_map/all_to_all | solution.py:401
  230.3 1.0 team_backward.8
  231.3 0.8 collective-permute-start.21
  232.5 1.3 slice-done.1
  233.8 1.2 slice-done.2
  235.0 1.2 slice-done.3
  236.2 0.7 team_backward.9
  236.9 0.7 collective-permute-start.22
  237.6 0.7 team_backward.10
  238.3 0.7 collective-permute-start.23
  239.0 0.7 team_backward.11
  239.8 0.7 collective-permute-start.24
  240.5 0.7 team_backward.12
  241.2 0.7 collective-permute-start.25
  241.9 0.7 team_backward.13
  242.7 0.7 collective-permute-start.26
  243.4 0.7 team_backward.14
  244.1 1.3 collective-permute-start.27
  245.4 176.5 %collective-permute-done.27.c_ref = bf16[16,8192]{1,0:T(8,128)(2,1)S(1)} collective-permute-done((bf16[16,8192]{1,0:T(8,128)(2,1)S(1)}, bf16[16,8192]{1,0:T(8,128)(2,1)S(1)}, u32[]{:S(2)}, u32[]{:S(2)}) %collective-permute-start.27) | collective-permute-done | bytes 262176 | tf_op jit(solution)/shard_map/ppermute | solution.py:393
  421.9 10.4 %team_backward.15 = (bf16[16,8192]{1,0:T(8,128)(2,1)}, bf16[8,8,16,1152]{3,2,1,0:T(8,128)(2,1)}) custom-call(s32[3]{0:T(128)S(1)} %pad_add_fusion.place, bf16[16,8192]{1,0:T(8,128)(2,1)S(1)} %collective-permute-done.27.c_ref, bf16[8,8192,128]{2,1,0:T(8,128)(2,1)S(1)} %bitcast.25, ...), custom_call_target="tpu_custom_call", output_to_operand_aliasing={{1}: (6, {})} | custom-call | flops 536870912 | bytes 37748736 | tf_op jit(solution)/shard_map/team_backward/pallas_call | solution.py:359
  432.3 15.8 %all-to-all-start.2 = ((bf16[64,16,1152]{2,1,0:T(8,128)(2,1)}), bf16[64,16,1152]{2,1,0:T(8,128)(2,1)}, u32[]{:S(2)}, u32[]{:S(2)}) async-start(bf16[64,16,1152]{2,1,0:T(8,128)(2,1)} %bitcast.27), calls=%async_computation.2 | async-start | bytes 4718592 | tf_op jit(solution)/shard_map/all_to_all | solution.py:401
  448.2 0.7 constant_dynamic-slice_fusion
  448.8 55.6 %all-to-all-done.2 = bf16[64,16,1152]{2,1,0:T(8,128)(2,1)} async-done(((bf16[64,16,1152]{2,1,0:T(8,128)(2,1)}), bf16[64,16,1152]{2,1,0:T(8,128)(2,1)}, u32[]{:S(2)}, u32[]{:S(2)}) %all-to-all-start.2) | async-done | bytes 2359328 | tf_op jit(solution)/shard_map/all_to_all | solution.py:401
  504.4 2.8 fusion.20
  507.2 2.4 fusion.23
  (38 shorter events, 1.8 us)
Async XLA Ops:
  0.6 60.7 %copy-start.2 = (bf16[8,16,128]{2,1,0:T(8,128)(2,1)S(1)}, bf16[8,16,128]{2,1,0:T(8,128)(2,1)}, u32[]{:S(2)}) copy-start(bf16[8,16,128]{2,1,0:T(8,128)(2,1)} %param.4) | copy-start | bytes 98308
  3.1 166.1 %copy-start = (bf16[8192,128]{1,0:T(8,128)(2,1)}, bf16[8192,128]{1,0:T(8,128)(2,1)S(1)}, u32[]{:S(2)}) copy-start(bf16[8192,128]{1,0:T(8,128)(2,1)S(1)} %fusion.refs_0_) | copy-start | bytes 6291460
  3.1 56.8 %collective-permute-start.2 = (bf16[8192,128]{1,0:T(8,128)(2,1)S(1)}, bf16[8192,128]{1,0:T(8,128)(2,1)S(1)}, u32[]{:S(2)}, u32[]{:S(2)}) collective-permute-start(bf16[8192,128]{1,0:T(8,128)(2,1)S(1)} %fusion.refs_0_), channel_id=1, source_target_pairs={{0,16},{16,32},{32,48},{48,1},{1,17},{17,33},{33,49},{49,0},{2,18}... | collective-permute-start | bytes 6291464 | tf_op jit(solution)/shard_map/ppermute | solution.py:385
  8.0 53.4 %collective-permute-start.3 = (bf16[128,8192]{1,0:T(8,128)(2,1)}, bf16[128,8192]{1,0:T(8,128)(2,1)}, u32[]{:S(2)}, u32[]{:S(2)}) collective-permute-start(bf16[128,8192]{1,0:T(8,128)(2,1)} %bitcast.3.refs_8_.refs_0_), channel_id=1, source_target_pairs={{0,49},{16,0},{32,16},{48,32},{1,48},{17,1},{33,17},{49,33},{2,51}... | collective-permute-start | bytes 6291464 | tf_op jit(solution)/shard_map/ppermute | solution.py:385
  16.6 89.4 %collective-permute-start.1 = (bf16[8192,128]{1,0:T(8,128)(2,1)S(1)}, bf16[8192,128]{1,0:T(8,128)(2,1)}, u32[]{:S(2)}, u32[]{:S(2)}) collective-permute-start(bf16[8192,128]{1,0:T(8,128)(2,1)S(1)} %fusion.refs_0_), channel_id=1, source_target_pairs={{0,49},{16,0},{32,16},{48,32},{1,48},{17,1},{33,17},{49,33},{2,51}... | collective-permute-start | bytes 6291464 | tf_op jit(solution)/shard_map/ppermute | solution.py:385
  20.0 93.4 %collective-permute-start = (bf16[128,8192]{1,0:T(8,128)(2,1)}, bf16[128,8192]{1,0:T(8,128)(2,1)}, u32[]{:S(2)}, u32[]{:S(2)}) collective-permute-start(bf16[128,8192]{1,0:T(8,128)(2,1)} %bitcast.3.refs_8_.refs_0_), channel_id=1, source_target_pairs={{0,16},{16,32},{32,48},{48,1},{1,17},{17,33},{33,49},{49,0},{2,18}... | collective-permute-start | bytes 6291464 | tf_op jit(solution)/shard_map/ppermute | solution.py:385
  60.0 1.4 copy-start.1
  62.1 53.3 %all-to-all-start = ((bf16[64,16,128]{2,1,0:T(8,128)(2,1)}), bf16[64,16,128]{2,1,0:T(8,128)(2,1)S(1)}, u32[]{:S(2)}, u32[]{:S(2)}) async-start(bf16[64,16,128]{2,1,0:T(8,128)(2,1)} %bitcast.6), calls=%async_computation | async-start | bytes 524288 | tf_op jit(solution)/shard_map/all_to_all | solution.py:415
  76.0 74.0 %collective-permute-start.6 = (bf16[8192,128]{1,0:T(8,128)(2,1)}, bf16[8192,128]{1,0:T(8,128)(2,1)}, u32[]{:S(2)}, u32[]{:S(2)}) collective-permute-start(bf16[8192,128]{1,0:T(8,128)(2,1)} %copy-done.1), channel_id=1, source_target_pairs={{0,16},{16,32},{32,48},{48,1},{1,17},{17,33},{33,49},{49,0},{2,18}... | collective-permute-start | bytes 6291464 | tf_op jit(solution)/shard_map/ppermute | solution.py:385
  79.3 73.9 %collective-permute-start.7 = (bf16[128,8192]{1,0:T(8,128)(2,1)}, bf16[128,8192]{1,0:T(8,128)(2,1)}, u32[]{:S(2)}, u32[]{:S(2)}) collective-permute-start(bf16[128,8192]{1,0:T(8,128)(2,1)} %collective-permute-done.3.refs_10_.refs_2_), channel_id=1, source_target_pairs={{0,49},{16,0},{32,16},{48,32},{1,48},{17,1},{33,17},{49,33},{2,51}... | collective-permute-start | bytes 6291464 | tf_op jit(solution)/shard_map/ppermute | solution.py:385
  82.5 72.6 %collective-permute-start.4 = (bf16[8192,128]{1,0:T(8,128)(2,1)S(1)}, bf16[8192,128]{1,0:T(8,128)(2,1)}, u32[]{:S(2)}, u32[]{:S(2)}) collective-permute-start(bf16[8192,128]{1,0:T(8,128)(2,1)S(1)} %fusion.refs_0_), channel_id=1, source_target_pairs={{0,8},{8,0},{1,9},{9,1},{2,10},{10,2},{3,11},{11,3},{4,12},{12,4},... | collective-permute-start | bytes 6291464 | tf_op jit(solution)/shard_map/ppermute | solution.py:389
  106.0 51.5 %collective-permute-start.10 = (bf16[128,8192]{1,0:T(8,128)(2,1)}, bf16[128,8192]{1,0:T(8,128)(2,1)}, u32[]{:S(2)}, u32[]{:S(2)}) collective-permute-start(bf16[128,8192]{1,0:T(8,128)(2,1)} %bitcast.3.refs_8_.refs_0_), channel_id=1, source_target_pairs={{0,8},{8,0},{1,9},{9,1},{2,10},{10,2},{3,11},{11,3},{4,12},{12,4},... | collective-permute-start | bytes 6291464 | tf_op jit(solution)/shard_map/ppermute | solution.py:389
  113.4 46.0 %collective-permute-start.9 = (bf16[8192,128]{1,0:T(8,128)(2,1)}, bf16[8192,128]{1,0:T(8,128)(2,1)}, u32[]{:S(2)}, u32[]{:S(2)}) collective-permute-start(bf16[8192,128]{1,0:T(8,128)(2,1)} %copy-done.1), channel_id=1, source_target_pairs={{0,8},{8,0},{1,9},{9,1},{2,10},{10,2},{3,11},{11,3},{4,12},{12,4},... | collective-permute-start | bytes 6291464 | tf_op jit(solution)/shard_map/ppermute | solution.py:389
  150.0 12.0 %collective-permute-start.11 = (bf16[128,8192]{1,0:T(8,128)(2,1)}, bf16[128,8192]{1,0:T(8,128)(2,1)}, u32[]{:S(2)}, u32[]{:S(2)}) collective-permute-start(bf16[128,8192]{1,0:T(8,128)(2,1)} %collective-permute-done.3.refs_10_.refs_2_), channel_id=1, source_target_pairs={{0,8},{8,0},{1,9},{9,1},{2,10},{10,2},{3,11},{11,3},{4,12},{12,4},... | collective-permute-start | bytes 6291464 | tf_op jit(solution)/shard_map/ppermute | solution.py:389
  153.1 8.8 %collective-permute-start.5 = (bf16[8192,128]{1,0:T(8,128)(2,1)}, bf16[8192,128]{1,0:T(8,128)(2,1)}, u32[]{:S(2)}, u32[]{:S(2)}) collective-permute-start(bf16[8192,128]{1,0:T(8,128)(2,1)} %collective-permute-done.1.refs_2_), channel_id=1, source_target_pairs={{0,8},{8,0},{1,9},{9,1},{2,10},{10,2},{3,11},{11,3},{4,12},{12,4},... | collective-permute-start | bytes 6291464 | tf_op jit(solution)/shard_map/ppermute | solution.py:389
  155.1 8.2 %collective-permute-start.13 = (bf16[128,8192]{1,0:T(8,128)(2,1)}, bf16[128,8192]{1,0:T(8,128)(2,1)}, u32[]{:S(2)}, u32[]{:S(2)}) collective-permute-start(bf16[128,8192]{1,0:T(8,128)(2,1)} %collective-permute-done.refs_14_.refs_6_), channel_id=1, source_target_pairs={{0,8},{8,0},{1,9},{9,1},{2,10},{10,2},{3,11},{11,3},{4,12},{12,4},... | collective-permute-start | bytes 6291464 | tf_op jit(solution)/shard_map/ppermute | solution.py:389
  157.5 8.7 %collective-permute-start.8 = (bf16[8192,128]{1,0:T(8,128)(2,1)}, bf16[8192,128]{1,0:T(8,128)(2,1)}, u32[]{:S(2)}, u32[]{:S(2)}) collective-permute-start(bf16[8192,128]{1,0:T(8,128)(2,1)} %collective-permute-done.6.refs_4_), channel_id=1, source_target_pairs={{0,8},{8,0},{1,9},{9,1},{2,10},{10,2},{3,11},{11,3},{4,12},{12,4},... | collective-permute-start | bytes 6291464 | tf_op jit(solution)/shard_map/ppermute | solution.py:389
  159.4 9.8 %collective-permute-start.12 = (bf16[128,8192]{1,0:T(8,128)(2,1)}, bf16[128,8192]{1,0:T(8,128)(2,1)}, u32[]{:S(2)}, u32[]{:S(2)}) collective-permute-start(bf16[128,8192]{1,0:T(8,128)(2,1)} %collective-permute-done.7.refs_12_.refs_4_), channel_id=1, source_target_pairs={{0,8},{8,0},{1,9},{9,1},{2,10},{10,2},{3,11},{11,3},{4,12},{12,4},... | collective-permute-start | bytes 6291464 | tf_op jit(solution)/shard_map/ppermute | solution.py:389
  182.2 14.2 %collective-permute-start.14 = (bf16[16,8192]{1,0:T(8,128)(2,1)S(1)}, bf16[16,8192]{1,0:T(8,128)(2,1)S(1)}, u32[]{:S(2)}, u32[]{:S(2)}) collective-permute-start(bf16[16,8192]{1,0:T(8,128)(2,1)S(1)} %get-tuple-element.65.refs_8_), channel_id=1, source_target_pairs={{0,64},{1,65},{2,66},{3,67},{4,68},{5,69},{6,70},{7,71},{8,72},{9,... | collective-permute-start | bytes 786440 | tf_op jit(solution)/shard_map/ppermute | solution.py:393
  197.0 13.6 %collective-permute-start.15 = (bf16[16,8192]{1,0:T(8,128)(2,1)S(1)}, bf16[16,8192]{1,0:T(8,128)(2,1)S(1)}, u32[]{:S(2)}, u32[]{:S(2)}) collective-permute-start(bf16[16,8192]{1,0:T(8,128)(2,1)S(1)} %get-tuple-element.69.refs_8_), channel_id=1, source_target_pairs={{64,128},{65,129},{66,130},{67,131},{68,132},{69,133},{70,134},{71... | collective-permute-start | bytes 786440 | tf_op jit(solution)/shard_map/ppermute | solution.py:393
  211.3 0.7 collective-permute-start.16
  212.6 0.7 collective-permute-start.17
  213.9 0.7 collective-permute-start.18
  215.3 0.7 collective-permute-start.19
  216.6 0.7 collective-permute-start.20
  217.9 214.4 %all-to-all-start.1 = ((bf16[64,16,1152]{2,1,0:T(8,128)(2,1)}), bf16[64,16,1152]{2,1,0:T(8,128)(2,1)S(1)}, u32[]{:S(2)}, u32[]{:S(2)}) async-start(bf16[64,16,1152]{2,1,0:T(8,128)(2,1)} %bitcast.26), calls=%async_computation.1 | async-start | bytes 4718592 | tf_op jit(solution)/shard_map/all_to_all | solution.py:401
  230.3 2.2 slice-start
  230.3 3.5 slice-start.1
  230.3 4.6 slice-start.2
  230.3 5.8 %slice-start.3 = ((s8[16777216]{0:T(1024)(128)(4,1)}), s8[4194304]{0:T(1024)(128)(4,1)S(1)}, s32[]{:S(2)}) async-start(s8[16777216]{0:T(1024)(128)(4,1)} %bitcast.24), calls=%async_computation.6 | async-start | bytes 8388608
  231.3 0.8 collective-permute-start.21
  236.9 0.7 collective-permute-start.22
  238.3 0.7 collective-permute-start.23
  239.8 0.7 collective-permute-start.24
  241.2 0.7 collective-permute-start.25
  242.7 0.7 collective-permute-start.26
  244.1 177.8 %collective-permute-start.27 = (bf16[16,8192]{1,0:T(8,128)(2,1)S(1)}, bf16[16,8192]{1,0:T(8,128)(2,1)S(1)}, u32[]{:S(2)}, u32[]{:S(2)}) collective-permute-start(bf16[16,8192]{1,0:T(8,128)(2,1)S(1)} %get-tuple-element.109), channel_id=1, source_target_pairs={{64,0},{65,1},{66,2},{67,3},{68,4},{69,5},{70,6},{71,7},{72,8},{73... | collective-permute-start | bytes 786440 | tf_op jit(solution)/shard_map/ppermute | solution.py:393
  432.3 72.1 %all-to-all-start.2 = ((bf16[64,16,1152]{2,1,0:T(8,128)(2,1)}), bf16[64,16,1152]{2,1,0:T(8,128)(2,1)}, u32[]{:S(2)}, u32[]{:S(2)}) async-start(bf16[64,16,1152]{2,1,0:T(8,128)(2,1)} %bitcast.27), calls=%async_computation.2 | async-start | bytes 4718592 | tf_op jit(solution)/shard_map/all_to_all | solution.py:401
